TPU v7x, 32 devices: a whole 2x2x4 slice. The times are simulated.
32 devices in a mesh: ctx: 4 (over y, core), section: 2 (over x), tp: 4 (over z).
Axes of the slice: x: 2, y: 2, z: 4, core: 2. Of those that a mesh axis runs over, the one named last changes fastest.
Arguments:
- row_offsets: int32 [2], P('section'), may hold values from 1408 to 2048
- queries: bfloat16 [2, 512, 4096], P('section', 'ctx', 'tp'), may hold values from -8 to 8
- cache_keys: bfloat16 [2, 2560, 1024], P('section', 'ctx', 'tp'), may hold values from -4 to 4
- cache_values: bfloat16 [2, 2560, 1024], P('section', 'ctx', 'tp'), may hold values from -6 to 6
- residual: bfloat16 [2, 512, 5120], P('section', 'ctx', 'tp'), may hold values from -6 to 6
- out_weight: bfloat16 [2, 4096, 5120], P('section', 'tp'), may hold values from -0.09375 to 0.09375
Outputs:
- next_inputs: bfloat16 [2, 512, 5120], P('section', 'ctx', 'tp')
All inputs are finite; a program needn't handle non-finite values.
Results may differ from a plain program's by a relative error of at most 0.0085.
Values may be sent and summed in bfloat16 or wider, within the bound.
No kernel may reach another device: no remote copies, remote signals or barrier semaphores. Data moves between devices by JAX's collectives and lax.ppermute only.
A program may use at most 64 MiB of HBM per device.

v0:
```python
import math

import jax
import jax.numpy as jnp
from jax import lax
from jax.sharding import PartitionSpec as P

HD = 128
G = 4


NEG_FILL = -1e30


def from_behind(block, axis, distance):
    devices = range(lax.axis_size(axis))
    route = [((i - distance) % len(devices), i) for i in devices]
    return lax.ppermute(block, axis, route)


def attend_block(carried, query_heads, key_rows, value_rows, query_pos, key_start):
    run_max, run_sum, run_acc = carried
    row_count = key_rows.shape[0]
    scores = jnp.einsum(
        "kgqd,skd->kgqs", query_heads, key_rows, preferred_element_type=jnp.float32
    ) * HD ** (-0.5)
    key_pos = key_start + lax.iota(jnp.int32, row_count)
    visible = key_pos[None, :] <= query_pos[:, None]
    scores = jnp.where(visible, scores, NEG_FILL)
    new_max = jnp.maximum(run_max, jnp.max(scores, axis=-1))
    weights = jnp.where(visible, jnp.exp(scores - new_max[..., None]), 0.0)
    factor = jnp.exp(run_max - new_max)
    run_sum = run_sum * factor + jnp.sum(weights, axis=-1)
    mixed = jnp.einsum(
        "kgqs,skd->kgqd",
        weights.astype(jnp.bfloat16),
        value_rows,
        preferred_element_type=jnp.float32,
    )
    run_acc = run_acc * factor[..., None] + mixed
    return (new_max, run_sum, run_acc)


def attend_piece(carried, query_heads, key_rows, value_rows, query_pos):
    length = key_rows.shape[0]
    block_len = math.gcd(length, 512)
    block_count = length // block_len
    key_blocks = key_rows.reshape((block_count, block_len) + key_rows.shape[1:])
    value_blocks = value_rows.reshape((block_count, block_len) + value_rows.shape[1:])
    starts = block_len * lax.iota(jnp.int32, block_count)

    def advance(inner, operands):
        key_part, value_part, first_row = operands
        return (attend_block(inner, query_heads, key_part, value_part, query_pos, first_row), None)

    result, unused = lax.scan(advance, carried, (key_blocks, value_blocks, starts))
    return result


def on_device(row_offsets, queries, cache_keys, cache_values, residual, out_weight):
    own_index = lax.axis_index("ctx")
    block_rows = queries.shape[1]
    kv_local = cache_keys.shape[2] // HD
    offset = row_offsets[0]
    query_heads = queries[0].reshape(block_rows, kv_local, G, HD).transpose(1, 2, 0, 3)
    own_pos = offset + own_index * block_rows + lax.iota(jnp.int32, block_rows)
    key_piece = lax.all_gather(cache_keys, "ctx", axis=1, tiled=True)
    value_piece = lax.all_gather(cache_values, "ctx", axis=1, tiled=True)
    key_part = key_piece[0].reshape(key_piece.shape[1], kv_local, HD)
    value_part = value_piece[0].reshape(value_piece.shape[1], kv_local, HD)
    run_max, run_sum, run_acc = attend_piece(
        (
            jnp.full((kv_local, G, block_rows), NEG_FILL, jnp.float32),
            jnp.zeros((kv_local, G, block_rows), jnp.float32),
            jnp.zeros((kv_local, G, block_rows, HD), jnp.float32),
        ),
        query_heads,
        key_part,
        value_part,
        own_pos,
    )
    attended = (
        (run_acc / run_sum[..., None])
        .transpose(2, 0, 1, 3)
        .reshape(block_rows, kv_local * G * HD)
        .astype(jnp.bfloat16)
    )
    weight_local = out_weight[0]
    projected = lax.psum_scatter(
        lax.dot_general(
            weight_local, attended, (((0,), (1,)), ((), ())), preferred_element_type=jnp.float32
        ).astype(jnp.bfloat16),
        "tp",
        scatter_dimension=0,
        tiled=True,
    ).astype(jnp.float32)
    updated = (residual[0].astype(jnp.float32) + projected.T).astype(jnp.bfloat16)
    handed = from_behind(updated, "section", 1)
    return handed[None]


def solution(mesh):
    placed = (
        P("section"),
        P("section", "ctx", "tp"),
        P("section", "ctx", "tp"),
        P("section", "ctx", "tp"),
        P("section", "ctx", "tp"),
        P("section", "tp", None),
    )
    return jax.shard_map(
        on_device, mesh=mesh, in_specs=placed, out_specs=P("section", "ctx", "tp"), check_vma=False
    )
```

profile of v0, /device:TPU:0, one launch (start us, length us, event | category | flops | bytes accessed | tf_op | source)
XLA Modules:
  0.0 128.2 jit_solution(13094317784813468565)
XLA Ops:
  6.5 0.0 all-gather.3.cloned.1.call-start
  6.5 0.7 all-gather.3.cloned.1.call-update
  7.3 0.0 all-gather.5.cloned.1.call-start
  7.3 0.7 all-gather.5.cloned.1.call-update
  8.0 0.0 reduce-scatter.2.cloned.1.call-start
  8.7 1.1 copy.9
  9.9 0.2 copy.11
  10.1 19.8 %all-gather.3.cloned.1.call-done = bf16[1,2560,256]{2,1,0:T(8,128)(2,1)} async-done(((bf16[1,640,256]{2,1,0:T(8,128)(2,1)}), bf16[1,2560,256]{2,1,0:T(8,128)(2,1)}) %all-gather.3.cloned.1.call-update) | async-done | bytes 1310736 | tf_op jit(solution)/shard_map/all_gather | solution.py:67
  29.8 2.9 %reshape_reshape_squeeze.6 = bf16[5,512,2,128]{3,2,1,0:T(2,128)(2,1)S(1)} reshape(bf16[1,2560,256]{2,1,0:T(8,128)(2,1)} %all-gather.3.cloned.1.call-done) | data formatting | bytes 2621440 | tf_op jit(solution)/shard_map/reshape;reshape;squeeze | solution.py:48
  32.8 16.8 %all-gather.5.cloned.1.call-done = bf16[1,2560,256]{2,1,0:T(8,128)(2,1)} async-done(((bf16[1,640,256]{2,1,0:T(8,128)(2,1)}), bf16[1,2560,256]{2,1,0:T(8,128)(2,1)}) %all-gather.5.cloned.1.call-update) | async-done | bytes 1310736 | tf_op jit(solution)/shard_map/all_gather | solution.py:68
  49.6 2.9 %reshape_reshape_squeeze.7 = bf16[5,512,2,128]{3,2,1,0:T(2,128)(2,1)S(1)} reshape(bf16[1,2560,256]{2,1,0:T(8,128)(2,1)} %all-gather.5.cloned.1.call-done) | data formatting | bytes 2621440 | tf_op jit(solution)/shard_map/reshape;reshape;squeeze | solution.py:49
  52.6 19.6 %while.15 = (s32[]{:T(128)}, f32[2,4,128]{2,1,0:T(4,128)S(1)}, f32[2,4,128]{2,1,0:T(4,128)S(1)}, f32[2,4,128,128]{3,2,1,0:T(8,128)S(1)}, s32[5]{0:T(128)S(1)}, /...) while((s32[]{:T(128)}, f32[2,4,128]{2,1,0:T(4,128)S(1)}, ...), condition=%wide.region_3.4_spmd.clone, body=%wide.region_0.3_spmd.clone.sunk | while | flops 275715712 | bytes 9507993 | solution.py:56
  52.6 0.7 dynamic_slice.19
  53.3 0.7 iota_add_fusion.5
  54.0 0.1 broadcast_compare_fusion.2
  54.1 0.4 constant_dynamic-slice_fusion.3
  54.5 0.5 fusion.33
  55.0 0.5 fusion.34
  55.5 1.0 convolution_add_fusion.2
  56.5 0.7 dynamic_slice.19
  57.2 0.7 iota_add_fusion.5
  57.9 0.1 broadcast_compare_fusion.2
  58.0 0.4 constant_dynamic-slice_fusion.3
  58.4 0.5 fusion.33
  58.9 0.5 fusion.34
  59.4 1.0 convolution_add_fusion.2
  60.4 0.7 dynamic_slice.19
  61.1 0.7 iota_add_fusion.5
  61.8 0.1 broadcast_compare_fusion.2
  62.0 0.4 constant_dynamic-slice_fusion.3
  62.3 0.5 fusion.33
  62.8 0.5 fusion.34
  63.4 1.0 convolution_add_fusion.2
  64.4 0.7 dynamic_slice.19
  65.0 0.7 iota_add_fusion.5
  65.7 0.1 broadcast_compare_fusion.2
  65.9 0.4 constant_dynamic-slice_fusion.3
  66.3 0.5 fusion.33
  66.7 0.5 fusion.34
  67.3 1.0 convolution_add_fusion.2
  68.3 0.7 dynamic_slice.19
  69.0 0.7 iota_add_fusion.5
  69.7 0.1 broadcast_compare_fusion.2
  69.8 0.4 constant_dynamic-slice_fusion.3
  70.2 0.5 fusion.33
  70.7 0.5 fusion.34
  71.2 1.0 convolution_add_fusion.2
  72.2 0.2 copy.13
  72.4 0.1 divide_convert_fusion
  72.5 0.0 copy-start
  72.5 6.7 %fusion.20 = bf16[5120,128]{0,1:T(8,128)(2,1)} fusion(bf16[128,1024]{0,1:T(8,128)(2,1)S(1)} %bitcast.65, bf16[1,1024,5120]{2,1,0:T(8,128)(2,1)} %param.13), kind=kOutput, calls=%fused_computation.30 | convolution fusion | flops 1342832640 | bytes 12058624 | tf_op jit(solution)/shard_map/dot_general | solution.py:90
  79.2 0.0 reduce-scatter.2.cloned.1.call-update
  79.2 31.4 %reduce-scatter.2.cloned.1.call-done = bf16[1280,128]{0,1:T(8,128)(2,1)} async-done(((bf16[5120,128]{0,1:T(8,128)(2,1)}), bf16[1280,128]{0,1:T(8,128)(2,1)}) %reduce-scatter.2.cloned.1.call-update) | async-done | bytes 327696 | tf_op jit(solution)/shard_map/reduce_scatter | solution.py:89
  110.6 0.0 copy-done
  110.6 1.0 fusion.23
  111.6 1.5 %collective-permute-start = (bf16[128,1280]{1,0:T(8,128)(2,1)S(1)}, bf16[128,1280]{1,0:T(8,128)(2,1)S(1)}, u32[]{:S(2)}, u32[]{:S(2)}) collective-permute-start(bf16[128,1280]{1,0:T(8,128)(2,1)S(1)} %fusion.23), channel_id=1, source_target_pairs={{4,0},{0,4},{5,1},{1,5},{6,2},{2,6},{7,3},{3,7},{12,8},{8,12},{13,... | collective-permute-start | bytes 983048 | tf_op jit(solution)/shard_map/ppermute | solution.py:18
  113.1 7.8 %collective-permute-done = bf16[128,1280]{1,0:T(8,128)(2,1)S(1)} collective-permute-done((bf16[128,1280]{1,0:T(8,128)(2,1)S(1)}, bf16[128,1280]{1,0:T(8,128)(2,1)S(1)}, u32[]{:S(2)}, u32[]{:S(2)}) %collective-permute-start) | collective-permute-done | bytes 327712 | tf_op jit(solution)/shard_map/ppermute | solution.py:18
  121.0 0.7 copy.43
  (24 shorter events, 0.2 us)
Async XLA Ops:
  6.5 23.3 %all-gather.3.cloned.1.call-start = ((), (), s32[]{:S(2)}) async-start(), calls=%async_computation.1 | async-start | bytes 1638400 | tf_op jit(solution)/shard_map/all_gather | solution.py:67
  7.3 42.4 %all-gather.5.cloned.1.call-start = ((), (), s32[]{:S(2)}) async-start(), calls=%async_computation.2 | async-start | bytes 1638400 | tf_op jit(solution)/shard_map/all_gather | solution.py:68
  8.0 102.6 %reduce-scatter.2.cloned.1.call-start = ((), (), s32[]{:S(2)}) async-start(), calls=%async_computation.3 | async-start | bytes 1638400 | tf_op jit(solution)/shard_map/reduce_scatter | solution.py:89
  72.5 38.1 %copy-start = (bf16[1,128,1280]{2,1,0:T(8,128)(2,1)S(1)}, bf16[1,128,1280]{2,1,0:T(8,128)(2,1)}, u32[]{:S(2)}) copy-start(bf16[1,128,1280]{2,1,0:T(8,128)(2,1)} %param.12) | copy-start | bytes 983044
  111.6 9.4 %collective-permute-start = (bf16[128,1280]{1,0:T(8,128)(2,1)S(1)}, bf16[128,1280]{1,0:T(8,128)(2,1)S(1)}, u32[]{:S(2)}, u32[]{:S(2)}) collective-permute-start(bf16[128,1280]{1,0:T(8,128)(2,1)S(1)} %fusion.23), channel_id=1, source_target_pairs={{4,0},{0,4},{5,1},{1,5},{6,2},{2,6},{7,3},{3,7},{12,8},{8,12},{13,... | collective-permute-start | bytes 983048 | tf_op jit(solution)/shard_map/ppermute | solution.py:18
Sparse Core Ops, SparseCore 0:
  8.9 20.8 all-gather.2
  31.4 18.1 all-gather.4
  79.3 31.2 reduce-scatter.1
where the time goes:
time: 129 us; the launch traced here: 128 us
  waiting for transfers between devices  77.2 us (60%)
  matrix products  13.9 us (11%)
  between operations  13.9 us (11%)
  local copies, waits for them, and re-layouts  13.3 us (10%)
  other arithmetic  7.97 us (6%)
  starting transfers between devices  1.61 us (1%)
    reduce_scatter x1, waiting for transfers between devices, on_device(): lax.psum_scatter(lax.dot_general(weight_local, attended, (((0,), (1,)), (...  31.4 us
    all_gather x1, waiting for transfers between devices, on_device(): key_piece = lax.all_gather(cache_keys, 'ctx', axis=1, tiled=True)  19.8 us
    all_gather x1, waiting for transfers between devices, on_device(): value_piece = lax.all_gather(cache_values, 'ctx', axis=1, tiled=True)  16.8 us
    ppermute x1, waiting for transfers between devices, from_behind(): return lax.ppermute(block, axis, route)  7.83 us
    dot_general x1, matrix products, on_device(): lax.dot_general(weight_local, attended, (((0,), (1,)), ((), ())), preferr...  6.68 us
    dynamic_slice x10, local copies, waits for them, and re-layouts, attend_piece(): lax.scan(advance, carried, (key_blocks, value_blocks, starts))  5.18 us
    dot_general x5, matrix products, attend_block(): jnp.einsum('kgqs,skd->kgqd', weights.astype(jnp.bfloat16), value_rows, pr...  4.88 us
    add x5, other arithmetic, attend_block(): key_pos = key_start + lax.iota(jnp.int32, row_count)  3.45 us
  transfers between devices with their start and end apart: 4, of which 4 were waited for; matrix products, arithmetic and copies ran while one was open for 3% of the time, Pallas kernels for 0%

commit v1 on v0

v1 whole, which is shorter than its diff:
```python
import functools
import math

import jax
import jax.numpy as jnp
from jax import lax
from jax.experimental import pallas as pl
from jax.experimental.pallas import tpu as pltpu
from jax.sharding import PartitionSpec as P

HD = 128
G = 4
LANES = 128
NEG_FILL = -1e30
MAX_FLOOR = -1e29
EXP_SCALE = HD ** (-0.5) * math.log2(math.e)
MIB = 1 << 20

WHOLE = pl.BlockSpec(memory_space=pltpu.VMEM)
SCALARS = pl.BlockSpec(memory_space=pltpu.SMEM)


def exchange(block, axis, mask):
    route = [(i, i ^ mask) for i in range(lax.axis_size(axis))]
    return lax.ppermute(block, axis, route)


def from_behind(block, axis, distance):
    devices = range(lax.axis_size(axis))
    route = [((i - distance) % len(devices), i) for i in devices]
    return lax.ppermute(block, axis, route)


def in_vmem(array):
    return pltpu.with_memory_space_constraint(array, pltpu.VMEM)


def local_call(body, outs, limit, flops, scratch=()):
    return pl.pallas_call(
        body,
        out_shape=[pltpu.VMEM(shape, dtype) for shape, dtype in outs],
        out_specs=[WHOLE] * len(outs),
        scratch_shapes=list(scratch),
        compiler_params=pltpu.CompilerParams(vmem_limit_bytes=limit),
        cost_estimate=pl.CostEstimate(flops=flops, bytes_accessed=0, transcendentals=0),
    )


def stacked_query(q_ref, kv_head):
    heads = range(kv_head * G, (kv_head + 1) * G)
    return jnp.concatenate([q_ref[0, :, h * HD : (h + 1) * HD] for h in heads], axis=0)


def masked_scores(query, key_ref, kv_head, bound):
    keys = key_ref[0, :, kv_head * HD : (kv_head + 1) * HD]
    scores = lax.dot_general(query, keys, (((1,), (1,)), ((), ())), preferred_element_type=jnp.float32)
    rows = query.shape[0] // G
    ahead = lax.broadcasted_iota(jnp.int32, scores.shape, 1) - lax.broadcasted_iota(jnp.int32, scores.shape, 0) % rows
    return jnp.where(ahead <= bound, scores, NEG_FILL)


def early_kernel(masks, offset_ref, q_ref, *refs):
    count = len(masks)
    key_refs, value_refs = refs[:count], refs[count : 2 * count]
    max_ref, sum_ref, acc_ref = refs[2 * count :]
    own = lax.axis_index("ctx")
    rows, length = q_ref.shape[1], key_refs[0].shape[1]
    first_row = offset_ref[0] + own * rows
    for kv_head in range(key_refs[0].shape[2] // HD):
        columns = slice(kv_head * HD, (kv_head + 1) * HD)
        query = stacked_query(q_ref, kv_head)
        parts = [
            masked_scores(query, ref, kv_head, first_row - (own ^ mask) * length) for ref, mask in zip(key_refs, masks)
        ]
        top = functools.reduce(jnp.maximum, [jnp.max(part, axis=1, keepdims=True) for part in parts])
        top = jnp.maximum(top, MAX_FLOOR)
        weights = [jnp.exp2((part - top) * EXP_SCALE) for part in parts]
        total = sum(jnp.sum(part, axis=1, keepdims=True) for part in weights)
        mixed = sum(
            jnp.dot(part.astype(jnp.bfloat16), ref[0, :, columns], preferred_element_type=jnp.float32)
            for part, ref in zip(weights, value_refs)
        )
        max_ref[kv_head] = jnp.broadcast_to(top, max_ref.shape[1:])
        sum_ref[kv_head] = jnp.broadcast_to(total, sum_ref.shape[1:])
        acc_ref[kv_head] = mixed


def late_kernel(masks, offset_ref, q_ref, max_ref, sum_ref, acc_ref, *refs):
    count = len(masks)
    key_refs = refs[:count]
    total_ref, scaled_ref = refs[count : count + 2]
    weight_refs = refs[count + 2 :]
    own = lax.axis_index("ctx")
    rows, length = q_ref.shape[1], key_refs[0].shape[1]
    first_row = offset_ref[0] + own * rows
    for kv_head in range(key_refs[0].shape[2] // HD):
        query = stacked_query(q_ref, kv_head)
        parts = [
            masked_scores(query, ref, kv_head, first_row - (own ^ mask) * length) for ref, mask in zip(key_refs, masks)
        ]
        before = max_ref[kv_head]
        top = functools.reduce(jnp.maximum, [jnp.max(part, axis=1, keepdims=True) for part in parts])
        top = jnp.maximum(top, before[:, :1])
        weights = [jnp.exp2((part - top) * EXP_SCALE) for part in parts]
        total = sum(jnp.sum(part, axis=1, keepdims=True) for part in weights)
        factor = jnp.exp2((before - top) * EXP_SCALE)
        total_ref[kv_head] = sum_ref[kv_head] * factor + total
        scaled_ref[kv_head] = acc_ref[kv_head] * factor
        for ref, part in zip(weight_refs, weights):
            ref[kv_head] = part.astype(jnp.bfloat16)


def project(att, weight_ref, out_ref, blocks, block_width, lower):
    width = out_ref.shape[2]
    for slot, block in enumerate(blocks):
        start = pl.multiple_of(block * block_width + lower, LANES)
        out_ref[slot] = jnp.dot(
            att, weight_ref[0, :, pl.ds(start, width)], preferred_element_type=jnp.float32
        ).astype(jnp.bfloat16)


def finish_kernel(count, blocks_of, block_width, total_ref, scaled_ref, *refs):
    value_refs, weight_refs = refs[:count], refs[count : 2 * count]
    w_ref, att_ref, out_ref = refs[2 * count :]
    rows = att_ref.shape[0]
    for kv_head in range(scaled_ref.shape[0]):
        columns = slice(kv_head * HD, (kv_head + 1) * HD)
        mixed = scaled_ref[kv_head]
        for value_ref, part_ref in zip(value_refs, weight_refs):
            mixed += jnp.dot(part_ref[kv_head], value_ref[0, :, columns], preferred_element_type=jnp.float32)
        attended = (mixed / total_ref[kv_head]).astype(jnp.bfloat16)
        for g in range(G):
            head = kv_head * G + g
            att_ref[:, head * HD : (head + 1) * HD] = attended[g * rows : (g + 1) * rows]
    project(att_ref[...], w_ref, out_ref, blocks_of(lax.axis_index("tp")), block_width, 0)


def project_kernel(blocks_of, block_width, lower, att_ref, w_ref, out_ref):
    project(att_ref[...], w_ref, out_ref, blocks_of(lax.axis_index("tp")), block_width, lower)


def xor_order(lowest, size):
    if lowest >= size:
        return [0]
    rest = xor_order(lowest * 2, size)
    return [x + lowest for x in rest] + rest


def chunk_widths(width):
    units = width // LANES
    first = max(1, (2 * units) // 5)
    widths = [first, first, units - 2 * first]
    return [u * LANES for u in widths if u > 0]


def on_device(row_offsets, queries, cache_keys, cache_values, residual, out_weight):
    n_ctx, n_tp = lax.axis_size("ctx"), lax.axis_size("tp")
    rows, length = queries.shape[1], cache_keys.shape[1]
    kv_local = cache_keys.shape[2] // HD
    stacked = G * rows
    top_bit = n_ctx // 2
    block_width = out_weight.shape[2] // n_tp

    far_key = exchange(cache_keys, "ctx", top_bit)
    far_value = exchange(cache_values, "ctx", top_bit)
    near = [(0, cache_keys, cache_values)]
    bit = top_bit // 2
    while bit:
        near += [(m | bit, exchange(k, "ctx", bit), exchange(v, "ctx", bit)) for m, k, v in near]
        bit //= 2
    state = [((kv_local, stacked, HD), jnp.float32)] * 3
    half_flops = 4 * kv_local * stacked * length * HD * len(near)
    top, total, acc = local_call(
        functools.partial(early_kernel, [m for m, _, _ in near]), state, 32 * MIB, half_flops
    )(
        row_offsets, in_vmem(queries), *[in_vmem(k) for _, k, _ in near], *[in_vmem(v) for _, _, v in near]
    )
    far_keys = [(top_bit, far_key)]
    bit = top_bit // 2
    while bit:
        far_keys += [(m | bit, exchange(k, "ctx", bit)) for m, k in far_keys]
        bit //= 2
    total, scaled, *weights = local_call(
        functools.partial(late_kernel, [m for m, _ in far_keys]),
        state[:2] + [((kv_local, stacked, length), jnp.bfloat16)] * len(far_keys),
        32 * MIB,
        half_flops // 2,
    )(row_offsets, in_vmem(queries), top, total, acc, *[in_vmem(k) for _, k in far_keys])
    far_values = [far_value]
    bit = top_bit // 2
    while bit:
        far_values += [exchange(v, "ctx", bit) for v in far_values]
        bit //= 2

    order = xor_order(2, n_tp)
    keep_blocks = lambda me: [me ^ x for x in order]
    send_blocks = lambda me: [me ^ 1 ^ x for x in order]
    weight = in_vmem(out_weight)
    widths = chunk_widths(block_width)
    block_flops = 2 * rows * out_weight.shape[1] * len(order)
    attended, first_send = local_call(
        functools.partial(finish_kernel, len(far_values), send_blocks, block_width),
        [((rows, out_weight.shape[1]), jnp.bfloat16), ((len(order), rows, widths[0]), jnp.bfloat16)],
        16 * MIB,
        half_flops // 2 + block_flops * widths[0],
    )(total, scaled, *[in_vmem(v) for v in far_values], *weights, weight)

    def projected(blocks_of, lower, width):
        return local_call(
            functools.partial(project_kernel, blocks_of, block_width, lower),
            [((len(order), rows, width), jnp.bfloat16)],
            16 * MIB,
            block_flops * width,
        )(attended, weight)[0]

    outs = []
    lower = 0
    for width in widths:
        send = first_send if lower == 0 else projected(send_blocks, lower, width)
        keep = projected(keep_blocks, lower, width).astype(jnp.float32)
        bit = 1
        while bit < n_tp:
            keep = keep + exchange(send, "tp", bit).astype(jnp.float32)
            half = keep.shape[0] // 2
            send, keep = keep[:half].astype(jnp.bfloat16), keep[half:]
            bit *= 2
        updated = residual[0, :, lower : lower + width].astype(jnp.float32) + keep[0]
        outs.append(from_behind(updated.astype(jnp.bfloat16), "section", 1))
        lower += width
    return jnp.concatenate(outs, axis=1)[None]


def solution(mesh):
    placed = (
        P("section"),
        P("section", "ctx", "tp"),
        P("section", "ctx", "tp"),
        P("section", "ctx", "tp"),
        P("section", "ctx", "tp"),
        P("section", "tp", None),
    )
    return jax.shard_map(
        on_device, mesh=mesh, in_specs=placed, out_specs=P("section", "ctx", "tp"), check_vma=False
    )
```

time: 129 us -> 74.7 us (0.58)
  waiting for transfers between devices: 77.2 us -> 37.1 us
  starting transfers between devices: 1.61 us -> 17.9 us
  matrix products: 13.9 us -> 0 us
  between operations: 13.9 us -> 0.83 us
  Pallas kernels: 0 us -> 7.82 us
  other arithmetic: 7.97 us -> 1.04 us
  local copies, waits for them, and re-layouts: 13.3 us -> 9.72 us
    all_gather x2 -> x0, waiting for transfers between devices: 36.6 us -> none  [the longest x1 19.8 us: on_device(): key_piece = lax.all_gather(cache_keys, 'ctx', axis=1, tiled=True)]
    reduce_scatter x1 -> x0, waiting for transfers between devices: 31.4 us -> none  [on_device(): lax.psum_scatter(lax.dot_general(weight_local, attended, (((0,), (1,)), (...]
    ppermute x0 -> x12, waiting for transfers between devices: none -> 31.2 us  [exchange(): return lax.ppermute(block, axis, route)]
    ppermute x0 -> x12, starting transfers between devices: none -> 14.2 us  [exchange(): return lax.ppermute(block, axis, route)]
    dot_general x11 -> x0, matrix products: 13.9 us -> none  [the longest x1 6.68 us: on_device(): lax.dot_general(weight_local, attended, (((0,), (1,)), ((), ())), preferr...]
    pallas_call x0 -> x8, Pallas kernels: none -> 7.82 us  [the longest x1 2.45 us: on_device(): local_call(functools.partial(early_kernel, [m for m, _, _ in near]), stat...]
    unnamed x5 -> x12, local copies, waits for them, and re-layouts: 2.06 us -> 9.67 us
    another operation x2 -> x0, local copies, waits for them, and re-layouts: 5.9 us -> none  [the longest x1 2.95 us: attend_piece(): key_blocks = key_rows.reshape((block_count, block_len) + key_rows.shape[1:])]
  transfers between devices with their start and end apart: 4 -> 15, of which waited for: 4 -> 7; matrix products, arithmetic and copies ran while one was open for 3% -> 0% of each run, Pallas kernels for 0% -> 8%
where the time goes in v1:
time: 74.7 us; the launch traced here: 74.4 us
  waiting for transfers between devices  37.1 us (50%)
  starting transfers between devices  17.9 us (24%)
  local copies, waits for them, and re-layouts  9.72 us (13%)
  Pallas kernels  7.82 us (10%)
  other arithmetic  1.04 us (1%)
  between operations  0.83 us (1%)
    ppermute x12, waiting for transfers between devices, exchange(): return lax.ppermute(block, axis, route)  31.2 us
    ppermute x12, starting transfers between devices, exchange(): return lax.ppermute(block, axis, route)  14.2 us
    unnamed x12, local copies, waits for them, and re-layouts  9.67 us
    ppermute x3, waiting for transfers between devices, from_behind(): return lax.ppermute(block, axis, route)  5.92 us
    ppermute x3, starting transfers between devices, from_behind(): return lax.ppermute(block, axis, route)  3.65 us
    pallas_call x1, Pallas kernels, on_device(): local_call(functools.partial(early_kernel, [m for m, _, _ in near]), stat...  2.45 us
    pallas_call x1, Pallas kernels, on_device(): local_call(functools.partial(late_kernel, [m for m, _ in far_keys]), stat...  2.18 us
    pallas_call x5, Pallas kernels, projected(): local_call(functools.partial(project_kernel, blocks_of, block_width, lowe...  2.03 us
  transfers between devices with their start and end apart: 15, of which 7 were waited for; matrix products, arithmetic and copies ran while one was open for 0% of the time, Pallas kernels for 8%

profile of v1, /device:TPU:0, one launch (start us, length us, event | category | flops | bytes accessed | tf_op | source)
XLA Modules:
  0.0 74.4 jit_solution(17717043195392731577)
XLA Ops:
  0.0 3.0 %collective-permute-start.2 = (bf16[1,640,256]{2,1,0:T(8,128)(2,1)}, bf16[1,640,256]{2,1,0:T(8,128)(2,1)S(1)}, u32[]{:S(2)}, u32[]{:S(2)}) collective-permute-start(bf16[1,640,256]{2,1,0:T(8,128)(2,1)} %refs_0_.1), channel_id=1, source_target_pairs={{0,16},{8,24},{16,0},{24,8},{1,17},{9,25},{17,1},{25,9},{2,18},{10... | collective-permute-start | bytes 983048 | tf_op jit(solution)/shard_map/ppermute | solution.py:25
  3.0 0.0 collective-permute-start.4
  3.0 0.0 collective-permute-start
  3.0 0.5 collective-permute-start.1
  3.5 8.2 %collective-permute-done.2.refs_0_ = bf16[1,640,256]{2,1,0:T(8,128)(2,1)S(1)} collective-permute-done((bf16[1,640,256]{2,1,0:T(8,128)(2,1)}, bf16[1,640,256]{2,1,0:T(8,128)(2,1)S(1)}, u32[]{:S(2)}, u32[]{:S(2)}) %collective-permute-start.2) | collective-permute-done | bytes 327712 | tf_op jit(solution)/shard_map/ppermute | solution.py:25
  11.7 0.0 collective-permute-start.3
  11.7 6.2 %collective-permute-done.4.refs_0_ = bf16[1,640,256]{2,1,0:T(8,128)(2,1)S(1)} collective-permute-done((bf16[1,640,256]{2,1,0:T(8,128)(2,1)}, bf16[1,640,256]{2,1,0:T(8,128)(2,1)S(1)}, u32[]{:S(2)}, u32[]{:S(2)}) %collective-permute-start.4) | collective-permute-done | bytes 327712 | tf_op jit(solution)/shard_map/ppermute | solution.py:25
  17.9 0.0 collective-permute-start.5
  18.6 0.0 collective-permute-done.refs_1_
  18.6 0.0 collective-permute-done.1.refs_3_
  18.6 0.0 copy-start.2
  18.6 0.9 %copy-done.2 = bf16[1,128,1024]{2,1,0:T(8,128)(2,1)S(1)} copy-done((bf16[1,128,1024]{2,1,0:T(8,128)(2,1)S(1)}, bf16[1,128,1024]{2,1,0:T(8,128)(2,1)}, u32[]{:S(2)}) %copy-start.2) | copy-done | bytes 262168
  19.5 0.0 copy-start.3
  19.5 1.0 %copy-done.3 = bf16[1,640,256]{2,1,0:T(8,128)(2,1)S(1)} copy-done((bf16[1,640,256]{2,1,0:T(8,128)(2,1)S(1)}, bf16[1,640,256]{2,1,0:T(8,128)(2,1)}, u32[]{:S(2)}) %copy-start.3) | copy-done | bytes 327704
  20.5 0.0 copy-start.4
  20.5 1.0 %copy-done.4 = bf16[1,640,256]{2,1,0:T(8,128)(2,1)S(1)} copy-done((bf16[1,640,256]{2,1,0:T(8,128)(2,1)S(1)}, bf16[1,640,256]{2,1,0:T(8,128)(2,1)}, u32[]{:S(2)}) %copy-start.4) | copy-done | bytes 327704
  21.5 2.4 %shard_map.64 = (f32[2,512,128]{2,1,0:T(8,128)S(1)}, f32[2,512,128]{2,1,0:T(8,128)S(1)}, f32[2,512,128]{2,1,0:T(8,128)S(1)}) custom-call(s32[1]{0:T(128)S(6)} %copy.7.offset_ref, bf16[1,128,1024]{2,1,0:T(8,128)(2,1)S(1)} %copy-done.2, bf16[1,640,256]{2,1,0:T(8,128)(2,1)S(1)} %copy-done.3, bf16[1,640,256]{2,1,0:T(8,128)(2,1)S(1)} %collective-permute-done.refs_1_, ...), custom_call_target="tpu_custom_call" | custom-call | flops 671088640 | tf_op jit(solution)/shard_map/pallas_call | solution.py:173
  23.9 0.0 collective-permute-done.3.refs_1_
  23.9 2.2 %shard_map.65 = (f32[2,512,128]{2,1,0:T(8,128)S(1)}, f32[2,512,128]{2,1,0:T(8,128)S(1)}, bf16[2,512,640]{2,1,0:T(8,128)(2,1)S(1)}, bf16[2,512,640]{2,1,0:T(8,128)(2,1)S(1)}) custom-call(s32[1]{0:T(128)S(6)} %copy.7.offset_ref, bf16[1,128,1024]{2,1,0:T(8,128)(2,1)S(1)} %copy-done.2, f32[2,512,128]{2,1,0:T(8,128)S(1)} %get-tuple-element.14.max_ref, ...), custom_call_target="tpu_custom_call" | custom-call | flops 335544320 | tf_op jit(solution)/shard_map/pallas_call | solution.py:183
  26.1 0.0 collective-permute-done.5.refs_1_
  26.1 0.0 copy-start
  26.1 4.0 %copy-done = bf16[1,1024,5120]{2,1,0:T(8,128)(2,1)S(1)} copy-done((bf16[1,1024,5120]{2,1,0:T(8,128)(2,1)S(1)}, bf16[1,1024,5120]{2,1,0:T(8,128)(2,1)}, u32[]{:S(2)}) %copy-start) | copy-done | bytes 10485784
  30.1 0.0 copy-start.1
  30.1 1.2 %shard_map.66 = (bf16[128,1024]{1,0:T(8,128)(2,1)S(1)}, bf16[2,128,512]{2,1,0:T(8,128)(2,1)S(1)}) custom-call(f32[2,512,128]{2,1,0:T(8,128)S(1)} %get-tuple-element.17.total_ref, f32[2,512,128]{2,1,0:T(8,128)S(1)} %get-tuple-element.18.scaled_ref, bf16[1,640,256]{2,1,0:T(8,128)(2,1)S(1)} %collective-permute-done.4.refs_0_, ...), custom_call_target="tpu_custom_call" | custom-call | flops 603979776 | tf_op jit(solution)/shard_map/pallas_call | solution.py:201
  31.3 2.8 %copy-done.1 = bf16[1,1024,5120]{2,1,0:T(8,128)(2,1)S(1)} copy-done((bf16[1,1024,5120]{2,1,0:T(8,128)(2,1)S(1)}, bf16[1,1024,5120]{2,1,0:T(8,128)(2,1)}, u32[]{:S(2)}) %copy-start.1) | copy-done | bytes 10485784
  34.1 0.5 shard_map.69
  34.6 1.9 %collective-permute-start.9 = (bf16[2,128,512]{2,1,0:T(8,128)(2,1)S(1)}, bf16[2,128,512]{2,1,0:T(8,128)(2,1)S(1)}, u32[]{:S(2)}, u32[]{:S(2)}) collective-permute-start(bf16[2,128,512]{2,1,0:T(8,128)(2,1)S(1)} %shard_map.69), channel_id=1, source_target_pairs={{0,1},{1,0},{2,3},{3,2},{4,5},{5,4},{6,7},{7,6},{8,9},{9,8},{10,11... | collective-permute-start | bytes 786440 | tf_op jit(solution)/shard_map/ppermute | solution.py:25
  36.4 0.2 collective-permute-start.6
  36.7 0.3 shard_map.71
  37.0 1.8 %collective-permute-start.12 = (bf16[2,128,256]{2,1,0:T(8,128)(2,1)S(1)}, bf16[2,128,256]{2,1,0:T(8,128)(2,1)S(1)}, u32[]{:S(2)}, u32[]{:S(2)}) collective-permute-start(bf16[2,128,256]{2,1,0:T(8,128)(2,1)S(1)} %shard_map.71), channel_id=1, source_target_pairs={{0,1},{1,0},{2,3},{3,2},{4,5},{5,4},{6,7},{7,6},{8,9},{9,8},{10,11... | collective-permute-start | bytes 393224 | tf_op jit(solution)/shard_map/ppermute | solution.py:25
  38.8 0.5 shard_map.68
  39.3 0.5 shard_map.67
  39.8 0.3 shard_map.70
  40.1 3.6 %collective-permute-done.9 = bf16[2,128,512]{2,1,0:T(8,128)(2,1)S(1)} collective-permute-done((bf16[2,128,512]{2,1,0:T(8,128)(2,1)S(1)}, bf16[2,128,512]{2,1,0:T(8,128)(2,1)S(1)}, u32[]{:S(2)}, u32[]{:S(2)}) %collective-permute-start.9) | collective-permute-done | bytes 262176 | tf_op jit(solution)/shard_map/ppermute | solution.py:25
  43.7 0.1 convert_add_fusion
  43.8 0.0 copy-start.5
  43.8 2.9 %collective-permute-start.10 = (bf16[1,128,512]{2,1,0:T(8,128)(2,1)S(1)}, bf16[1,128,512]{2,1,0:T(8,128)(2,1)S(1)}, u32[]{:S(2)}, u32[]{:S(2)}) collective-permute-start(bf16[1,128,512]{2,1,0:T(8,128)(2,1)S(1)} %slice.72), channel_id=1, source_target_pairs={{0,2},{1,3},{2,0},{3,1},{4,6},{5,7},{6,4},{7,5},{8,10},{9,11},{10,... | collective-permute-start | bytes 393224 | tf_op jit(solution)/shard_map/ppermute | solution.py:25
  46.7 5.4 %collective-permute-done.6 = bf16[2,128,512]{2,1,0:T(8,128)(2,1)S(1)} collective-permute-done((bf16[2,128,512]{2,1,0:T(8,128)(2,1)S(1)}, bf16[2,128,512]{2,1,0:T(8,128)(2,1)S(1)}, u32[]{:S(2)}, u32[]{:S(2)}) %collective-permute-start.6) | collective-permute-done | bytes 262176 | tf_op jit(solution)/shard_map/ppermute | solution.py:25
  52.1 0.1 convert_add_fusion.1
  52.3 2.0 %collective-permute-start.7 = (bf16[1,128,512]{2,1,0:T(8,128)(2,1)S(1)}, bf16[1,128,512]{2,1,0:T(8,128)(2,1)S(1)}, u32[]{:S(2)}, u32[]{:S(2)}) collective-permute-start(bf16[1,128,512]{2,1,0:T(8,128)(2,1)S(1)} %slice.73), channel_id=1, source_target_pairs={{0,2},{1,3},{2,0},{3,1},{4,6},{5,7},{6,4},{7,5},{8,10},{9,11},{10,... | collective-permute-start | bytes 393224 | tf_op jit(solution)/shard_map/ppermute | solution.py:25
  54.2 0.4 collective-permute-done.12
  54.7 1.9 %collective-permute-start.13 = (bf16[1,128,256]{2,1,0:T(8,128)(2,1)S(1)}, bf16[1,128,256]{2,1,0:T(8,128)(2,1)S(1)}, u32[]{:S(2)}, u32[]{:S(2)}) collective-permute-start(bf16[1,128,256]{2,1,0:T(8,128)(2,1)S(1)} %slice.74), channel_id=1, source_target_pairs={{0,2},{1,3},{2,0},{3,1},{4,6},{5,7},{6,4},{7,5},{8,10},{9,11},{10,... | collective-permute-start | bytes 196616 | tf_op jit(solution)/shard_map/ppermute | solution.py:25
  56.6 0.0 collective-permute-done.10
  56.6 7.3 %collective-permute-done.7 = bf16[1,128,512]{2,1,0:T(8,128)(2,1)S(1)} collective-permute-done((bf16[1,128,512]{2,1,0:T(8,128)(2,1)S(1)}, bf16[1,128,512]{2,1,0:T(8,128)(2,1)S(1)}, u32[]{:S(2)}, u32[]{:S(2)}) %collective-permute-start.7) | collective-permute-done | bytes 131104 | tf_op jit(solution)/shard_map/ppermute | solution.py:25
  63.9 0.0 copy-done.5
  63.9 0.1 fusion.4
  64.0 1.6 %collective-permute-start.11 = (bf16[128,512]{1,0:T(8,128)(2,1)S(1)}, bf16[128,512]{1,0:T(8,128)(2,1)S(1)}, u32[]{:S(2)}, u32[]{:S(2)}) collective-permute-start(bf16[128,512]{1,0:T(8,128)(2,1)S(1)} %get-tuple-element.24), channel_id=1, source_target_pairs={{4,0},{0,4},{5,1},{1,5},{6,2},{2,6},{7,3},{3,7},{12,8},{8,12},{13,... | collective-permute-start | bytes 393224 | tf_op jit(solution)/shard_map/ppermute | solution.py:31
  65.6 0.5 collective-permute-start.8
  66.1 0.0 collective-permute-done.13
  66.2 1.6 %collective-permute-start.14 = (bf16[128,256]{1,0:T(8,128)(2,1)S(1)}, bf16[128,256]{1,0:T(8,128)(2,1)S(1)}, u32[]{:S(2)}, u32[]{:S(2)}) collective-permute-start(bf16[128,256]{1,0:T(8,128)(2,1)S(1)} %fusion.8), channel_id=1, source_target_pairs={{4,0},{0,4},{5,1},{1,5},{6,2},{2,6},{7,3},{3,7},{12,8},{8,12},{13,... | collective-permute-start | bytes 196616 | tf_op jit(solution)/shard_map/ppermute | solution.py:31
  67.7 5.9 %collective-permute-done.14 = bf16[128,256]{1,0:T(8,128)(2,1)S(1)} collective-permute-done((bf16[128,256]{1,0:T(8,128)(2,1)S(1)}, bf16[128,256]{1,0:T(8,128)(2,1)S(1)}, u32[]{:S(2)}, u32[]{:S(2)}) %collective-permute-start.14) | collective-permute-done | bytes 65568 | tf_op jit(solution)/shard_map/ppermute | solution.py:31
  73.7 0.0 collective-permute-done.11
  73.7 0.0 collective-permute-done.8
  73.7 0.7 %maximum_bitcast_fusion = bf16[1,128,1280]{2,1,0:T(8,128)(2,1)} fusion(bf16[128,256]{1,0:T(8,128)(2,1)S(1)} %collective-permute-done.14, bf16[128,512]{1,0:T(8,128)(2,1)S(1)} %collective-permute-done.11, bf16[128,512]{1,0:T(8,128)(2,1)S(1)} %collective-permute-done.8), kind=kLoop, calls=%fused_computation.2 | loop fusion | flops 983040 | bytes 655360 | tf_op jit(solution)/shard_map/broadcast_in_dim | solution.py:230
  (5 shorter events, 0.1 us)
Async XLA Ops:
  0.0 11.7 %collective-permute-start.2 = (bf16[1,640,256]{2,1,0:T(8,128)(2,1)}, bf16[1,640,256]{2,1,0:T(8,128)(2,1)S(1)}, u32[]{:S(2)}, u32[]{:S(2)}) collective-permute-start(bf16[1,640,256]{2,1,0:T(8,128)(2,1)} %refs_0_.1), channel_id=1, source_target_pairs={{0,16},{8,24},{16,0},{24,8},{1,17},{9,25},{17,1},{25,9},{2,18},{10... | collective-permute-start | bytes 983048 | tf_op jit(solution)/shard_map/ppermute | solution.py:25
  3.0 14.9 %collective-permute-start.4 = (bf16[1,640,256]{2,1,0:T(8,128)(2,1)}, bf16[1,640,256]{2,1,0:T(8,128)(2,1)S(1)}, u32[]{:S(2)}, u32[]{:S(2)}) collective-permute-start(bf16[1,640,256]{2,1,0:T(8,128)(2,1)} %refs_2_.1), channel_id=1, source_target_pairs={{0,16},{8,24},{16,0},{24,8},{1,17},{9,25},{17,1},{25,9},{2,18},{10... | collective-permute-start | bytes 983048 | tf_op jit(solution)/shard_map/ppermute | solution.py:25
  3.0 15.6 %collective-permute-start = (bf16[1,640,256]{2,1,0:T(8,128)(2,1)}, bf16[1,640,256]{2,1,0:T(8,128)(2,1)S(1)}, u32[]{:S(2)}, u32[]{:S(2)}) collective-permute-start(bf16[1,640,256]{2,1,0:T(8,128)(2,1)} %refs_0_.1), channel_id=1, source_target_pairs={{0,8},{8,0},{16,24},{24,16},{1,9},{9,1},{17,25},{25,17},{2,10},{10... | collective-permute-start | bytes 983048 | tf_op jit(solution)/shard_map/ppermute | solution.py:25
  3.0 15.6 %collective-permute-start.1 = (bf16[1,640,256]{2,1,0:T(8,128)(2,1)}, bf16[1,640,256]{2,1,0:T(8,128)(2,1)S(1)}, u32[]{:S(2)}, u32[]{:S(2)}) collective-permute-start(bf16[1,640,256]{2,1,0:T(8,128)(2,1)} %refs_2_.1), channel_id=1, source_target_pairs={{0,8},{8,0},{16,24},{24,16},{1,9},{9,1},{17,25},{25,17},{2,10},{10... | collective-permute-start | bytes 983048 | tf_op jit(solution)/shard_map/ppermute | solution.py:25
  11.7 12.2 %collective-permute-start.3 = (bf16[1,640,256]{2,1,0:T(8,128)(2,1)S(1)}, bf16[1,640,256]{2,1,0:T(8,128)(2,1)S(1)}, u32[]{:S(2)}, u32[]{:S(2)}) collective-permute-start(bf16[1,640,256]{2,1,0:T(8,128)(2,1)S(1)} %collective-permute-done.2.refs_0_), channel_id=1, source_target_pairs={{0,8},{8,0},{16,24},{24,16},{1,9},{9,1},{17,25},{25,17},{2,10},{10... | collective-permute-start | bytes 983048 | tf_op jit(solution)/shard_map/ppermute | solution.py:25
  17.9 8.2 %collective-permute-start.5 = (bf16[1,640,256]{2,1,0:T(8,128)(2,1)S(1)}, bf16[1,640,256]{2,1,0:T(8,128)(2,1)S(1)}, u32[]{:S(2)}, u32[]{:S(2)}) collective-permute-start(bf16[1,640,256]{2,1,0:T(8,128)(2,1)S(1)} %collective-permute-done.4.refs_0_), channel_id=1, source_target_pairs={{0,8},{8,0},{16,24},{24,16},{1,9},{9,1},{17,25},{25,17},{2,10},{10... | collective-permute-start | bytes 983048 | tf_op jit(solution)/shard_map/ppermute | solution.py:25
  18.6 1.0 %copy-start.2 = (bf16[1,128,1024]{2,1,0:T(8,128)(2,1)S(1)}, bf16[1,128,1024]{2,1,0:T(8,128)(2,1)}, u32[]{:S(2)}) copy-start(bf16[1,128,1024]{2,1,0:T(8,128)(2,1)} %q_ref.3) | copy-start | bytes 786436
  19.5 1.0 %copy-start.3 = (bf16[1,640,256]{2,1,0:T(8,128)(2,1)S(1)}, bf16[1,640,256]{2,1,0:T(8,128)(2,1)}, u32[]{:S(2)}) copy-start(bf16[1,640,256]{2,1,0:T(8,128)(2,1)} %refs_0_.1) | copy-start | bytes 983044
  20.5 1.0 %copy-start.4 = (bf16[1,640,256]{2,1,0:T(8,128)(2,1)S(1)}, bf16[1,640,256]{2,1,0:T(8,128)(2,1)}, u32[]{:S(2)}) copy-start(bf16[1,640,256]{2,1,0:T(8,128)(2,1)} %refs_2_.1) | copy-start | bytes 983044
  26.1 4.0 %copy-start = (bf16[1,1024,5120]{2,1,0:T(8,128)(2,1)S(1)}, bf16[1,1024,5120]{2,1,0:T(8,128)(2,1)}, u32[]{:S(2)}) copy-start(bf16[1,1024,5120]{2,1,0:T(8,128)(2,1)} %w_ref.9) | copy-start | bytes 31457284
  30.1 4.0 %copy-start.1 = (bf16[1,1024,5120]{2,1,0:T(8,128)(2,1)S(1)}, bf16[1,1024,5120]{2,1,0:T(8,128)(2,1)}, u32[]{:S(2)}) copy-start(bf16[1,1024,5120]{2,1,0:T(8,128)(2,1)} %w_ref.9) | copy-start | bytes 31457284
  34.6 9.2 %collective-permute-start.9 = (bf16[2,128,512]{2,1,0:T(8,128)(2,1)S(1)}, bf16[2,128,512]{2,1,0:T(8,128)(2,1)S(1)}, u32[]{:S(2)}, u32[]{:S(2)}) collective-permute-start(bf16[2,128,512]{2,1,0:T(8,128)(2,1)S(1)} %shard_map.69), channel_id=1, source_target_pairs={{0,1},{1,0},{2,3},{3,2},{4,5},{5,4},{6,7},{7,6},{8,9},{9,8},{10,11... | collective-permute-start | bytes 786440 | tf_op jit(solution)/shard_map/ppermute | solution.py:25
  36.4 15.7 %collective-permute-start.6 = (bf16[2,128,512]{2,1,0:T(8,128)(2,1)S(1)}, bf16[2,128,512]{2,1,0:T(8,128)(2,1)S(1)}, u32[]{:S(2)}, u32[]{:S(2)}) collective-permute-start(bf16[2,128,512]{2,1,0:T(8,128)(2,1)S(1)} %get-tuple-element.22), channel_id=1, source_target_pairs={{0,1},{1,0},{2,3},{3,2},{4,5},{5,4},{6,7},{7,6},{8,9},{9,8},{10,11... | collective-permute-start | bytes 786440 | tf_op jit(solution)/shard_map/ppermute | solution.py:25
  37.0 17.6 %collective-permute-start.12 = (bf16[2,128,256]{2,1,0:T(8,128)(2,1)S(1)}, bf16[2,128,256]{2,1,0:T(8,128)(2,1)S(1)}, u32[]{:S(2)}, u32[]{:S(2)}) collective-permute-start(bf16[2,128,256]{2,1,0:T(8,128)(2,1)S(1)} %shard_map.71), channel_id=1, source_target_pairs={{0,1},{1,0},{2,3},{3,2},{4,5},{5,4},{6,7},{7,6},{8,9},{9,8},{10,11... | collective-permute-start | bytes 393224 | tf_op jit(solution)/shard_map/ppermute | solution.py:25
  43.8 20.1 %copy-start.5 = (bf16[1,128,1280]{2,1,0:T(8,128)(2,1)S(1)}, bf16[1,128,1280]{2,1,0:T(8,128)(2,1)}, u32[]{:S(2)}) copy-start(bf16[1,128,1280]{2,1,0:T(8,128)(2,1)} %param.10) | copy-start | bytes 983044
  43.8 12.8 %collective-permute-start.10 = (bf16[1,128,512]{2,1,0:T(8,128)(2,1)S(1)}, bf16[1,128,512]{2,1,0:T(8,128)(2,1)S(1)}, u32[]{:S(2)}, u32[]{:S(2)}) collective-permute-start(bf16[1,128,512]{2,1,0:T(8,128)(2,1)S(1)} %slice.72), channel_id=1, source_target_pairs={{0,2},{1,3},{2,0},{3,1},{4,6},{5,7},{6,4},{7,5},{8,10},{9,11},{10,... | collective-permute-start | bytes 393224 | tf_op jit(solution)/shard_map/ppermute | solution.py:25
  52.3 11.7 %collective-permute-start.7 = (bf16[1,128,512]{2,1,0:T(8,128)(2,1)S(1)}, bf16[1,128,512]{2,1,0:T(8,128)(2,1)S(1)}, u32[]{:S(2)}, u32[]{:S(2)}) collective-permute-start(bf16[1,128,512]{2,1,0:T(8,128)(2,1)S(1)} %slice.73), channel_id=1, source_target_pairs={{0,2},{1,3},{2,0},{3,1},{4,6},{5,7},{6,4},{7,5},{8,10},{9,11},{10,... | collective-permute-start | bytes 393224 | tf_op jit(solution)/shard_map/ppermute | solution.py:25
  54.7 11.4 %collective-permute-start.13 = (bf16[1,128,256]{2,1,0:T(8,128)(2,1)S(1)}, bf16[1,128,256]{2,1,0:T(8,128)(2,1)S(1)}, u32[]{:S(2)}, u32[]{:S(2)}) collective-permute-start(bf16[1,128,256]{2,1,0:T(8,128)(2,1)S(1)} %slice.74), channel_id=1, source_target_pairs={{0,2},{1,3},{2,0},{3,1},{4,6},{5,7},{6,4},{7,5},{8,10},{9,11},{10,... | collective-permute-start | bytes 196616 | tf_op jit(solution)/shard_map/ppermute | solution.py:25
  64.0 9.6 %collective-permute-start.11 = (bf16[128,512]{1,0:T(8,128)(2,1)S(1)}, bf16[128,512]{1,0:T(8,128)(2,1)S(1)}, u32[]{:S(2)}, u32[]{:S(2)}) collective-permute-start(bf16[128,512]{1,0:T(8,128)(2,1)S(1)} %get-tuple-element.24), channel_id=1, source_target_pairs={{4,0},{0,4},{5,1},{1,5},{6,2},{2,6},{7,3},{3,7},{12,8},{8,12},{13,... | collective-permute-start | bytes 393224 | tf_op jit(solution)/shard_map/ppermute | solution.py:31
  65.6 8.1 %collective-permute-start.8 = (bf16[128,512]{1,0:T(8,128)(2,1)S(1)}, bf16[128,512]{1,0:T(8,128)(2,1)S(1)}, u32[]{:S(2)}, u32[]{:S(2)}) collective-permute-start(bf16[128,512]{1,0:T(8,128)(2,1)S(1)} %get-tuple-element.23), channel_id=1, source_target_pairs={{4,0},{0,4},{5,1},{1,5},{6,2},{2,6},{7,3},{3,7},{12,8},{8,12},{13,... | collective-permute-start | bytes 393224 | tf_op jit(solution)/shard_map/ppermute | solution.py:31
  66.2 7.5 %collective-permute-start.14 = (bf16[128,256]{1,0:T(8,128)(2,1)S(1)}, bf16[128,256]{1,0:T(8,128)(2,1)S(1)}, u32[]{:S(2)}, u32[]{:S(2)}) collective-permute-start(bf16[128,256]{1,0:T(8,128)(2,1)S(1)} %fusion.8), channel_id=1, source_target_pairs={{4,0},{0,4},{5,1},{1,5},{6,2},{2,6},{7,3},{3,7},{12,8},{8,12},{13,... | collective-permute-start | bytes 196616 | tf_op jit(solution)/shard_map/ppermute | solution.py:31

commit v2 on v1

v2 whole, which is shorter than its diff:
```python
import functools
import math

import jax
import jax.numpy as jnp
from jax import lax
from jax.experimental import pallas as pl
from jax.experimental.pallas import tpu as pltpu
from jax.sharding import PartitionSpec as P

HD = 128
G = 4
LANES = 128
NEG_FILL = -1e30
MAX_FLOOR = -1e29
EXP_SCALE = HD ** (-0.5) * math.log2(math.e)
MIB = 1 << 20

WHOLE = pl.BlockSpec(memory_space=pltpu.VMEM)
IN_HBM = pl.BlockSpec(memory_space=pltpu.HBM)
SCALARS = pl.BlockSpec(memory_space=pltpu.SMEM)


def exchange(block, axis, mask):
    route = [(i, i ^ mask) for i in range(lax.axis_size(axis))]
    return lax.ppermute(block, axis, route)


def handed(block, mask):
    sections, n_tp = lax.axis_size("section"), lax.axis_size("tp")
    route = [(s * n_tp + i, (s + 1) % sections * n_tp + (i ^ mask)) for s in range(sections) for i in range(n_tp)]
    return lax.ppermute(block, ("section", "tp"), route)


def in_vmem(array):
    return pltpu.with_memory_space_constraint(array, pltpu.VMEM)


def local_call(body, ins, outs, limit, flops, scratch=()):
    return pl.pallas_call(
        body,
        in_specs=ins,
        out_shape=[pltpu.VMEM(shape, dtype) for shape, dtype in outs],
        out_specs=[WHOLE] * len(outs),
        scratch_shapes=list(scratch),
        compiler_params=pltpu.CompilerParams(vmem_limit_bytes=limit),
        cost_estimate=pl.CostEstimate(flops=0 * flops, bytes_accessed=0, transcendentals=0),
    )


def stacked_query(q_ref, kv_head):
    heads = range(kv_head * G, (kv_head + 1) * G)
    return jnp.concatenate([q_ref[0, :, h * HD : (h + 1) * HD] for h in heads], axis=0)


def masked_scores(query, key_ref, kv_head, bound):
    keys = key_ref[0, :, kv_head * HD : (kv_head + 1) * HD]
    scores = lax.dot_general(query, keys, (((1,), (1,)), ((), ())), preferred_element_type=jnp.float32)
    rows = query.shape[0] // G
    ahead = lax.broadcasted_iota(jnp.int32, scores.shape, 1) - lax.broadcasted_iota(jnp.int32, scores.shape, 0) % rows
    return jnp.where(ahead <= bound, scores, NEG_FILL)


def early_kernel(masks, offset_ref, q_hbm, key_hbm, value_hbm, w_hbm, *refs):
    count = len(masks)
    key_refs, value_refs = list(refs[: count - 1]), list(refs[count - 1 : 2 * count - 2])
    max_ref, sum_ref, acc_ref, query_ref, w_ref, q_ref, key_ref, value_ref, sems = refs[2 * count - 2 :]
    sources = (q_hbm, key_hbm, value_hbm, w_hbm)
    targets = (q_ref, key_ref, value_ref, w_ref)
    copies = [pltpu.make_async_copy(a, b, sems.at[i]) for i, (a, b) in enumerate(zip(sources, targets))]
    for copy in copies:
        copy.start()
    for copy in copies[:3]:
        copy.wait()
    key_refs, value_refs = [key_ref] + key_refs, [value_ref] + value_refs
    own = lax.axis_index("ctx")
    rows, length = q_ref.shape[1], key_refs[0].shape[1]
    first_row = offset_ref[0] + own * rows
    for kv_head in range(key_refs[0].shape[2] // HD):
        columns = slice(kv_head * HD, (kv_head + 1) * HD)
        query = stacked_query(q_ref, kv_head)
        query_ref[kv_head] = query
        parts = [
            masked_scores(query, ref, kv_head, first_row - (own ^ mask) * length) for ref, mask in zip(key_refs, masks)
        ]
        top = functools.reduce(jnp.maximum, [jnp.max(part, axis=1, keepdims=True) for part in parts])
        top = jnp.maximum(top, MAX_FLOOR)
        weights = [jnp.exp2((part - top) * EXP_SCALE) for part in parts]
        total = sum(jnp.sum(part, axis=1, keepdims=True) for part in weights)
        mixed = sum(
            jnp.dot(part.astype(jnp.bfloat16), ref[0, :, columns], preferred_element_type=jnp.float32)
            for part, ref in zip(weights, value_refs)
        )
        max_ref[kv_head] = jnp.broadcast_to(top, max_ref.shape[1:])
        sum_ref[kv_head] = jnp.broadcast_to(total, sum_ref.shape[1:])
        acc_ref[kv_head] = mixed
    copies[3].wait()


def late_kernel(masks, offset_ref, q_ref, max_ref, sum_ref, acc_ref, *refs):
    count = len(masks)
    key_refs, refs = refs[:count], refs[count:]
    outs = refs[-(3 + count) :]
    before_refs = refs[: -(3 + count)]
    top_ref, total_ref, scaled_ref = outs[:3]
    weight_refs = outs[3:]
    own = lax.axis_index("ctx")
    rows, length = q_ref.shape[1] // G, key_refs[0].shape[1]
    first_row = offset_ref[0] + own * rows
    for kv_head in range(key_refs[0].shape[2] // HD):
        columns = slice(kv_head * HD, (kv_head + 1) * HD)
        parts = [
            masked_scores(q_ref[kv_head], ref, kv_head, first_row - (own ^ mask) * length)
            for ref, mask in zip(key_refs, masks)
        ]
        before = max_ref[kv_head]
        top = functools.reduce(jnp.maximum, [jnp.max(part, axis=1, keepdims=True) for part in parts])
        top = jnp.maximum(top, before[:, :1])
        weights = [jnp.exp2((part - top) * EXP_SCALE) for part in parts]
        total = sum(jnp.sum(part, axis=1, keepdims=True) for part in weights)
        factor = jnp.exp2((before - top) * EXP_SCALE)
        mixed = acc_ref[kv_head]
        if before_refs:
            mixed += jnp.dot(
                before_refs[0][kv_head], before_refs[1][0, :, columns], preferred_element_type=jnp.float32
            )
        top_ref[kv_head] = jnp.broadcast_to(top, before.shape)
        total_ref[kv_head] = sum_ref[kv_head] * factor + total
        scaled_ref[kv_head] = mixed * factor
        for ref, part in zip(weight_refs, weights):
            ref[kv_head] = part.astype(jnp.bfloat16)


def project(att, weight_ref, out_refs, blocks, block_width, lower):
    slots = []
    for ref in out_refs:
        slots += [ref.at[i] for i in range(ref.shape[0])] if len(ref.shape) == 3 else [ref]
    for ref, block in zip(slots, blocks):
        start = pl.multiple_of(block * block_width + lower, LANES)
        ref[...] = jnp.dot(
            att, weight_ref[0, :, pl.ds(start, ref.shape[1])], preferred_element_type=jnp.float32
        ).astype(jnp.bfloat16)


def finish_kernel(count, blocks_of, block_width, lower, total_ref, scaled_ref, *refs):
    value_refs, weight_refs = refs[:count], refs[count : 2 * count]
    w_ref, att_ref, out_ref = refs[2 * count :]
    rows = att_ref.shape[0]
    for kv_head in range(scaled_ref.shape[0]):
        columns = slice(kv_head * HD, (kv_head + 1) * HD)
        mixed = scaled_ref[kv_head]
        for value_ref, part_ref in zip(value_refs, weight_refs):
            mixed += jnp.dot(part_ref[kv_head], value_ref[0, :, columns], preferred_element_type=jnp.float32)
        attended = (mixed / total_ref[kv_head]).astype(jnp.bfloat16)
        for g in range(G):
            head = kv_head * G + g
            att_ref[:, head * HD : (head + 1) * HD] = attended[g * rows : (g + 1) * rows]
    project(att_ref[...], w_ref, [out_ref], blocks_of(lax.axis_index("tp")), block_width, lower)


def project_kernel(blocks_of, block_width, lower, att_ref, w_ref, *out_refs):
    project(att_ref[...], w_ref, out_refs, blocks_of(lax.axis_index("tp")), block_width, lower)


def xor_order(lowest, size):
    if lowest >= size:
        return [0]
    rest = xor_order(lowest * 2, size)
    return [x + lowest for x in rest] + rest


def chunk_plan(width):
    units = width // LANES
    first = (units + 1) // 2
    return [u * LANES for u in (first, units - first) if u > 0]


def on_device(row_offsets, queries, cache_keys, cache_values, residual, out_weight):
    n_ctx, n_tp = lax.axis_size("ctx"), lax.axis_size("tp")
    rows, length = queries.shape[1], cache_keys.shape[1]
    kv_local = cache_keys.shape[2] // HD
    stacked = G * rows
    top_bit = n_ctx // 2
    block_width = out_weight.shape[2] // n_tp

    far_key = exchange(cache_keys, "ctx", top_bit)
    far_value = exchange(cache_values, "ctx", top_bit)
    near = [(0, cache_keys, cache_values)]
    bit = top_bit // 2
    while bit:
        near += [(m | bit, exchange(k, "ctx", bit), exchange(v, "ctx", bit)) for m, k, v in near]
        bit //= 2
    state = [((kv_local, stacked, HD), jnp.float32)] * 3
    half_flops = 4 * kv_local * stacked * length * HD * len(near)
    local = [queries, cache_keys, cache_values, out_weight]
    top, total, acc, query, weight = local_call(
        functools.partial(early_kernel, [m for m, _, _ in near]),
        [SCALARS] + [IN_HBM] * 4 + [WHOLE] * (2 * len(near) - 2),
        state + [((kv_local, stacked, HD), jnp.bfloat16), (out_weight.shape, out_weight.dtype)],
        32 * MIB,
        half_flops,
        [pltpu.VMEM(a.shape, a.dtype) for a in local[:3]] + [pltpu.SemaphoreType.DMA((4,))],
    )(
        row_offsets,
        *[pltpu.with_memory_space_constraint(a, pltpu.HBM) for a in local],
        *[in_vmem(k) for _, k, _ in near[1:]],
        *[in_vmem(v) for _, _, v in near[1:]],
    )
    near_key, top = lax.optimization_barrier((far_key, top))
    far_keys = [(top_bit, near_key)]
    bit = top_bit // 2
    while bit:
        far_keys += [(m | bit, exchange(k, "ctx", bit)) for m, k in far_keys]
        bit //= 2

    def late(masks, outs, *operands):
        return local_call(
            functools.partial(late_kernel, masks),
            [SCALARS] + [WHOLE] * len(operands),
            state + [((kv_local, stacked, length), jnp.bfloat16)] * len(masks),
            32 * MIB,
            half_flops,
        )(row_offsets, *operands)

    top, total, acc, far_weights = late([top_bit], 0, query, top, total, acc, in_vmem(far_key))
    far_value, total = lax.optimization_barrier((far_value, total))
    far_values = [far_value]
    bit = top_bit // 2
    while bit:
        far_values += [exchange(v, "ctx", bit) for v in far_values]
        bit //= 2
    masks, keys = zip(*far_keys[1:])
    top, total, acc, *weights = late(
        list(masks), 0, query, top, total, acc, *[in_vmem(k) for k in keys], far_weights, in_vmem(far_value)
    )
    far_values = far_values[1:]

    order = xor_order(2, n_tp)
    across = order[:-1]
    widths = chunk_plan(block_width)
    lowers = [sum(widths[:i]) for i in range(len(widths))]
    block_flops = 2 * rows * out_weight.shape[1]
    attended, send = local_call(
        functools.partial(finish_kernel, len(far_values), lambda me: [me ^ 1 ^ x for x in across], block_width, 0),
        [WHOLE] * (3 + 2 * len(far_values)),
        [((rows, out_weight.shape[1]), jnp.bfloat16), ((len(across), rows, widths[0]), jnp.bfloat16)],
        16 * MIB,
        half_flops // 2 + block_flops * widths[0] * len(across),
    )(total, acc, *[in_vmem(v) for v in far_values], *weights, weight)

    def projected(masks, lower, width, stack=False):
        shapes = [((len(masks), rows, width), jnp.bfloat16)] if stack else [((rows, width), jnp.bfloat16)] * len(masks)
        return local_call(
            functools.partial(project_kernel, lambda me: [me ^ x for x in masks], block_width, lower),
            [WHOLE] * 2,
            shapes,
            16 * MIB,
            block_flops * width * len(masks),
        )(attended, weight)

    firsts = []
    for lower, width in zip(lowers, widths):
        if lower:
            (send,) = projected([1 ^ x for x in across], lower, width, True)
        firsts.append(exchange(send, "tp", 1))
    pair, own = projected([1, 0], 0, block_width)
    kept = [projected(across, lower, width) for lower, width in zip(lowers, widths)]
    own = (own.astype(jnp.float32) + residual[0].astype(jnp.float32)).astype(jnp.bfloat16)
    whole = [handed(own, 0), handed(pair, 1)]
    outs = []
    for lower, width, first, part in zip(lowers, widths, firsts, kept):
        part = [a.astype(jnp.float32) + first[i].astype(jnp.float32) for i, a in enumerate(part)]
        terms = [a[:, lower : lower + width] for a in whole]
        bit = 2
        while bit < n_tp:
            half = (len(part) + 1) // 2
            sends = [a.astype(jnp.bfloat16) for a in part[:half]]
            received = [exchange(a, "tp", bit) for a in sends[:-1]]
            terms.append(handed(sends[-1], bit))
            part = [a + r.astype(jnp.float32) for a, r in zip(part[half:], received)]
            bit *= 2
        outs.append(sum(term.astype(jnp.float32) for term in terms).astype(jnp.bfloat16))
    return jnp.concatenate(outs, axis=1)[None]


def solution(mesh):
    placed = (
        P("section"),
        P("section", "ctx", "tp"),
        P("section", "ctx", "tp"),
        P("section", "ctx", "tp"),
        P("section", "ctx", "tp"),
        P("section", "tp", None),
    )
    return jax.shard_map(
        on_device, mesh=mesh, in_specs=placed, out_specs=P("section", "ctx", "tp"), check_vma=False
    )
```

time: 74.7 us -> 54.1 us (0.72)
  waiting for transfers between devices: 37.1 us -> 20.5 us
  local copies, waits for them, and re-layouts: 9.72 us -> 0.01 us
  Pallas kernels: 7.82 us -> 11.2 us
  starting transfers between devices: 17.9 us -> 20.4 us
    ppermute x12 -> x8, waiting for transfers between devices: 31.2 us -> 10.3 us  [exchange(): return lax.ppermute(block, axis, route)]
    ppermute x3 -> x4, starting transfers between devices: 3.65 us -> 14.8 us  [handed(): return lax.ppermute(block, ('section', 'tp'), route)]
    unnamed x12 -> x2, local copies, waits for them, and re-layouts: 9.67 us -> 0.01 us
    ppermute x12 -> x8, starting transfers between devices: 14.2 us -> 5.61 us  [exchange(): return lax.ppermute(block, axis, route)]
    ppermute x3 -> x4, waiting for transfers between devices: 5.92 us -> 10.3 us  [handed(): return lax.ppermute(block, ('section', 'tp'), route)]
    pallas_call x8, Pallas kernels: 7.82 us -> 11.2 us  [the longest x1 4.32 us: on_device(): local_call(functools.partial(early_kernel, [m for m, _, _ in near]), [SCA...]
  transfers between devices with their start and end apart: 15 -> 12, of which waited for: 7 -> 5; matrix products, arithmetic and copies ran while one was open for 0% -> 0% of each run, Pallas kernels for 8% -> 16%
where the time goes in v2:
time: 54.1 us; the launch traced here: 53.9 us
  waiting for transfers between devices  20.5 us (38%)
  starting transfers between devices  20.4 us (38%)
  Pallas kernels  11.2 us (21%)
  other arithmetic  1.05 us (2%)
  between operations  0.75 us (1%)
    ppermute x4, starting transfers between devices, handed(): return lax.ppermute(block, ('section', 'tp'), route)  14.8 us
    ppermute x4, waiting for transfers between devices, handed(): return lax.ppermute(block, ('section', 'tp'), route)  10.3 us
    ppermute x8, waiting for transfers between devices, exchange(): return lax.ppermute(block, axis, route)  10.3 us
    ppermute x8, starting transfers between devices, exchange(): return lax.ppermute(block, axis, route)  5.61 us
    pallas_call x1, Pallas kernels, on_device(): local_call(functools.partial(early_kernel, [m for m, _, _ in near]), [SCA...  4.32 us
    pallas_call x2, Pallas kernels, late(): local_call(functools.partial(late_kernel, masks), [SCALARS] + [WHOLE] * l...  4.04 us
    pallas_call x4, Pallas kernels, projected(): local_call(functools.partial(project_kernel, lambda me: [me ^ x for x in...  2.11 us
  transfers between devices with their start and end apart: 12, of which 5 were waited for; matrix products, arithmetic and copies ran while one was open for 0% of the time, Pallas kernels for 16%

profile of v2, /device:TPU:0, one launch (start us, length us, event | category | flops | bytes accessed | tf_op | source)
XLA Modules:
  0.0 53.9 jit_solution(15710639390438204157)
XLA Ops:
  0.0 0.5 collective-permute-start
  0.5 0.1 collective-permute-start.1
  0.5 3.0 %collective-permute-start.2 = (bf16[1,640,256]{2,1,0:T(8,128)(2,1)}, bf16[1,640,256]{2,1,0:T(8,128)(2,1)S(1)}, u32[]{:S(2)}, u32[]{:S(2)}) collective-permute-start(bf16[1,640,256]{2,1,0:T(8,128)(2,1)} %key_hbm.1), channel_id=1, source_target_pairs={{0,16},{8,24},{16,0},{24,8},{1,17},{9,25},{17,1},{25,9},{2,18},{10... | collective-permute-start | bytes 983048 | tf_op jit(solution)/shard_map/ppermute | solution.py:26
  3.5 0.0 collective-permute-start.3
  4.2 0.0 collective-permute-done.refs_0_
  4.2 0.0 collective-permute-done.1.refs_1_
  4.2 4.3 %shard_map.64 = (f32[2,512,128]{2,1,0:T(8,128)S(1)}, f32[2,512,128]{2,1,0:T(8,128)S(1)}, f32[2,512,128]{2,1,0:T(8,128)S(1)}, bf16[2,512,128]{2,1,0:T(8,128)(2,1)S(1)}, bf16[1,1024,5120]{2,1,0:T(8,128)(2,1)S(1)}) custom-call(s32[1]{0:T(128)S(6)} %copy.7.offset_ref, bf16[1,128,1024]{2,1,0:T(8,128)(2,1)} %q_hbm.1, bf16[1,640,256]{2,1,0:T(8,128)(2,1)} %key_hbm.1, ...), custom_call_target="tpu_custom_call" | custom-call | tf_op jit(solution)/shard_map/pallas_call | solution.py:196
  8.5 3.7 %collective-permute-done.2.refs_0_ = bf16[1,640,256]{2,1,0:T(8,128)(2,1)S(1)} collective-permute-done((bf16[1,640,256]{2,1,0:T(8,128)(2,1)}, bf16[1,640,256]{2,1,0:T(8,128)(2,1)S(1)}, u32[]{:S(2)}, u32[]{:S(2)}) %collective-permute-start.2) | collective-permute-done | bytes 327712 | tf_op jit(solution)/shard_map/ppermute | solution.py:26
  12.2 0.0 collective-permute-start.4
  12.2 1.4 %shard_map.65 = (f32[2,512,128]{2,1,0:T(8,128)S(1)}, f32[2,512,128]{2,1,0:T(8,128)S(1)}, f32[2,512,128]{2,1,0:T(8,128)S(1)}, bf16[2,512,640]{2,1,0:T(8,128)(2,1)S(1)}) custom-call(s32[1]{0:T(128)S(6)} %copy.7.offset_ref, bf16[2,512,128]{2,1,0:T(8,128)(2,1)S(1)} %get-tuple-element.25.q_ref, f32[2,512,128]{2,1,0:T(8,128)S(1)} %get-tuple-element.27.max_ref, ...), custom_call_target="tpu_custom_call" | custom-call | tf_op jit(solution)/shard_map/pallas_call | solution.py:217
  13.6 5.0 %collective-permute-done.3.refs_2_ = bf16[1,640,256]{2,1,0:T(8,128)(2,1)S(1)} collective-permute-done((bf16[1,640,256]{2,1,0:T(8,128)(2,1)}, bf16[1,640,256]{2,1,0:T(8,128)(2,1)S(1)}, u32[]{:S(2)}, u32[]{:S(2)}) %collective-permute-start.3) | collective-permute-done | bytes 327712 | tf_op jit(solution)/shard_map/ppermute | solution.py:26
  18.6 0.0 collective-permute-start.5
  18.6 0.0 collective-permute-done.4.refs_0_
  18.6 2.7 %shard_map.66 = (f32[2,512,128]{2,1,0:T(8,128)}, f32[2,512,128]{2,1,0:T(8,128)S(1)}, f32[2,512,128]{2,1,0:T(8,128)S(1)}, bf16[2,512,640]{2,1,0:T(8,128)(2,1)S(1)}) custom-call(s32[1]{0:T(128)S(6)} %copy.7.offset_ref, bf16[2,512,128]{2,1,0:T(8,128)(2,1)S(1)} %get-tuple-element.25.q_ref, f32[2,512,128]{2,1,0:T(8,128)S(1)} %get-tuple-element.30.max_ref, ...), custom_call_target="tpu_custom_call" | custom-call | tf_op jit(solution)/shard_map/pallas_call | solution.py:217
  21.3 0.0 collective-permute-done.5.refs_0_
  21.3 0.8 %shard_map.67 = (bf16[128,1024]{1,0:T(8,128)(2,1)S(1)}, bf16[1,128,640]{2,1,0:T(8,128)(2,1)S(1)}) custom-call(f32[2,512,128]{2,1,0:T(8,128)S(1)} %get-tuple-element.37.total_ref, f32[2,512,128]{2,1,0:T(8,128)S(1)} %get-tuple-element.38.scaled_ref, bf16[1,640,256]{2,1,0:T(8,128)(2,1)S(1)} %collective-permute-done.5.refs_0_, ...), custom_call_target="tpu_custom_call" | custom-call | tf_op jit(solution)/shard_map/pallas_call | solution.py:243
  22.0 0.4 shard_map.71
  22.5 0.4 shard_map.70
  22.9 0.0 copy-start
  22.9 0.4 shard_map.69
  23.3 0.9 %shard_map.68 = (bf16[128,1280]{1,0:T(8,128)(2,1)S(1)}, bf16[128,1280]{1,0:T(8,128)(2,1)S(1)}) custom-call(bf16[128,1024]{1,0:T(8,128)(2,1)S(1)} %get-tuple-element.41.att_ref, bf16[1,1024,5120]{2,1,0:T(8,128)(2,1)S(1)} %get-tuple-element.40.refs_2_.w_ref), custom_call_target="tpu_custom_call" | custom-call | tf_op jit(solution)/shard_map/pallas_call | solution.py:253
  24.2 1.9 %collective-permute-start.10 = (bf16[1,128,640]{2,1,0:T(8,128)(2,1)S(1)}, bf16[1,128,640]{2,1,0:T(8,128)(2,1)S(1)}, u32[]{:S(2)}, u32[]{:S(2)}) collective-permute-start(bf16[1,128,640]{2,1,0:T(8,128)(2,1)S(1)} %shard_map.71), channel_id=1, source_target_pairs={{0,1},{1,0},{2,3},{3,2},{4,5},{5,4},{6,7},{7,6},{8,9},{9,8},{10,11... | collective-permute-start | bytes 491528 | tf_op jit(solution)/shard_map/ppermute | solution.py:26
  26.0 0.2 collective-permute-start.8
  26.3 0.0 copy-done
  26.3 0.1 fusion
  26.4 1.8 %collective-permute-start.6 = (bf16[128,1280]{1,0:T(8,128)(2,1)S(1)}, bf16[128,1280]{1,0:T(8,128)(2,1)S(1)}, u32[]{:S(2)}, u32[]{:S(2)}) collective-permute-start(bf16[128,1280]{1,0:T(8,128)(2,1)S(1)} %fusion), channel_id=1, source_target_pairs={{0,4},{1,5},{2,6},{3,7},{4,0},{5,1},{6,2},{7,3},{8,12},{9,13},{10,... | collective-permute-start | bytes 983048 | tf_op jit(solution)/shard_map/ppermute | solution.py:32
  28.1 1.5 %collective-permute-start.7 = (bf16[128,1280]{1,0:T(8,128)(2,1)S(1)}, bf16[128,1280]{1,0:T(8,128)(2,1)S(1)}, u32[]{:S(2)}, u32[]{:S(2)}) collective-permute-start(bf16[128,1280]{1,0:T(8,128)(2,1)S(1)} %get-tuple-element.43), channel_id=1, source_target_pairs={{0,5},{1,4},{2,7},{3,6},{4,1},{5,0},{6,3},{7,2},{8,13},{9,12},{10,... | collective-permute-start | bytes 983048 | tf_op jit(solution)/shard_map/ppermute | solution.py:32
  29.7 1.6 %collective-permute-done.10 = bf16[1,128,640]{2,1,0:T(8,128)(2,1)S(1)} collective-permute-done((bf16[1,128,640]{2,1,0:T(8,128)(2,1)S(1)}, bf16[1,128,640]{2,1,0:T(8,128)(2,1)S(1)}, u32[]{:S(2)}, u32[]{:S(2)}) %collective-permute-start.10) | collective-permute-done | bytes 163872 | tf_op jit(solution)/shard_map/ppermute | solution.py:26
  31.3 3.8 %collective-permute-start.11 = (bf16[128,640]{1,0:T(8,128)(2,1)S(1)}, bf16[128,640]{1,0:T(8,128)(2,1)S(1)}, u32[]{:S(2)}, u32[]{:S(2)}) collective-permute-start(bf16[128,640]{1,0:T(8,128)(2,1)S(1)} %fusion.1), channel_id=1, source_target_pairs={{0,6},{1,7},{2,4},{3,5},{4,2},{5,3},{6,0},{7,1},{8,14},{9,15},{10,... | collective-permute-start | bytes 491528 | tf_op jit(solution)/shard_map/ppermute | solution.py:32
  35.1 0.0 collective-permute-done.8
  35.1 7.7 %collective-permute-start.9 = (bf16[128,640]{1,0:T(8,128)(2,1)S(1)}, bf16[128,640]{1,0:T(8,128)(2,1)S(1)}, u32[]{:S(2)}, u32[]{:S(2)}) collective-permute-start(bf16[128,640]{1,0:T(8,128)(2,1)S(1)} %fusion.2), channel_id=1, source_target_pairs={{0,6},{1,7},{2,4},{3,5},{4,2},{5,3},{6,0},{7,1},{8,14},{9,15},{10,... | collective-permute-start | bytes 491528 | tf_op jit(solution)/shard_map/ppermute | solution.py:32
  42.8 1.9 %collective-permute-done.11 = bf16[128,640]{1,0:T(8,128)(2,1)S(1)} collective-permute-done((bf16[128,640]{1,0:T(8,128)(2,1)S(1)}, bf16[128,640]{1,0:T(8,128)(2,1)S(1)}, u32[]{:S(2)}, u32[]{:S(2)}) %collective-permute-start.11) | collective-permute-done | bytes 163872 | tf_op jit(solution)/shard_map/ppermute | solution.py:32
  44.7 8.4 %collective-permute-done.9 = bf16[128,640]{1,0:T(8,128)(2,1)S(1)} collective-permute-done((bf16[128,640]{1,0:T(8,128)(2,1)S(1)}, bf16[128,640]{1,0:T(8,128)(2,1)S(1)}, u32[]{:S(2)}, u32[]{:S(2)}) %collective-permute-start.9) | collective-permute-done | bytes 163872 | tf_op jit(solution)/shard_map/ppermute | solution.py:32
  53.1 0.0 collective-permute-done.6
  53.1 0.0 collective-permute-done.7
  53.1 0.1 add_convert_fusion.1
  53.2 0.8 %maximum_bitcast_fusion = bf16[1,128,1280]{2,1,0:T(8,128)(2,1)} fusion(bf16[128,640]{1,0:T(8,128)(2,1)S(1)} %get-tuple-element.46, bf16[128,640]{1,0:T(8,128)(2,1)S(1)} %get-tuple-element.45), kind=kLoop, calls=%fused_computation.2 | loop fusion | flops 655360 | bytes 655360 | tf_op jit(solution)/shard_map/broadcast_in_dim | solution.py:283
  (2 shorter events, 0.1 us)
Async XLA Ops:
  0.0 4.2 %collective-permute-start = (bf16[1,640,256]{2,1,0:T(8,128)(2,1)}, bf16[1,640,256]{2,1,0:T(8,128)(2,1)S(1)}, u32[]{:S(2)}, u32[]{:S(2)}) collective-permute-start(bf16[1,640,256]{2,1,0:T(8,128)(2,1)} %key_hbm.1), channel_id=1, source_target_pairs={{0,8},{8,0},{16,24},{24,16},{1,9},{9,1},{17,25},{25,17},{2,10},{10... | collective-permute-start | bytes 983048 | tf_op jit(solution)/shard_map/ppermute | solution.py:26
  0.5 3.7 %collective-permute-start.1 = (bf16[1,640,256]{2,1,0:T(8,128)(2,1)}, bf16[1,640,256]{2,1,0:T(8,128)(2,1)S(1)}, u32[]{:S(2)}, u32[]{:S(2)}) collective-permute-start(bf16[1,640,256]{2,1,0:T(8,128)(2,1)} %value_hbm.1), channel_id=1, source_target_pairs={{0,8},{8,0},{16,24},{24,16},{1,9},{9,1},{17,25},{25,17},{2,10},{10... | collective-permute-start | bytes 983048 | tf_op jit(solution)/shard_map/ppermute | solution.py:26
  0.5 11.7 %collective-permute-start.2 = (bf16[1,640,256]{2,1,0:T(8,128)(2,1)}, bf16[1,640,256]{2,1,0:T(8,128)(2,1)S(1)}, u32[]{:S(2)}, u32[]{:S(2)}) collective-permute-start(bf16[1,640,256]{2,1,0:T(8,128)(2,1)} %key_hbm.1), channel_id=1, source_target_pairs={{0,16},{8,24},{16,0},{24,8},{1,17},{9,25},{17,1},{25,9},{2,18},{10... | collective-permute-start | bytes 983048 | tf_op jit(solution)/shard_map/ppermute | solution.py:26
  3.5 15.1 %collective-permute-start.3 = (bf16[1,640,256]{2,1,0:T(8,128)(2,1)}, bf16[1,640,256]{2,1,0:T(8,128)(2,1)S(1)}, u32[]{:S(2)}, u32[]{:S(2)}) collective-permute-start(bf16[1,640,256]{2,1,0:T(8,128)(2,1)} %value_hbm.1), channel_id=1, source_target_pairs={{0,16},{8,24},{16,0},{24,8},{1,17},{9,25},{17,1},{25,9},{2,18},{10... | collective-permute-start | bytes 983048 | tf_op jit(solution)/shard_map/ppermute | solution.py:26
  12.2 6.4 %collective-permute-start.4 = (bf16[1,640,256]{2,1,0:T(8,128)(2,1)S(1)}, bf16[1,640,256]{2,1,0:T(8,128)(2,1)S(1)}, u32[]{:S(2)}, u32[]{:S(2)}) collective-permute-start(bf16[1,640,256]{2,1,0:T(8,128)(2,1)S(1)} %collective-permute-done.2.refs_0_), channel_id=1, source_target_pairs={{0,8},{8,0},{16,24},{24,16},{1,9},{9,1},{17,25},{25,17},{2,10},{10... | collective-permute-start | bytes 983048 | tf_op jit(solution)/shard_map/ppermute | solution.py:26
  18.6 2.7 %collective-permute-start.5 = (bf16[1,640,256]{2,1,0:T(8,128)(2,1)S(1)}, bf16[1,640,256]{2,1,0:T(8,128)(2,1)S(1)}, u32[]{:S(2)}, u32[]{:S(2)}) collective-permute-start(bf16[1,640,256]{2,1,0:T(8,128)(2,1)S(1)} %collective-permute-done.3.refs_2_), channel_id=1, source_target_pairs={{0,8},{8,0},{16,24},{24,16},{1,9},{9,1},{17,25},{25,17},{2,10},{10... | collective-permute-start | bytes 983048 | tf_op jit(solution)/shard_map/ppermute | solution.py:26
  22.9 3.4 %copy-start = (bf16[1,128,1280]{2,1,0:T(8,128)(2,1)S(1)}, bf16[1,128,1280]{2,1,0:T(8,128)(2,1)}, u32[]{:S(2)}) copy-start(bf16[1,128,1280]{2,1,0:T(8,128)(2,1)} %param.10) | copy-start | bytes 983044
  24.2 7.0 %collective-permute-start.10 = (bf16[1,128,640]{2,1,0:T(8,128)(2,1)S(1)}, bf16[1,128,640]{2,1,0:T(8,128)(2,1)S(1)}, u32[]{:S(2)}, u32[]{:S(2)}) collective-permute-start(bf16[1,128,640]{2,1,0:T(8,128)(2,1)S(1)} %shard_map.71), channel_id=1, source_target_pairs={{0,1},{1,0},{2,3},{3,2},{4,5},{5,4},{6,7},{7,6},{8,9},{9,8},{10,11... | collective-permute-start | bytes 491528 | tf_op jit(solution)/shard_map/ppermute | solution.py:26
  26.0 9.0 %collective-permute-start.8 = (bf16[1,128,640]{2,1,0:T(8,128)(2,1)S(1)}, bf16[1,128,640]{2,1,0:T(8,128)(2,1)S(1)}, u32[]{:S(2)}, u32[]{:S(2)}) collective-permute-start(bf16[1,128,640]{2,1,0:T(8,128)(2,1)S(1)} %get-tuple-element.44), channel_id=1, source_target_pairs={{0,1},{1,0},{2,3},{3,2},{4,5},{5,4},{6,7},{7,6},{8,9},{9,8},{10,11... | collective-permute-start | bytes 491528 | tf_op jit(solution)/shard_map/ppermute | solution.py:26
  26.4 26.7 %collective-permute-start.6 = (bf16[128,1280]{1,0:T(8,128)(2,1)S(1)}, bf16[128,1280]{1,0:T(8,128)(2,1)S(1)}, u32[]{:S(2)}, u32[]{:S(2)}) collective-permute-start(bf16[128,1280]{1,0:T(8,128)(2,1)S(1)} %fusion), channel_id=1, source_target_pairs={{0,4},{1,5},{2,6},{3,7},{4,0},{5,1},{6,2},{7,3},{8,12},{9,13},{10,... | collective-permute-start | bytes 983048 | tf_op jit(solution)/shard_map/ppermute | solution.py:32
  28.1 24.9 %collective-permute-start.7 = (bf16[128,1280]{1,0:T(8,128)(2,1)S(1)}, bf16[128,1280]{1,0:T(8,128)(2,1)S(1)}, u32[]{:S(2)}, u32[]{:S(2)}) collective-permute-start(bf16[128,1280]{1,0:T(8,128)(2,1)S(1)} %get-tuple-element.43), channel_id=1, source_target_pairs={{0,5},{1,4},{2,7},{3,6},{4,1},{5,0},{6,3},{7,2},{8,13},{9,12},{10,... | collective-permute-start | bytes 983048 | tf_op jit(solution)/shard_map/ppermute | solution.py:32
  31.3 13.4 %collective-permute-start.11 = (bf16[128,640]{1,0:T(8,128)(2,1)S(1)}, bf16[128,640]{1,0:T(8,128)(2,1)S(1)}, u32[]{:S(2)}, u32[]{:S(2)}) collective-permute-start(bf16[128,640]{1,0:T(8,128)(2,1)S(1)} %fusion.1), channel_id=1, source_target_pairs={{0,6},{1,7},{2,4},{3,5},{4,2},{5,3},{6,0},{7,1},{8,14},{9,15},{10,... | collective-permute-start | bytes 491528 | tf_op jit(solution)/shard_map/ppermute | solution.py:32
  35.1 17.9 %collective-permute-start.9 = (bf16[128,640]{1,0:T(8,128)(2,1)S(1)}, bf16[128,640]{1,0:T(8,128)(2,1)S(1)}, u32[]{:S(2)}, u32[]{:S(2)}) collective-permute-start(bf16[128,640]{1,0:T(8,128)(2,1)S(1)} %fusion.2), channel_id=1, source_target_pairs={{0,6},{1,7},{2,4},{3,5},{4,2},{5,3},{6,0},{7,1},{8,14},{9,15},{10,... | collective-permute-start | bytes 491528 | tf_op jit(solution)/shard_map/ppermute | solution.py:32

commit v3 on v2

--- a/solution.py
+++ b/solution.py
@@ -44,7 +44,7 @@
         out_specs=[WHOLE] * len(outs),
         scratch_shapes=list(scratch),
         compiler_params=pltpu.CompilerParams(vmem_limit_bytes=limit),
-        cost_estimate=pl.CostEstimate(flops=0 * flops, bytes_accessed=0, transcendentals=0),
+        cost_estimate=pl.CostEstimate(flops=flops, bytes_accessed=0, transcendentals=0),
     )
 
 
@@ -100,15 +100,12 @@
 def late_kernel(masks, offset_ref, q_ref, max_ref, sum_ref, acc_ref, *refs):
     count = len(masks)
     key_refs, refs = refs[:count], refs[count:]
-    outs = refs[-(3 + count) :]
-    before_refs = refs[: -(3 + count)]
-    top_ref, total_ref, scaled_ref = outs[:3]
-    weight_refs = outs[3:]
+    top_ref, total_ref, scaled_ref = refs[:3]
+    weight_refs = refs[3:]
     own = lax.axis_index("ctx")
     rows, length = q_ref.shape[1] // G, key_refs[0].shape[1]
     first_row = offset_ref[0] + own * rows
     for kv_head in range(key_refs[0].shape[2] // HD):
-        columns = slice(kv_head * HD, (kv_head + 1) * HD)
         parts = [
             masked_scores(q_ref[kv_head], ref, kv_head, first_row - (own ^ mask) * length)
             for ref, mask in zip(key_refs, masks)
@@ -119,47 +116,43 @@
         weights = [jnp.exp2((part - top) * EXP_SCALE) for part in parts]
         total = sum(jnp.sum(part, axis=1, keepdims=True) for part in weights)
         factor = jnp.exp2((before - top) * EXP_SCALE)
-        mixed = acc_ref[kv_head]
-        if before_refs:
-            mixed += jnp.dot(
-                before_refs[0][kv_head], before_refs[1][0, :, columns], preferred_element_type=jnp.float32
-            )
         top_ref[kv_head] = jnp.broadcast_to(top, before.shape)
         total_ref[kv_head] = sum_ref[kv_head] * factor + total
-        scaled_ref[kv_head] = mixed * factor
+        scaled_ref[kv_head] = acc_ref[kv_head] * factor
         for ref, part in zip(weight_refs, weights):
             ref[kv_head] = part.astype(jnp.bfloat16)
 
 
-def project(att, weight_ref, out_refs, blocks, block_width, lower):
-    slots = []
-    for ref in out_refs:
-        slots += [ref.at[i] for i in range(ref.shape[0])] if len(ref.shape) == 3 else [ref]
-    for ref, block in zip(slots, blocks):
-        start = pl.multiple_of(block * block_width + lower, LANES)
-        ref[...] = jnp.dot(
-            att, weight_ref[0, :, pl.ds(start, ref.shape[1])], preferred_element_type=jnp.float32
-        ).astype(jnp.bfloat16)
-
-
-def finish_kernel(count, blocks_of, block_width, lower, total_ref, scaled_ref, *refs):
+def finish_kernel(count, block_width, before_ref, top_ref, total_ref, acc_ref, residual_ref, w_ref, *refs):
     value_refs, weight_refs = refs[:count], refs[count : 2 * count]
-    w_ref, att_ref, out_ref = refs[2 * count :]
+    att_ref, own_ref = refs[2 * count :]
     rows = att_ref.shape[0]
-    for kv_head in range(scaled_ref.shape[0]):
+    for kv_head in range(acc_ref.shape[0]):
         columns = slice(kv_head * HD, (kv_head + 1) * HD)
-        mixed = scaled_ref[kv_head]
-        for value_ref, part_ref in zip(value_refs, weight_refs):
-            mixed += jnp.dot(part_ref[kv_head], value_ref[0, :, columns], preferred_element_type=jnp.float32)
+        parts = [
+            jnp.dot(part_ref[kv_head], value_ref[0, :, columns], preferred_element_type=jnp.float32)
+            for value_ref, part_ref in zip(value_refs, weight_refs)
+        ]
+        factor = jnp.exp2((before_ref[kv_head] - top_ref[kv_head]) * EXP_SCALE)
+        mixed = acc_ref[kv_head] + parts[0] * factor + sum(parts[1:])
         attended = (mixed / total_ref[kv_head]).astype(jnp.bfloat16)
         for g in range(G):
             head = kv_head * G + g
             att_ref[:, head * HD : (head + 1) * HD] = attended[g * rows : (g + 1) * rows]
-    project(att_ref[...], w_ref, [out_ref], blocks_of(lax.axis_index("tp")), block_width, lower)
-
-
-def project_kernel(blocks_of, block_width, lower, att_ref, w_ref, *out_refs):
-    project(att_ref[...], w_ref, out_refs, blocks_of(lax.axis_index("tp")), block_width, lower)
+    start = pl.multiple_of(lax.axis_index("tp") * block_width, LANES)
+    width = own_ref.shape[1]
+    own = jnp.dot(att_ref[...], w_ref[0, :, pl.ds(start, width)], preferred_element_type=jnp.float32)
+    own_ref[...] = (residual_ref[0, :, :width].astype(jnp.float32) + own).astype(jnp.bfloat16)
+
+
+def project_kernel(groups, block_width, att_ref, w_ref, *out_refs):
+    me = lax.axis_index("tp")
+    for (xs, lower, width), out_ref in zip(groups, out_refs):
+        for slot, x in enumerate(xs):
+            start = pl.multiple_of((me ^ x) * block_width + lower, LANES)
+            out_ref[slot] = jnp.dot(
+                att_ref[...], w_ref[0, :, pl.ds(start, width)], preferred_element_type=jnp.float32
+            ).astype(jnp.bfloat16)
 
 
 def xor_order(lowest, size):
@@ -169,10 +162,8 @@
     return [x + lowest for x in rest] + rest
 
 
-def chunk_plan(width):
-    units = width // LANES
-    first = (units + 1) // 2
-    return [u * LANES for u in (first, units - first) if u > 0]
+def cross_first_width(width):
+    return max(1, (2 * (width // LANES)) // 10) * LANES
 
 
 def on_device(row_offsets, queries, cache_keys, cache_values, residual, out_weight):
@@ -198,7 +189,7 @@
         [SCALARS] + [IN_HBM] * 4 + [WHOLE] * (2 * len(near) - 2),
         state + [((kv_local, stacked, HD), jnp.bfloat16), (out_weight.shape, out_weight.dtype)],
         32 * MIB,
-        half_flops,
+        0,
         [pltpu.VMEM(a.shape, a.dtype) for a in local[:3]] + [pltpu.SemaphoreType.DMA((4,))],
     )(
         row_offsets,
@@ -219,10 +210,10 @@
             [SCALARS] + [WHOLE] * len(operands),
             state + [((kv_local, stacked, length), jnp.bfloat16)] * len(masks),
             32 * MIB,
-            half_flops,
+            0,
         )(row_offsets, *operands)
 
-    top, total, acc, far_weights = late([top_bit], 0, query, top, total, acc, in_vmem(far_key))
+    near_top, total, acc, far_weights = late([top_bit], 0, query, top, total, acc, in_vmem(far_key))
     far_value, total = lax.optimization_barrier((far_value, total))
     far_values = [far_value]
     bit = top_bit // 2
@@ -230,57 +221,66 @@
         far_values += [exchange(v, "ctx", bit) for v in far_values]
         bit //= 2
     masks, keys = zip(*far_keys[1:])
-    top, total, acc, *weights = late(
-        list(masks), 0, query, top, total, acc, *[in_vmem(k) for k in keys], far_weights, in_vmem(far_value)
-    )
-    far_values = far_values[1:]
-
-    order = xor_order(2, n_tp)
-    across = order[:-1]
-    widths = chunk_plan(block_width)
-    lowers = [sum(widths[:i]) for i in range(len(widths))]
+    top, total, acc, *weights = late(list(masks), 0, query, near_top, total, acc, *[in_vmem(k) for k in keys])
+    weights = [far_weights, *weights]
+
+    across = xor_order(2, n_tp)[:-1]
+    cross_width = cross_first_width(block_width)
+    pair_width = block_width - cross_width
     block_flops = 2 * rows * out_weight.shape[1]
-    attended, send = local_call(
-        functools.partial(finish_kernel, len(far_values), lambda me: [me ^ 1 ^ x for x in across], block_width, 0),
-        [WHOLE] * (3 + 2 * len(far_values)),
-        [((rows, out_weight.shape[1]), jnp.bfloat16), ((len(across), rows, widths[0]), jnp.bfloat16)],
+    attended, own_a = local_call(
+        functools.partial(finish_kernel, len(far_values), block_width),
+        [WHOLE] * (6 + 2 * len(far_values)),
+        [((rows, out_weight.shape[1]), jnp.bfloat16), ((rows, pair_width), jnp.bfloat16)],
         16 * MIB,
-        half_flops // 2 + block_flops * widths[0] * len(across),
-    )(total, acc, *[in_vmem(v) for v in far_values], *weights, weight)
-
-    def projected(masks, lower, width, stack=False):
-        shapes = [((len(masks), rows, width), jnp.bfloat16)] if stack else [((rows, width), jnp.bfloat16)] * len(masks)
+        0,
+    )(near_top, top, total, acc, in_vmem(residual), weight, *[in_vmem(v) for v in far_values], *weights)
+
+    def projected(*groups):
         return local_call(
-            functools.partial(project_kernel, lambda me: [me ^ x for x in masks], block_width, lower),
+            functools.partial(project_kernel, groups, block_width),
             [WHOLE] * 2,
-            shapes,
+            [((len(xs), rows, width), jnp.bfloat16) for xs, _, width in groups],
             16 * MIB,
-            block_flops * width * len(masks),
+            block_flops * sum(len(xs) * width for xs, _, width in groups),
         )(attended, weight)
 
-    firsts = []
-    for lower, width in zip(lowers, widths):
-        if lower:
-            (send,) = projected([1 ^ x for x in across], lower, width, True)
-        firsts.append(exchange(send, "tp", 1))
-    pair, own = projected([1, 0], 0, block_width)
-    kept = [projected(across, lower, width) for lower, width in zip(lowers, widths)]
-    own = (own.astype(jnp.float32) + residual[0].astype(jnp.float32)).astype(jnp.bfloat16)
-    whole = [handed(own, 0), handed(pair, 1)]
-    outs = []
-    for lower, width, first, part in zip(lowers, widths, firsts, kept):
-        part = [a.astype(jnp.float32) + first[i].astype(jnp.float32) for i, a in enumerate(part)]
-        terms = [a[:, lower : lower + width] for a in whole]
-        bit = 2
-        while bit < n_tp:
-            half = (len(part) + 1) // 2
-            sends = [a.astype(jnp.bfloat16) for a in part[:half]]
-            received = [exchange(a, "tp", bit) for a in sends[:-1]]
-            terms.append(handed(sends[-1], bit))
-            part = [a + r.astype(jnp.float32) for a, r in zip(part[half:], received)]
-            bit *= 2
-        outs.append(sum(term.astype(jnp.float32) for term in terms).astype(jnp.bfloat16))
-    return jnp.concatenate(outs, axis=1)[None]
+    half = n_tp // 2
+    own_a = handed(own_a, 0)
+    (send_a,) = projected(([1 ^ x for x in across], 0, pair_width))
+    send_b, pair_a = projected((list(range(half, n_tp)), pair_width, cross_width), ([1], 0, pair_width))
+    kept_a, kept_b = projected((across, 0, pair_width), (list(range(half)), pair_width, cross_width))
+    got_a = exchange(send_a, "tp", 1)
+    got_b = exchange(send_b, "tp", half)
+    pair_a = handed(pair_a[0], 1)
+    own_a, got_a = lax.optimization_barrier((own_a, got_a))
+
+    part = [kept_a[i].astype(jnp.float32) + got_a[i].astype(jnp.float32) for i in range(len(across))]
+    terms_a = [own_a, pair_a]
+    bit = 2
+    while bit < n_tp:
+        count = (len(part) + 1) // 2
+        sends = [a.astype(jnp.bfloat16) for a in part[:count]]
+        received = [exchange(a, "tp", bit) for a in sends[:-1]]
+        terms_a.append(handed(sends[-1], bit))
+        part = [a + r.astype(jnp.float32) for a, r in zip(part[count:], received)]
+        bit *= 2
+
+    part = [kept_b[i].astype(jnp.float32) + got_b[i].astype(jnp.float32) for i in range(half)]
+    while len(part) > 2:
+        count = len(part) // 2
+        received = [exchange(a.astype(jnp.bfloat16), "tp", count) for a in part[count:]]
+        part = [a + r.astype(jnp.float32) for a, r in zip(part[:count], received)]
+    part[0] = part[0] + residual[0, :, pair_width:].astype(jnp.float32)
+    part = [a.astype(jnp.bfloat16) for a in part]
+    terms_b = [handed(a, x) for x, a in enumerate(part)]
+
+    def total_of(terms):
+        return sum(term.astype(jnp.float32) for term in terms).astype(jnp.bfloat16)
+
+    total_a = total_of(terms_a)
+    total_a, *terms_b = lax.optimization_barrier((total_a, *terms_b))
+    return jnp.concatenate([total_a, total_of(terms_b)], axis=1)[None]
 
 
 def solution(mesh):

time: 54.1 us -> 49.9 us (0.922)
  starting transfers between devices: 20.4 us -> 16.9 us
  Pallas kernels: 11.2 us -> 9.91 us
  waiting for transfers between devices: 20.5 us -> 21.2 us
    ppermute x4 -> x5, starting transfers between devices: 14.8 us -> 8.87 us  [handed(): return lax.ppermute(block, ('section', 'tp'), route)]
    ppermute x8, waiting for transfers between devices: 10.3 us -> 13.3 us  [exchange(): return lax.ppermute(block, axis, route)]
    ppermute x8, starting transfers between devices: 5.61 us -> 8.06 us  [exchange(): return lax.ppermute(block, axis, route)]
    ppermute x4 -> x5, waiting for transfers between devices: 10.3 us -> 7.87 us  [handed(): return lax.ppermute(block, ('section', 'tp'), route)]
    pallas_call x2, Pallas kernels: 4.04 us -> 2.76 us  [late(): local_call(functools.partial(late_kernel, masks), [SCALARS] + [WHOLE] * l...]
    pallas_call x5 -> x4, Pallas kernels: 2.89 us -> 2.83 us  [the longest x3 1.67 us: projected(): local_call(functools.partial(project_kernel, groups, block_width), [WHOLE...]
  transfers between devices with their start and end apart: 12 -> 13, of which waited for: 5 -> 6; matrix products, arithmetic and copies ran while one was open for 0% -> 0% of each run, Pallas kernels for 16% -> 17%
where the time goes in v3:
time: 49.9 us; the launch traced here: 49.8 us
  waiting for transfers between devices  21.2 us (42%)
  starting transfers between devices  16.9 us (34%)
  Pallas kernels  9.91 us (20%)
  other arithmetic  1 us (2%)
  between operations  0.77 us (2%)
    ppermute x8, waiting for transfers between devices, exchange(): return lax.ppermute(block, axis, route)  13.3 us
    ppermute x5, starting transfers between devices, handed(): return lax.ppermute(block, ('section', 'tp'), route)  8.87 us
    ppermute x8, starting transfers between devices, exchange(): return lax.ppermute(block, axis, route)  8.06 us
    ppermute x5, waiting for transfers between devices, handed(): return lax.ppermute(block, ('section', 'tp'), route)  7.87 us
    pallas_call x1, Pallas kernels, on_device(): local_call(functools.partial(early_kernel, [m for m, _, _ in near]), [SCA...  4.32 us
    pallas_call x2, Pallas kernels, late(): local_call(functools.partial(late_kernel, masks), [SCALARS] + [WHOLE] * l...  2.76 us
    pallas_call x3, Pallas kernels, projected(): local_call(functools.partial(project_kernel, groups, block_width), [WHOLE...  1.67 us
    pallas_call x1, Pallas kernels, on_device(): local_call(functools.partial(finish_kernel, len(far_values), block_width)...  1.17 us
  transfers between devices with their start and end apart: 13, of which 6 were waited for; matrix products, arithmetic and copies ran while one was open for 0% of the time, Pallas kernels for 17%

profile of v3, /device:TPU:0, one launch (start us, length us, event | category | flops | bytes accessed | tf_op | source)
XLA Modules:
  0.0 49.8 jit_solution(12054335133422537450)
XLA Ops:
  0.0 0.0 copy-start
  0.0 0.5 collective-permute-start
  0.5 0.1 collective-permute-start.1
  0.5 3.0 %collective-permute-start.2 = (bf16[1,640,256]{2,1,0:T(8,128)(2,1)}, bf16[1,640,256]{2,1,0:T(8,128)(2,1)S(1)}, u32[]{:S(2)}, u32[]{:S(2)}) collective-permute-start(bf16[1,640,256]{2,1,0:T(8,128)(2,1)} %key_hbm.1), channel_id=1, source_target_pairs={{0,16},{8,24},{16,0},{24,8},{1,17},{9,25},{17,1},{25,9},{2,18},{10... | collective-permute-start | bytes 983048 | tf_op jit(solution)/shard_map/ppermute | solution.py:26
  3.5 0.0 collective-permute-start.3
  4.2 0.0 collective-permute-done.refs_0_
  4.2 0.0 collective-permute-done.1.refs_1_
  4.2 4.3 %shard_map.64 = (f32[2,512,128]{2,1,0:T(8,128)S(1)}, f32[2,512,128]{2,1,0:T(8,128)S(1)}, f32[2,512,128]{2,1,0:T(8,128)S(1)}, bf16[2,512,128]{2,1,0:T(8,128)(2,1)S(1)}, bf16[1,1024,5120]{2,1,0:T(8,128)(2,1)S(1)}) custom-call(s32[1]{0:T(128)S(6)} %copy.7.offset_ref, bf16[1,128,1024]{2,1,0:T(8,128)(2,1)} %q_hbm.1, bf16[1,640,256]{2,1,0:T(8,128)(2,1)} %key_hbm.1, ...), custom_call_target="tpu_custom_call" | custom-call | tf_op jit(solution)/shard_map/pallas_call | solution.py:187
  8.5 3.7 %collective-permute-done.2.refs_0_ = bf16[1,640,256]{2,1,0:T(8,128)(2,1)S(1)} collective-permute-done((bf16[1,640,256]{2,1,0:T(8,128)(2,1)}, bf16[1,640,256]{2,1,0:T(8,128)(2,1)S(1)}, u32[]{:S(2)}, u32[]{:S(2)}) %collective-permute-start.2) | collective-permute-done | bytes 327712 | tf_op jit(solution)/shard_map/ppermute | solution.py:26
  12.2 0.0 collective-permute-start.4
  12.2 1.4 %shard_map.65 = (f32[2,512,128]{2,1,0:T(8,128)S(1)}, f32[2,512,128]{2,1,0:T(8,128)S(1)}, f32[2,512,128]{2,1,0:T(8,128)S(1)}, bf16[2,512,640]{2,1,0:T(8,128)(2,1)S(1)}) custom-call(s32[1]{0:T(128)S(6)} %copy.7.offset_ref, bf16[2,512,128]{2,1,0:T(8,128)(2,1)S(1)} %get-tuple-element.33.q_ref, f32[2,512,128]{2,1,0:T(8,128)S(1)} %get-tuple-element.35.max_ref, ...), custom_call_target="tpu_custom_call" | custom-call | tf_op jit(solution)/shard_map/pallas_call | solution.py:208
  13.6 5.1 %collective-permute-done.3.refs_0_ = bf16[1,640,256]{2,1,0:T(8,128)(2,1)S(1)} collective-permute-done((bf16[1,640,256]{2,1,0:T(8,128)(2,1)}, bf16[1,640,256]{2,1,0:T(8,128)(2,1)S(1)}, u32[]{:S(2)}, u32[]{:S(2)}) %collective-permute-start.3) | collective-permute-done | bytes 327712 | tf_op jit(solution)/shard_map/ppermute | solution.py:26
  18.6 0.0 collective-permute-start.5
  18.7 0.0 collective-permute-done.4.refs_0_
  18.7 1.4 %shard_map.66 = (f32[2,512,128]{2,1,0:T(8,128)S(1)}, f32[2,512,128]{2,1,0:T(8,128)S(1)}, f32[2,512,128]{2,1,0:T(8,128)S(1)}, bf16[2,512,640]{2,1,0:T(8,128)(2,1)S(1)}) custom-call(s32[1]{0:T(128)S(6)} %copy.7.offset_ref, bf16[2,512,128]{2,1,0:T(8,128)(2,1)S(1)} %get-tuple-element.33.q_ref, f32[2,512,128]{2,1,0:T(8,128)S(1)} %get-tuple-element.38.max_ref.before_ref, ...), custom_call_target="tpu_custom_call" | custom-call | tf_op jit(solution)/shard_map/pallas_call | solution.py:208
  20.0 0.2 collective-permute-done.5.refs_1_
  20.3 0.0 copy-done
  20.3 1.2 %shard_map.67 = (bf16[128,1024]{1,0:T(8,128)(2,1)S(1)}, bf16[128,1024]{1,0:T(8,128)(2,1)S(1)}) custom-call(f32[2,512,128]{2,1,0:T(8,128)S(1)} %get-tuple-element.38.max_ref.before_ref, f32[2,512,128]{2,1,0:T(8,128)S(1)} %get-tuple-element.43.top_ref, f32[2,512,128]{2,1,0:T(8,128)S(1)} %get-tuple-element.44.total_ref, ...), custom_call_target="tpu_custom_call" | custom-call | tf_op jit(solution)/shard_map/pallas_call | solution.py:231
  21.5 0.5 shard_map.68
  21.9 1.9 %collective-permute-start.7 = (bf16[1,128,1024]{2,1,0:T(8,128)(2,1)S(1)}, bf16[1,128,1024]{2,1,0:T(8,128)(2,1)S(1)}, u32[]{:S(2)}, u32[]{:S(2)}) collective-permute-start(bf16[1,128,1024]{2,1,0:T(8,128)(2,1)S(1)} %shard_map.68), channel_id=1, source_target_pairs={{0,1},{1,0},{2,3},{3,2},{4,5},{5,4},{6,7},{7,6},{8,9},{9,8},{10,11... | collective-permute-start | bytes 786440 | tf_op jit(solution)/shard_map/ppermute | solution.py:26
  23.8 1.5 %collective-permute-start.6 = (bf16[128,1024]{1,0:T(8,128)(2,1)S(1)}, bf16[128,1024]{1,0:T(8,128)(2,1)S(1)}, u32[]{:S(2)}, u32[]{:S(2)}) collective-permute-start(bf16[128,1024]{1,0:T(8,128)(2,1)S(1)} %get-tuple-element.50), channel_id=1, source_target_pairs={{0,4},{1,5},{2,6},{3,7},{4,0},{5,1},{6,2},{7,3},{8,12},{9,13},{10,... | collective-permute-start | bytes 786440 | tf_op jit(solution)/shard_map/ppermute | solution.py:32
  25.3 0.6 %shard_map.69 = (bf16[2,128,256]{2,1,0:T(8,128)(2,1)S(1)}, bf16[1,128,1024]{2,1,0:T(8,128)(2,1)S(1)}) custom-call(bf16[128,1024]{1,0:T(8,128)(2,1)S(1)} %get-tuple-element.51.att_ref, bf16[1,1024,5120]{2,1,0:T(8,128)(2,1)S(1)} %get-tuple-element.46.w_ref), custom_call_target="tpu_custom_call" | custom-call | flops 402653184 | tf_op jit(solution)/shard_map/pallas_call | solution.py:240
  25.9 2.6 %collective-permute-start.10 = (bf16[2,128,256]{2,1,0:T(8,128)(2,1)S(1)}, bf16[2,128,256]{2,1,0:T(8,128)(2,1)S(1)}, u32[]{:S(2)}, u32[]{:S(2)}) collective-permute-start(bf16[2,128,256]{2,1,0:T(8,128)(2,1)S(1)} %get-tuple-element.57), channel_id=1, source_target_pairs={{0,2},{1,3},{2,0},{3,1},{4,6},{5,7},{6,4},{7,5},{8,10},{9,11},{10,... | collective-permute-start | bytes 393224 | tf_op jit(solution)/shard_map/ppermute | solution.py:26
  28.6 0.4 collective-permute-start.8
  29.0 0.6 %shard_map.70 = (bf16[1,128,1024]{2,1,0:T(8,128)(2,1)S(1)}, bf16[2,128,256]{2,1,0:T(8,128)(2,1)S(1)}) custom-call(bf16[128,1024]{1,0:T(8,128)(2,1)S(1)} %get-tuple-element.51.att_ref, bf16[1,1024,5120]{2,1,0:T(8,128)(2,1)S(1)} %get-tuple-element.46.w_ref), custom_call_target="tpu_custom_call" | custom-call | flops 402653184 | tf_op jit(solution)/shard_map/pallas_call | solution.py:240
  29.6 4.3 %collective-permute-done.7 = bf16[1,128,1024]{2,1,0:T(8,128)(2,1)S(1)} collective-permute-done((bf16[1,128,1024]{2,1,0:T(8,128)(2,1)S(1)}, bf16[1,128,1024]{2,1,0:T(8,128)(2,1)S(1)}, u32[]{:S(2)}, u32[]{:S(2)}) %collective-permute-start.7) | collective-permute-done | bytes 262176 | tf_op jit(solution)/shard_map/ppermute | solution.py:26
  33.9 0.0 collective-permute-done.6
  33.9 0.1 fusion
  34.0 2.9 %collective-permute-start.9 = (bf16[128,1024]{1,0:T(8,128)(2,1)S(1)}, bf16[128,1024]{1,0:T(8,128)(2,1)S(1)}, u32[]{:S(2)}, u32[]{:S(2)}) collective-permute-start(bf16[128,1024]{1,0:T(8,128)(2,1)S(1)} %fusion), channel_id=1, source_target_pairs={{0,6},{1,7},{2,4},{3,5},{4,2},{5,3},{6,0},{7,1},{8,14},{9,15},{10,... | collective-permute-start | bytes 786440 | tf_op jit(solution)/shard_map/ppermute | solution.py:32
  36.9 0.0 collective-permute-done.10
  37.0 0.5 collective-permute-start.11
  37.5 3.5 %collective-permute-start.12 = (bf16[128,256]{1,0:T(8,128)(2,1)S(1)}, bf16[128,256]{1,0:T(8,128)(2,1)S(1)}, u32[]{:S(2)}, u32[]{:S(2)}) collective-permute-start(bf16[128,256]{1,0:T(8,128)(2,1)S(1)} %get-tuple-element.61), channel_id=1, source_target_pairs={{0,5},{1,4},{2,7},{3,6},{4,1},{5,0},{6,3},{7,2},{8,13},{9,12},{10,... | collective-permute-start | bytes 196616 | tf_op jit(solution)/shard_map/ppermute | solution.py:32
  41.0 4.4 %collective-permute-done.8 = bf16[128,1024]{1,0:T(8,128)(2,1)S(1)} collective-permute-done((bf16[128,1024]{1,0:T(8,128)(2,1)S(1)}, bf16[128,1024]{1,0:T(8,128)(2,1)S(1)}, u32[]{:S(2)}, u32[]{:S(2)}) %collective-permute-start.8) | collective-permute-done | bytes 262176 | tf_op jit(solution)/shard_map/ppermute | solution.py:32
  45.4 3.4 %collective-permute-done.9 = bf16[128,1024]{1,0:T(8,128)(2,1)S(1)} collective-permute-done((bf16[128,1024]{1,0:T(8,128)(2,1)S(1)}, bf16[128,1024]{1,0:T(8,128)(2,1)S(1)}, u32[]{:S(2)}, u32[]{:S(2)}) %collective-permute-start.9) | collective-permute-done | bytes 262176 | tf_op jit(solution)/shard_map/ppermute | solution.py:32
  48.9 0.1 add_convert_fusion
  49.0 0.0 collective-permute-done.11
  49.0 0.0 collective-permute-done.12
  49.0 0.7 %maximum_bitcast_fusion = bf16[1,128,1280]{2,1,0:T(8,128)(2,1)} fusion(bf16[128,256]{1,0:T(8,128)(2,1)S(1)} %add_convert_fusion.2, bf16[128,1024]{1,0:T(8,128)(2,1)S(1)} %add_convert_fusion), kind=kLoop, calls=%fused_computation.2 | loop fusion | flops 655360 | bytes 655360 | tf_op jit(solution)/shard_map/broadcast_in_dim | solution.py:283
  (2 shorter events, 0.1 us)
Async XLA Ops:
  0.0 20.3 %copy-start = (bf16[1,128,1280]{2,1,0:T(8,128)(2,1)S(1)}, bf16[1,128,1280]{2,1,0:T(8,128)(2,1)}, u32[]{:S(2)}) copy-start(bf16[1,128,1280]{2,1,0:T(8,128)(2,1)} %residual_ref.1) | copy-start | bytes 983044
  0.0 4.2 %collective-permute-start = (bf16[1,640,256]{2,1,0:T(8,128)(2,1)}, bf16[1,640,256]{2,1,0:T(8,128)(2,1)S(1)}, u32[]{:S(2)}, u32[]{:S(2)}) collective-permute-start(bf16[1,640,256]{2,1,0:T(8,128)(2,1)} %key_hbm.1), channel_id=1, source_target_pairs={{0,8},{8,0},{16,24},{24,16},{1,9},{9,1},{17,25},{25,17},{2,10},{10... | collective-permute-start | bytes 983048 | tf_op jit(solution)/shard_map/ppermute | solution.py:26
  0.5 3.7 %collective-permute-start.1 = (bf16[1,640,256]{2,1,0:T(8,128)(2,1)}, bf16[1,640,256]{2,1,0:T(8,128)(2,1)S(1)}, u32[]{:S(2)}, u32[]{:S(2)}) collective-permute-start(bf16[1,640,256]{2,1,0:T(8,128)(2,1)} %value_hbm.1), channel_id=1, source_target_pairs={{0,8},{8,0},{16,24},{24,16},{1,9},{9,1},{17,25},{25,17},{2,10},{10... | collective-permute-start | bytes 983048 | tf_op jit(solution)/shard_map/ppermute | solution.py:26
  0.5 11.7 %collective-permute-start.2 = (bf16[1,640,256]{2,1,0:T(8,128)(2,1)}, bf16[1,640,256]{2,1,0:T(8,128)(2,1)S(1)}, u32[]{:S(2)}, u32[]{:S(2)}) collective-permute-start(bf16[1,640,256]{2,1,0:T(8,128)(2,1)} %key_hbm.1), channel_id=1, source_target_pairs={{0,16},{8,24},{16,0},{24,8},{1,17},{9,25},{17,1},{25,9},{2,18},{10... | collective-permute-start | bytes 983048 | tf_op jit(solution)/shard_map/ppermute | solution.py:26
  3.5 15.2 %collective-permute-start.3 = (bf16[1,640,256]{2,1,0:T(8,128)(2,1)}, bf16[1,640,256]{2,1,0:T(8,128)(2,1)S(1)}, u32[]{:S(2)}, u32[]{:S(2)}) collective-permute-start(bf16[1,640,256]{2,1,0:T(8,128)(2,1)} %value_hbm.1), channel_id=1, source_target_pairs={{0,16},{8,24},{16,0},{24,8},{1,17},{9,25},{17,1},{25,9},{2,18},{10... | collective-permute-start | bytes 983048 | tf_op jit(solution)/shard_map/ppermute | solution.py:26
  12.2 6.5 %collective-permute-start.4 = (bf16[1,640,256]{2,1,0:T(8,128)(2,1)S(1)}, bf16[1,640,256]{2,1,0:T(8,128)(2,1)S(1)}, u32[]{:S(2)}, u32[]{:S(2)}) collective-permute-start(bf16[1,640,256]{2,1,0:T(8,128)(2,1)S(1)} %collective-permute-done.2.refs_0_), channel_id=1, source_target_pairs={{0,8},{8,0},{16,24},{24,16},{1,9},{9,1},{17,25},{25,17},{2,10},{10... | collective-permute-start | bytes 983048 | tf_op jit(solution)/shard_map/ppermute | solution.py:26
  18.6 1.6 %collective-permute-start.5 = (bf16[1,640,256]{2,1,0:T(8,128)(2,1)S(1)}, bf16[1,640,256]{2,1,0:T(8,128)(2,1)S(1)}, u32[]{:S(2)}, u32[]{:S(2)}) collective-permute-start(bf16[1,640,256]{2,1,0:T(8,128)(2,1)S(1)} %collective-permute-done.3.refs_0_), channel_id=1, source_target_pairs={{0,8},{8,0},{16,24},{24,16},{1,9},{9,1},{17,25},{25,17},{2,10},{10... | collective-permute-start | bytes 983048 | tf_op jit(solution)/shard_map/ppermute | solution.py:26
  21.9 12.0 %collective-permute-start.7 = (bf16[1,128,1024]{2,1,0:T(8,128)(2,1)S(1)}, bf16[1,128,1024]{2,1,0:T(8,128)(2,1)S(1)}, u32[]{:S(2)}, u32[]{:S(2)}) collective-permute-start(bf16[1,128,1024]{2,1,0:T(8,128)(2,1)S(1)} %shard_map.68), channel_id=1, source_target_pairs={{0,1},{1,0},{2,3},{3,2},{4,5},{5,4},{6,7},{7,6},{8,9},{9,8},{10,11... | collective-permute-start | bytes 786440 | tf_op jit(solution)/shard_map/ppermute | solution.py:26
  23.8 10.1 %collective-permute-start.6 = (bf16[128,1024]{1,0:T(8,128)(2,1)S(1)}, bf16[128,1024]{1,0:T(8,128)(2,1)S(1)}, u32[]{:S(2)}, u32[]{:S(2)}) collective-permute-start(bf16[128,1024]{1,0:T(8,128)(2,1)S(1)} %get-tuple-element.50), channel_id=1, source_target_pairs={{0,4},{1,5},{2,6},{3,7},{4,0},{5,1},{6,2},{7,3},{8,12},{9,13},{10,... | collective-permute-start | bytes 786440 | tf_op jit(solution)/shard_map/ppermute | solution.py:32
  25.9 11.0 %collective-permute-start.10 = (bf16[2,128,256]{2,1,0:T(8,128)(2,1)S(1)}, bf16[2,128,256]{2,1,0:T(8,128)(2,1)S(1)}, u32[]{:S(2)}, u32[]{:S(2)}) collective-permute-start(bf16[2,128,256]{2,1,0:T(8,128)(2,1)S(1)} %get-tuple-element.57), channel_id=1, source_target_pairs={{0,2},{1,3},{2,0},{3,1},{4,6},{5,7},{6,4},{7,5},{8,10},{9,11},{10,... | collective-permute-start | bytes 393224 | tf_op jit(solution)/shard_map/ppermute | solution.py:26
  28.6 16.9 %collective-permute-start.8 = (bf16[128,1024]{1,0:T(8,128)(2,1)S(1)}, bf16[128,1024]{1,0:T(8,128)(2,1)S(1)}, u32[]{:S(2)}, u32[]{:S(2)}) collective-permute-start(bf16[128,1024]{1,0:T(8,128)(2,1)S(1)} %bitcast.9), channel_id=1, source_target_pairs={{0,5},{1,4},{2,7},{3,6},{4,1},{5,0},{6,3},{7,2},{8,13},{9,12},{10,... | collective-permute-start | bytes 786440 | tf_op jit(solution)/shard_map/ppermute | solution.py:32
  34.0 14.9 %collective-permute-start.9 = (bf16[128,1024]{1,0:T(8,128)(2,1)S(1)}, bf16[128,1024]{1,0:T(8,128)(2,1)S(1)}, u32[]{:S(2)}, u32[]{:S(2)}) collective-permute-start(bf16[128,1024]{1,0:T(8,128)(2,1)S(1)} %fusion), channel_id=1, source_target_pairs={{0,6},{1,7},{2,4},{3,5},{4,2},{5,3},{6,0},{7,1},{8,14},{9,15},{10,... | collective-permute-start | bytes 786440 | tf_op jit(solution)/shard_map/ppermute | solution.py:32
  37.0 12.0 %collective-permute-start.11 = (bf16[128,256]{1,0:T(8,128)(2,1)S(1)}, bf16[128,256]{1,0:T(8,128)(2,1)S(1)}, u32[]{:S(2)}, u32[]{:S(2)}) collective-permute-start(bf16[128,256]{1,0:T(8,128)(2,1)S(1)} %get-tuple-element.62), channel_id=1, source_target_pairs={{0,4},{1,5},{2,6},{3,7},{4,0},{5,1},{6,2},{7,3},{8,12},{9,13},{10,... | collective-permute-start | bytes 196616 | tf_op jit(solution)/shard_map/ppermute | solution.py:32
  37.5 11.6 %collective-permute-start.12 = (bf16[128,256]{1,0:T(8,128)(2,1)S(1)}, bf16[128,256]{1,0:T(8,128)(2,1)S(1)}, u32[]{:S(2)}, u32[]{:S(2)}) collective-permute-start(bf16[128,256]{1,0:T(8,128)(2,1)S(1)} %get-tuple-element.61), channel_id=1, source_target_pairs={{0,5},{1,4},{2,7},{3,6},{4,1},{5,0},{6,3},{7,2},{8,13},{9,12},{10,... | collective-permute-start | bytes 196616 | tf_op jit(solution)/shard_map/ppermute | solution.py:32

commit v4 on v3

--- a/solution.py
+++ b/solution.py
@@ -123,9 +123,18 @@
             ref[kv_head] = part.astype(jnp.bfloat16)
 
 
-def finish_kernel(count, block_width, before_ref, top_ref, total_ref, acc_ref, residual_ref, w_ref, *refs):
+def project_blocks(att_ref, w_ref, block_width, group, out_ref):
+    xs, lower, width = group
+    for slot, x in enumerate(xs):
+        start = pl.multiple_of((lax.axis_index("tp") ^ x) * block_width + lower, LANES)
+        out_ref[slot] = jnp.dot(
+            att_ref[...], w_ref[0, :, pl.ds(start, width)], preferred_element_type=jnp.float32
+        ).astype(jnp.bfloat16)
+
+
+def finish_kernel(count, block_width, group, before_ref, top_ref, total_ref, acc_ref, w_ref, *refs):
     value_refs, weight_refs = refs[:count], refs[count : 2 * count]
-    att_ref, own_ref = refs[2 * count :]
+    att_ref, send_ref = refs[2 * count :]
     rows = att_ref.shape[0]
     for kv_head in range(acc_ref.shape[0]):
         columns = slice(kv_head * HD, (kv_head + 1) * HD)
@@ -139,6 +148,10 @@
         for g in range(G):
             head = kv_head * G + g
             att_ref[:, head * HD : (head + 1) * HD] = attended[g * rows : (g + 1) * rows]
+    project_blocks(att_ref, w_ref, block_width, group, send_ref)
+
+
+def own_kernel(block_width, att_ref, w_ref, residual_ref, own_ref):
     start = pl.multiple_of(lax.axis_index("tp") * block_width, LANES)
     width = own_ref.shape[1]
     own = jnp.dot(att_ref[...], w_ref[0, :, pl.ds(start, width)], preferred_element_type=jnp.float32)
@@ -146,13 +159,22 @@
 
 
 def project_kernel(groups, block_width, att_ref, w_ref, *out_refs):
-    me = lax.axis_index("tp")
-    for (xs, lower, width), out_ref in zip(groups, out_refs):
-        for slot, x in enumerate(xs):
-            start = pl.multiple_of((me ^ x) * block_width + lower, LANES)
-            out_ref[slot] = jnp.dot(
-                att_ref[...], w_ref[0, :, pl.ds(start, width)], preferred_element_type=jnp.float32
-            ).astype(jnp.bfloat16)
+    for group, out_ref in zip(groups, out_refs):
+        project_blocks(att_ref, w_ref, block_width, group, out_ref)
+
+
+def total_kernel(count, *refs):
+    *term_refs, out_ref, total_ref, sems = refs
+    lower = term_refs[0].shape[1]
+    half = out_ref.shape[0] // 2
+    copies = []
+    for i, rows in enumerate((slice(0, half), slice(half, 2 * half))):
+        for group, columns in ((term_refs[:count], slice(0, lower)), (term_refs[count:], slice(lower, None))):
+            total_ref[rows, columns] = sum(ref[rows].astype(jnp.float32) for ref in group).astype(jnp.bfloat16)
+        copies.append(pltpu.make_async_copy(total_ref.at[rows], out_ref.at[rows], sems.at[i]))
+        copies[-1].start()
+    for copy in copies:
+        copy.wait()
 
 
 def xor_order(lowest, size):
@@ -184,6 +206,9 @@
     state = [((kv_local, stacked, HD), jnp.float32)] * 3
     half_flops = 4 * kv_local * stacked * length * HD * len(near)
     local = [queries, cache_keys, cache_values, out_weight]
+    masks, keys, values = zip(*near)
+    far_key, keys, values = lax.optimization_barrier((far_key, keys, values))
+    near = list(zip(masks, keys, values))
     top, total, acc, query, weight = local_call(
         functools.partial(early_kernel, [m for m, _, _ in near]),
         [SCALARS] + [IN_HBM] * 4 + [WHOLE] * (2 * len(near) - 2),
@@ -228,13 +253,21 @@
     cross_width = cross_first_width(block_width)
     pair_width = block_width - cross_width
     block_flops = 2 * rows * out_weight.shape[1]
-    attended, own_a = local_call(
-        functools.partial(finish_kernel, len(far_values), block_width),
-        [WHOLE] * (6 + 2 * len(far_values)),
-        [((rows, out_weight.shape[1]), jnp.bfloat16), ((rows, pair_width), jnp.bfloat16)],
+    relay = ([1 ^ x for x in across], 0, pair_width)
+    attended, send_a = local_call(
+        functools.partial(finish_kernel, len(far_values), block_width, relay),
+        [WHOLE] * (5 + 2 * len(far_values)),
+        [((rows, out_weight.shape[1]), jnp.bfloat16), ((len(across), rows, pair_width), jnp.bfloat16)],
         16 * MIB,
         0,
-    )(near_top, top, total, acc, in_vmem(residual), weight, *[in_vmem(v) for v in far_values], *weights)
+    )(near_top, top, total, acc, weight, *[in_vmem(v) for v in far_values], *weights)
+    (own_a,) = local_call(
+        functools.partial(own_kernel, block_width),
+        [WHOLE] * 3,
+        [((rows, pair_width), jnp.bfloat16)],
+        16 * MIB,
+        block_flops * pair_width,
+    )(attended, weight, in_vmem(residual))
 
     def projected(*groups):
         return local_call(
@@ -247,23 +280,22 @@
 
     half = n_tp // 2
     own_a = handed(own_a, 0)
-    (send_a,) = projected(([1 ^ x for x in across], 0, pair_width))
     send_b, pair_a = projected((list(range(half, n_tp)), pair_width, cross_width), ([1], 0, pair_width))
     kept_a, kept_b = projected((across, 0, pair_width), (list(range(half)), pair_width, cross_width))
     got_a = exchange(send_a, "tp", 1)
     got_b = exchange(send_b, "tp", half)
     pair_a = handed(pair_a[0], 1)
-    own_a, got_a = lax.optimization_barrier((own_a, got_a))
 
     part = [kept_a[i].astype(jnp.float32) + got_a[i].astype(jnp.float32) for i in range(len(across))]
+    own_a, *part = lax.optimization_barrier((own_a, *[a.astype(jnp.bfloat16) for a in part]))
     terms_a = [own_a, pair_a]
     bit = 2
     while bit < n_tp:
         count = (len(part) + 1) // 2
-        sends = [a.astype(jnp.bfloat16) for a in part[:count]]
+        sends = part[:count]
         received = [exchange(a, "tp", bit) for a in sends[:-1]]
         terms_a.append(handed(sends[-1], bit))
-        part = [a + r.astype(jnp.float32) for a, r in zip(part[count:], received)]
+        part = [(a.astype(jnp.float32) + r.astype(jnp.float32)).astype(jnp.bfloat16) for a, r in zip(part[count:], received)]
         bit *= 2
 
     part = [kept_b[i].astype(jnp.float32) + got_b[i].astype(jnp.float32) for i in range(half)]
@@ -275,12 +307,16 @@
     part = [a.astype(jnp.bfloat16) for a in part]
     terms_b = [handed(a, x) for x, a in enumerate(part)]
 
-    def total_of(terms):
-        return sum(term.astype(jnp.float32) for term in terms).astype(jnp.bfloat16)
-
-    total_a = total_of(terms_a)
-    total_a, *terms_b = lax.optimization_barrier((total_a, *terms_b))
-    return jnp.concatenate([total_a, total_of(terms_b)], axis=1)[None]
+    terms = [*terms_a, *terms_b]
+    (out,) = pl.pallas_call(
+        functools.partial(total_kernel, len(terms_a)),
+        in_specs=[WHOLE] * len(terms),
+        out_shape=[pltpu.HBM((rows, block_width), jnp.bfloat16)],
+        out_specs=[IN_HBM],
+        scratch_shapes=[pltpu.VMEM((rows, block_width), jnp.bfloat16), pltpu.SemaphoreType.DMA((2,))],
+        compiler_params=pltpu.CompilerParams(vmem_limit_bytes=16 * MIB),
+    )(*[in_vmem(term) for term in terms])
+    return out[None]
 
 
 def solution(mesh):

time: 49.9 us -> 48.5 us (0.972)
  waiting for transfers between devices: 21.2 us -> 17.9 us
  starting transfers between devices: 16.9 us -> 18.9 us
  other arithmetic: 1 us -> 0.11 us
  Pallas kernels: 9.91 us -> 10.7 us
    ppermute x8, waiting for transfers between devices: 13.3 us -> 10.4 us  [exchange(): return lax.ppermute(block, axis, route)]
    ppermute x5, starting transfers between devices: 8.87 us -> 10.4 us  [handed(): return lax.ppermute(block, ('section', 'tp'), route)]
    pallas_call x1 -> x3, Pallas kernels: 1.17 us -> 2.45 us  [the longest x1 1.2 us: on_device(): local_call(functools.partial(finish_kernel, len(far_values), block_width,...]
    broadcast_in_dim x1 -> x0, other arithmetic: 0.75 us -> none  [on_device(): return jnp.concatenate([total_a, total_of(terms_b)], axis=1)[None]]
    pallas_call x3 -> x2, Pallas kernels: 1.67 us -> 1.21 us  [projected(): local_call(functools.partial(project_kernel, groups, block_width), [WHOLE...]
  transfers between devices with their start and end apart: 13 -> 13, of which waited for: 6 -> 5; matrix products, arithmetic and copies ran while one was open for 0% -> 0% of each run, Pallas kernels for 17% -> 18%
where the time goes in v4:
time: 48.5 us; the launch traced here: 48.3 us
  starting transfers between devices  18.9 us (39%)
  waiting for transfers between devices  17.9 us (37%)
  Pallas kernels  10.7 us (22%)
  between operations  0.76 us (2%)
    ppermute x8, waiting for transfers between devices, exchange(): return lax.ppermute(block, axis, route)  10.4 us
    ppermute x5, starting transfers between devices, handed(): return lax.ppermute(block, ('section', 'tp'), route)  10.4 us
    ppermute x8, starting transfers between devices, exchange(): return lax.ppermute(block, axis, route)  8.49 us
    ppermute x5, waiting for transfers between devices, handed(): return lax.ppermute(block, ('section', 'tp'), route)  7.5 us
    pallas_call x1, Pallas kernels, on_device(): local_call(functools.partial(early_kernel, [m for m, _, _ in near]), [SCA...  4.32 us
    pallas_call x2, Pallas kernels, late(): local_call(functools.partial(late_kernel, masks), [SCALARS] + [WHOLE] * l...  2.75 us
    pallas_call x2, Pallas kernels, projected(): local_call(functools.partial(project_kernel, groups, block_width), [WHOLE...  1.21 us
    pallas_call x1, Pallas kernels, on_device(): local_call(functools.partial(finish_kernel, len(far_values), block_width,...  1.2 us
  transfers between devices with their start and end apart: 13, of which 5 were waited for; matrix products, arithmetic and copies ran while one was open for 0% of the time, Pallas kernels for 18%

profile of v4, /device:TPU:0, one launch (start us, length us, event | category | flops | bytes accessed | tf_op | source)
XLA Modules:
  0.0 48.3 jit_solution(12172880483449186209)
XLA Ops:
  0.0 3.0 %collective-permute-start = (bf16[1,640,256]{2,1,0:T(8,128)(2,1)}, bf16[1,640,256]{2,1,0:T(8,128)(2,1)S(1)}, u32[]{:S(2)}, u32[]{:S(2)}) collective-permute-start(bf16[1,640,256]{2,1,0:T(8,128)(2,1)} %key_hbm.1), channel_id=1, source_target_pairs={{0,16},{8,24},{16,0},{24,8},{1,17},{9,25},{17,1},{25,9},{2,18},{10... | collective-permute-start | bytes 983048 | tf_op jit(solution)/shard_map/ppermute | solution.py:26
  3.0 0.0 collective-permute-start.1
  3.0 0.5 %collective-permute-start.2 = (bf16[1,640,256]{2,1,0:T(8,128)(2,1)}, bf16[1,640,256]{2,1,0:T(8,128)(2,1)S(1)}, u32[]{:S(2)}, u32[]{:S(2)}) collective-permute-start(bf16[1,640,256]{2,1,0:T(8,128)(2,1)} %value_hbm.1), channel_id=1, source_target_pairs={{0,8},{8,0},{16,24},{24,16},{1,9},{9,1},{17,25},{25,17},{2,10},{10... | collective-permute-start | bytes 983048 | tf_op jit(solution)/shard_map/ppermute | solution.py:26
  3.5 0.0 collective-permute-start.3
  4.1 7.6 %collective-permute-done.refs_0_ = bf16[1,640,256]{2,1,0:T(8,128)(2,1)S(1)} collective-permute-done((bf16[1,640,256]{2,1,0:T(8,128)(2,1)}, bf16[1,640,256]{2,1,0:T(8,128)(2,1)S(1)}, u32[]{:S(2)}, u32[]{:S(2)}) %collective-permute-start) | collective-permute-done | bytes 327712 | tf_op jit(solution)/shard_map/ppermute | solution.py:26
  11.7 0.0 collective-permute-done.1.refs_0_
  11.7 0.0 collective-permute-done.2.refs_1_
  11.7 4.3 %shard_map.64 = (f32[2,512,128]{2,1,0:T(8,128)S(1)}, f32[2,512,128]{2,1,0:T(8,128)S(1)}, f32[2,512,128]{2,1,0:T(8,128)S(1)}, bf16[2,512,128]{2,1,0:T(8,128)(2,1)S(1)}, bf16[1,1024,5120]{2,1,0:T(8,128)(2,1)S(1)}) custom-call(s32[1]{0:T(128)S(6)} %copy.7.offset_ref, bf16[1,128,1024]{2,1,0:T(8,128)(2,1)} %q_hbm.1, bf16[1,640,256]{2,1,0:T(8,128)(2,1)} %key_hbm.1, ...), custom_call_target="tpu_custom_call" | custom-call | tf_op jit(solution)/shard_map/pallas_call | solution.py:212
  16.0 0.0 copy-start
  16.1 0.1 collective-permute-start.4
  16.1 1.4 %shard_map.65 = (f32[2,512,128]{2,1,0:T(8,128)S(1)}, f32[2,512,128]{2,1,0:T(8,128)S(1)}, f32[2,512,128]{2,1,0:T(8,128)S(1)}, bf16[2,512,640]{2,1,0:T(8,128)(2,1)S(1)}) custom-call(s32[1]{0:T(128)S(6)} %copy.7.offset_ref, bf16[2,512,128]{2,1,0:T(8,128)(2,1)S(1)} %get-tuple-element.35.q_ref, f32[2,512,128]{2,1,0:T(8,128)S(1)} %get-tuple-element.38.max_ref, ...), custom_call_target="tpu_custom_call" | custom-call | tf_op jit(solution)/shard_map/pallas_call | solution.py:233
  17.5 0.4 collective-permute-done.3.refs_0_
  17.9 0.2 collective-permute-start.5
  18.1 0.0 collective-permute-done.4.refs_0_
  18.1 1.4 %shard_map.66 = (f32[2,512,128]{2,1,0:T(8,128)S(1)}, f32[2,512,128]{2,1,0:T(8,128)S(1)}, f32[2,512,128]{2,1,0:T(8,128)S(1)}, bf16[2,512,640]{2,1,0:T(8,128)(2,1)S(1)}) custom-call(s32[1]{0:T(128)S(6)} %copy.7.offset_ref, bf16[2,512,128]{2,1,0:T(8,128)(2,1)S(1)} %get-tuple-element.35.q_ref, f32[2,512,128]{2,1,0:T(8,128)S(1)} %get-tuple-element.41.max_ref.before_ref, ...), custom_call_target="tpu_custom_call" | custom-call | tf_op jit(solution)/shard_map/pallas_call | solution.py:233
  19.5 0.1 collective-permute-done.5.refs_1_
  19.5 1.2 %shard_map.67 = (bf16[128,1024]{1,0:T(8,128)(2,1)S(1)}, bf16[1,128,1024]{2,1,0:T(8,128)(2,1)S(1)}) custom-call(f32[2,512,128]{2,1,0:T(8,128)S(1)} %get-tuple-element.41.max_ref.before_ref, f32[2,512,128]{2,1,0:T(8,128)S(1)} %get-tuple-element.46.top_ref, f32[2,512,128]{2,1,0:T(8,128)S(1)} %get-tuple-element.47.total_ref, ...), custom_call_target="tpu_custom_call" | custom-call | tf_op jit(solution)/shard_map/pallas_call | solution.py:257
  20.7 2.1 %collective-permute-start.7 = (bf16[1,128,1024]{2,1,0:T(8,128)(2,1)S(1)}, bf16[1,128,1024]{2,1,0:T(8,128)(2,1)S(1)}, u32[]{:S(2)}, u32[]{:S(2)}) collective-permute-start(bf16[1,128,1024]{2,1,0:T(8,128)(2,1)S(1)} %get-tuple-element.55), channel_id=1, source_target_pairs={{0,1},{1,0},{2,3},{3,2},{4,5},{5,4},{6,7},{7,6},{8,9},{9,8},{10,11... | collective-permute-start | bytes 786440 | tf_op jit(solution)/shard_map/ppermute | solution.py:26
  22.9 0.0 copy-done
  22.9 0.5 shard_map.68
  23.3 1.6 %collective-permute-start.6 = (bf16[128,1024]{1,0:T(8,128)(2,1)S(1)}, bf16[128,1024]{1,0:T(8,128)(2,1)S(1)}, u32[]{:S(2)}, u32[]{:S(2)}) collective-permute-start(bf16[128,1024]{1,0:T(8,128)(2,1)S(1)} %shard_map.68), channel_id=1, source_target_pairs={{0,4},{1,5},{2,6},{3,7},{4,0},{5,1},{6,2},{7,3},{8,12},{9,13},{10,... | collective-permute-start | bytes 786440 | tf_op jit(solution)/shard_map/ppermute | solution.py:32
  24.9 0.6 %shard_map.70 = (bf16[2,128,256]{2,1,0:T(8,128)(2,1)S(1)}, bf16[1,128,1024]{2,1,0:T(8,128)(2,1)S(1)}) custom-call(bf16[128,1024]{1,0:T(8,128)(2,1)S(1)} %get-tuple-element.53.att_ref, bf16[1,1024,5120]{2,1,0:T(8,128)(2,1)S(1)} %get-tuple-element.49.w_ref), custom_call_target="tpu_custom_call" | custom-call | flops 402653184 | tf_op jit(solution)/shard_map/pallas_call | solution.py:273
  25.5 0.6 %shard_map.69 = (bf16[1,128,1024]{2,1,0:T(8,128)(2,1)S(1)}, bf16[2,128,256]{2,1,0:T(8,128)(2,1)S(1)}) custom-call(bf16[128,1024]{1,0:T(8,128)(2,1)S(1)} %get-tuple-element.53.att_ref, bf16[1,1024,5120]{2,1,0:T(8,128)(2,1)S(1)} %get-tuple-element.49.w_ref), custom_call_target="tpu_custom_call" | custom-call | flops 402653184 | tf_op jit(solution)/shard_map/pallas_call | solution.py:273
  26.1 2.6 %collective-permute-start.10 = (bf16[2,128,256]{2,1,0:T(8,128)(2,1)S(1)}, bf16[2,128,256]{2,1,0:T(8,128)(2,1)S(1)}, u32[]{:S(2)}, u32[]{:S(2)}) collective-permute-start(bf16[2,128,256]{2,1,0:T(8,128)(2,1)S(1)} %get-tuple-element.60), channel_id=1, source_target_pairs={{0,2},{1,3},{2,0},{3,1},{4,6},{5,7},{6,4},{7,5},{8,10},{9,11},{10,... | collective-permute-start | bytes 393224 | tf_op jit(solution)/shard_map/ppermute | solution.py:26
  28.7 0.5 collective-permute-start.8
  29.2 2.3 %collective-permute-done.7 = bf16[1,128,1024]{2,1,0:T(8,128)(2,1)S(1)} collective-permute-done((bf16[1,128,1024]{2,1,0:T(8,128)(2,1)S(1)}, bf16[1,128,1024]{2,1,0:T(8,128)(2,1)S(1)}, u32[]{:S(2)}, u32[]{:S(2)}) %collective-permute-start.7) | collective-permute-done | bytes 262176 | tf_op jit(solution)/shard_map/ppermute | solution.py:26
  31.6 0.1 fusion
  31.6 0.0 collective-permute-done.6.refs_0_
  31.7 4.2 %collective-permute-start.9 = (bf16[128,1024]{1,0:T(8,128)(2,1)S(1)}, bf16[128,1024]{1,0:T(8,128)(2,1)S(1)}, u32[]{:S(2)}, u32[]{:S(2)}) collective-permute-start(bf16[128,1024]{1,0:T(8,128)(2,1)S(1)} %fusion), channel_id=1, source_target_pairs={{0,6},{1,7},{2,4},{3,5},{4,2},{5,3},{6,0},{7,1},{8,14},{9,15},{10,... | collective-permute-start | bytes 786440 | tf_op jit(solution)/shard_map/ppermute | solution.py:32
  35.8 0.0 collective-permute-done.10
  35.9 0.1 collective-permute-start.11
  36.0 4.1 %collective-permute-start.12 = (bf16[128,256]{1,0:T(8,128)(2,1)S(1)}, bf16[128,256]{1,0:T(8,128)(2,1)S(1)}, u32[]{:S(2)}, u32[]{:S(2)}) collective-permute-start(bf16[128,256]{1,0:T(8,128)(2,1)S(1)} %get-tuple-element.61), channel_id=1, source_target_pairs={{0,5},{1,4},{2,7},{3,6},{4,1},{5,0},{6,3},{7,2},{8,13},{9,12},{10,... | collective-permute-start | bytes 196616 | tf_op jit(solution)/shard_map/ppermute | solution.py:32
  40.0 7.5 %collective-permute-done.11.refs_3_ = bf16[128,256]{1,0:T(8,128)(2,1)S(1)} collective-permute-done((bf16[128,256]{1,0:T(8,128)(2,1)S(1)}, bf16[128,256]{1,0:T(8,128)(2,1)S(1)}, u32[]{:S(2)}, u32[]{:S(2)}) %collective-permute-start.11) | collective-permute-done | bytes 65568 | tf_op jit(solution)/shard_map/ppermute | solution.py:32
  47.5 0.0 collective-permute-done.12.refs_4_
  47.5 0.0 collective-permute-done.8.refs_1_
  47.5 0.0 collective-permute-done.9.refs_2_
  47.5 0.8 %shard_map.71 = bf16[128,1280]{1,0:T(8,128)(2,1)} custom-call(bf16[128,1024]{1,0:T(8,128)(2,1)S(1)} %collective-permute-done.6.refs_0_, bf16[128,1024]{1,0:T(8,128)(2,1)S(1)} %collective-permute-done.8.refs_1_, bf16[128,1024]{1,0:T(8,128)(2,1)S(1)} %collective-permute-done.9.refs_2_, bf16[128,256]{1,0:T(8,128)(2,1)S(1)} %collective-permute-done.11.refs_3_, ...), custom_call_target="tpu_custom_call" | custom-call | tf_op jit(solution)/shard_map/pallas_call | solution.py:311
  (1 shorter events, 0.0 us)
Async XLA Ops:
  0.0 11.7 %collective-permute-start = (bf16[1,640,256]{2,1,0:T(8,128)(2,1)}, bf16[1,640,256]{2,1,0:T(8,128)(2,1)S(1)}, u32[]{:S(2)}, u32[]{:S(2)}) collective-permute-start(bf16[1,640,256]{2,1,0:T(8,128)(2,1)} %key_hbm.1), channel_id=1, source_target_pairs={{0,16},{8,24},{16,0},{24,8},{1,17},{9,25},{17,1},{25,9},{2,18},{10... | collective-permute-start | bytes 983048 | tf_op jit(solution)/shard_map/ppermute | solution.py:26
  3.0 8.7 %collective-permute-start.1 = (bf16[1,640,256]{2,1,0:T(8,128)(2,1)}, bf16[1,640,256]{2,1,0:T(8,128)(2,1)S(1)}, u32[]{:S(2)}, u32[]{:S(2)}) collective-permute-start(bf16[1,640,256]{2,1,0:T(8,128)(2,1)} %key_hbm.1), channel_id=1, source_target_pairs={{0,8},{8,0},{16,24},{24,16},{1,9},{9,1},{17,25},{25,17},{2,10},{10... | collective-permute-start | bytes 983048 | tf_op jit(solution)/shard_map/ppermute | solution.py:26
  3.0 8.7 %collective-permute-start.2 = (bf16[1,640,256]{2,1,0:T(8,128)(2,1)}, bf16[1,640,256]{2,1,0:T(8,128)(2,1)S(1)}, u32[]{:S(2)}, u32[]{:S(2)}) collective-permute-start(bf16[1,640,256]{2,1,0:T(8,128)(2,1)} %value_hbm.1), channel_id=1, source_target_pairs={{0,8},{8,0},{16,24},{24,16},{1,9},{9,1},{17,25},{25,17},{2,10},{10... | collective-permute-start | bytes 983048 | tf_op jit(solution)/shard_map/ppermute | solution.py:26
  3.5 14.4 %collective-permute-start.3 = (bf16[1,640,256]{2,1,0:T(8,128)(2,1)}, bf16[1,640,256]{2,1,0:T(8,128)(2,1)S(1)}, u32[]{:S(2)}, u32[]{:S(2)}) collective-permute-start(bf16[1,640,256]{2,1,0:T(8,128)(2,1)} %value_hbm.1), channel_id=1, source_target_pairs={{0,16},{8,24},{16,0},{24,8},{1,17},{9,25},{17,1},{25,9},{2,18},{10... | collective-permute-start | bytes 983048 | tf_op jit(solution)/shard_map/ppermute | solution.py:26
  16.0 6.8 %copy-start = (bf16[1,128,1280]{2,1,0:T(8,128)(2,1)S(1)}, bf16[1,128,1280]{2,1,0:T(8,128)(2,1)}, u32[]{:S(2)}) copy-start(bf16[1,128,1280]{2,1,0:T(8,128)(2,1)} %residual_ref.1) | copy-start | bytes 983044
  16.1 2.0 %collective-permute-start.4 = (bf16[1,640,256]{2,1,0:T(8,128)(2,1)S(1)}, bf16[1,640,256]{2,1,0:T(8,128)(2,1)S(1)}, u32[]{:S(2)}, u32[]{:S(2)}) collective-permute-start(bf16[1,640,256]{2,1,0:T(8,128)(2,1)S(1)} %collective-permute-done.refs_0_), channel_id=1, source_target_pairs={{0,8},{8,0},{16,24},{24,16},{1,9},{9,1},{17,25},{25,17},{2,10},{10... | collective-permute-start | bytes 983048 | tf_op jit(solution)/shard_map/ppermute | solution.py:26
  17.9 1.6 %collective-permute-start.5 = (bf16[1,640,256]{2,1,0:T(8,128)(2,1)S(1)}, bf16[1,640,256]{2,1,0:T(8,128)(2,1)S(1)}, u32[]{:S(2)}, u32[]{:S(2)}) collective-permute-start(bf16[1,640,256]{2,1,0:T(8,128)(2,1)S(1)} %collective-permute-done.3.refs_0_), channel_id=1, source_target_pairs={{0,8},{8,0},{16,24},{24,16},{1,9},{9,1},{17,25},{25,17},{2,10},{10... | collective-permute-start | bytes 983048 | tf_op jit(solution)/shard_map/ppermute | solution.py:26
  20.7 10.8 %collective-permute-start.7 = (bf16[1,128,1024]{2,1,0:T(8,128)(2,1)S(1)}, bf16[1,128,1024]{2,1,0:T(8,128)(2,1)S(1)}, u32[]{:S(2)}, u32[]{:S(2)}) collective-permute-start(bf16[1,128,1024]{2,1,0:T(8,128)(2,1)S(1)} %get-tuple-element.55), channel_id=1, source_target_pairs={{0,1},{1,0},{2,3},{3,2},{4,5},{5,4},{6,7},{7,6},{8,9},{9,8},{10,11... | collective-permute-start | bytes 786440 | tf_op jit(solution)/shard_map/ppermute | solution.py:26
  23.3 8.3 %collective-permute-start.6 = (bf16[128,1024]{1,0:T(8,128)(2,1)S(1)}, bf16[128,1024]{1,0:T(8,128)(2,1)S(1)}, u32[]{:S(2)}, u32[]{:S(2)}) collective-permute-start(bf16[128,1024]{1,0:T(8,128)(2,1)S(1)} %shard_map.68), channel_id=1, source_target_pairs={{0,4},{1,5},{2,6},{3,7},{4,0},{5,1},{6,2},{7,3},{8,12},{9,13},{10,... | collective-permute-start | bytes 786440 | tf_op jit(solution)/shard_map/ppermute | solution.py:32
  26.1 9.7 %collective-permute-start.10 = (bf16[2,128,256]{2,1,0:T(8,128)(2,1)S(1)}, bf16[2,128,256]{2,1,0:T(8,128)(2,1)S(1)}, u32[]{:S(2)}, u32[]{:S(2)}) collective-permute-start(bf16[2,128,256]{2,1,0:T(8,128)(2,1)S(1)} %get-tuple-element.60), channel_id=1, source_target_pairs={{0,2},{1,3},{2,0},{3,1},{4,6},{5,7},{6,4},{7,5},{8,10},{9,11},{10,... | collective-permute-start | bytes 393224 | tf_op jit(solution)/shard_map/ppermute | solution.py:26
  28.7 18.8 %collective-permute-start.8 = (bf16[128,1024]{1,0:T(8,128)(2,1)S(1)}, bf16[128,1024]{1,0:T(8,128)(2,1)S(1)}, u32[]{:S(2)}, u32[]{:S(2)}) collective-permute-start(bf16[128,1024]{1,0:T(8,128)(2,1)S(1)} %bitcast.8), channel_id=1, source_target_pairs={{0,5},{1,4},{2,7},{3,6},{4,1},{5,0},{6,3},{7,2},{8,13},{9,12},{10,... | collective-permute-start | bytes 786440 | tf_op jit(solution)/shard_map/ppermute | solution.py:32
  31.7 15.9 %collective-permute-start.9 = (bf16[128,1024]{1,0:T(8,128)(2,1)S(1)}, bf16[128,1024]{1,0:T(8,128)(2,1)S(1)}, u32[]{:S(2)}, u32[]{:S(2)}) collective-permute-start(bf16[128,1024]{1,0:T(8,128)(2,1)S(1)} %fusion), channel_id=1, source_target_pairs={{0,6},{1,7},{2,4},{3,5},{4,2},{5,3},{6,0},{7,1},{8,14},{9,15},{10,... | collective-permute-start | bytes 786440 | tf_op jit(solution)/shard_map/ppermute | solution.py:32
  35.9 11.6 %collective-permute-start.11 = (bf16[128,256]{1,0:T(8,128)(2,1)S(1)}, bf16[128,256]{1,0:T(8,128)(2,1)S(1)}, u32[]{:S(2)}, u32[]{:S(2)}) collective-permute-start(bf16[128,256]{1,0:T(8,128)(2,1)S(1)} %get-tuple-element.62), channel_id=1, source_target_pairs={{0,4},{1,5},{2,6},{3,7},{4,0},{5,1},{6,2},{7,3},{8,12},{9,13},{10,... | collective-permute-start | bytes 196616 | tf_op jit(solution)/shard_map/ppermute | solution.py:32
  36.0 11.6 %collective-permute-start.12 = (bf16[128,256]{1,0:T(8,128)(2,1)S(1)}, bf16[128,256]{1,0:T(8,128)(2,1)S(1)}, u32[]{:S(2)}, u32[]{:S(2)}) collective-permute-start(bf16[128,256]{1,0:T(8,128)(2,1)S(1)} %get-tuple-element.61), channel_id=1, source_target_pairs={{0,5},{1,4},{2,7},{3,6},{4,1},{5,0},{6,3},{7,2},{8,13},{9,12},{10,... | collective-permute-start | bytes 196616 | tf_op jit(solution)/shard_map/ppermute | solution.py:32

commit v5 on v4

v5 whole, which is shorter than its diff:
```python
import functools
import math

import jax
import jax.numpy as jnp
from jax import lax
from jax.experimental import pallas as pl
from jax.experimental.pallas import tpu as pltpu
from jax.sharding import PartitionSpec as P

HD = 128
G = 4
LANES = 128
NEG_FILL = -1e30
MAX_FLOOR = -1e29
EXP_SCALE = HD ** (-0.5) * math.log2(math.e)
LOG2_E = math.log2(math.e)
LOG_ROWS = 8
LOG_SPACE = 32
MIB = 1 << 20

WHOLE = pl.BlockSpec(memory_space=pltpu.VMEM)
IN_HBM = pl.BlockSpec(memory_space=pltpu.HBM)
SCALARS = pl.BlockSpec(memory_space=pltpu.SMEM)


def exchange(block, axis, mask):
    route = [(i, i ^ mask) for i in range(lax.axis_size(axis))]
    return lax.ppermute(block, axis, route)


def handed(block, mask):
    sections, n_tp = lax.axis_size("section"), lax.axis_size("tp")
    route = [(s * n_tp + i, (s + 1) % sections * n_tp + (i ^ mask)) for s in range(sections) for i in range(n_tp)]
    return lax.ppermute(block, ("section", "tp"), route)


def in_vmem(array):
    return pltpu.with_memory_space_constraint(array, pltpu.VMEM)


def local_call(body, ins, outs, limit, flops, scratch=()):
    return pl.pallas_call(
        body,
        in_specs=ins,
        out_shape=[pltpu.VMEM(shape, dtype) for shape, dtype in outs],
        out_specs=[WHOLE] * len(outs),
        scratch_shapes=list(scratch),
        compiler_params=pltpu.CompilerParams(vmem_limit_bytes=limit),
        cost_estimate=pl.CostEstimate(flops=flops, bytes_accessed=0, transcendentals=0),
    )


def stacked_query(q_ref, kv_head):
    heads = range(kv_head * G, (kv_head + 1) * G)
    return jnp.concatenate([q_ref[0, :, h * HD : (h + 1) * HD] for h in heads], axis=0)


def masked_scores(query, key_ref, kv_head, bound):
    keys = key_ref[0, :, kv_head * HD : (kv_head + 1) * HD]
    scores = lax.dot_general(query, keys, (((1,), (1,)), ((), ())), preferred_element_type=jnp.float32)
    rows = query.shape[0] // G
    ahead = lax.broadcasted_iota(jnp.int32, scores.shape, 1) - lax.broadcasted_iota(jnp.int32, scores.shape, 0) % rows
    return jnp.where(ahead <= bound, scores, NEG_FILL)


def attend(query, key_refs, value_refs, kv_head, bounds):
    columns = slice(kv_head * HD, (kv_head + 1) * HD)
    parts = [masked_scores(query, ref, kv_head, bound) for ref, bound in zip(key_refs, bounds)]
    top = functools.reduce(jnp.maximum, [jnp.max(part, axis=1, keepdims=True) for part in parts])
    top = jnp.maximum(top, MAX_FLOOR)
    weights = [jnp.exp2((part - top) * EXP_SCALE) for part in parts]
    total = sum(jnp.sum(part, axis=1, keepdims=True) for part in weights)
    mixed = sum(
        jnp.dot(part.astype(jnp.bfloat16), ref[0, :, columns], preferred_element_type=jnp.float32)
        for part, ref in zip(weights, value_refs)
    )
    some = total > 0.0
    total = jnp.where(some, total, 1.0)
    return mixed / total, jnp.where(some, top * EXP_SCALE + jnp.log(total) * LOG2_E, NEG_FILL)


def copy_all(pairs, sems):
    copies = [pltpu.make_async_copy(source, target, sems.at[i]) for i, (source, target) in enumerate(pairs)]
    for copy in copies:
        copy.start()
    return copies


def query_kernel(q_hbm, *refs):
    *query_refs, q_ref, sem = refs
    copy = pltpu.make_async_copy(q_hbm, q_ref, sem)
    copy.start()
    copy.wait()
    for kv_head, query_ref in enumerate(query_refs):
        query_ref[...] = stacked_query(q_ref, kv_head)


def cache_kernel(key_hbm, value_hbm, w_hbm, key_ref, value_ref, w_ref, sems):
    span = pl.ds(0, w_ref.shape[1])
    for copy in copy_all(((key_hbm, key_ref), (value_hbm, value_ref), (w_hbm.at[:, span], w_ref)), sems):
        copy.wait()


def bounds_of(masks, offset, block, rows, length):
    own = lax.axis_index("ctx")
    return [offset + block * rows - (own ^ mask) * length for mask in masks]


def near_kernel(masks, kv_local, offset_ref, w_hbm, *refs):
    count = len(masks)
    query_refs, refs = refs[:kv_local], refs[kv_local:]
    key_refs, value_refs, refs = refs[:count], refs[count : 2 * count], refs[2 * count :]
    result_ref, log_ref, *w_refs, sems = refs
    heights = [ref.shape[1] for ref in w_refs]
    parts = [w_hbm.at[:, pl.ds((i + 1) * height, height)] for i, height in enumerate(heights)]
    copies = copy_all(zip(parts, w_refs), sems)
    rows, length = query_refs[0].shape[0] // G, key_refs[0].shape[1]
    bounds = bounds_of(masks, offset_ref[0], lax.axis_index("ctx"), rows, length)
    for kv_head, query_ref in enumerate(query_refs):
        result, log_sum = attend(query_ref[...], key_refs, value_refs, kv_head, bounds)
        result_ref[kv_head] = result
        log_ref[kv_head] = jnp.broadcast_to(log_sum, log_ref.shape[1:])
    for copy in copies:
        copy.wait()


def far_kernel(masks, far, kv_head, offset_ref, query_ref, *refs):
    count = len(masks)
    key_refs, value_refs, (out_ref,) = refs[:count], refs[count : 2 * count], refs[2 * count :]
    stacked = query_ref.shape[0]
    rows, length = stacked // G, key_refs[0].shape[1]
    bounds = bounds_of(masks, offset_ref[0], lax.axis_index("ctx") ^ far, rows, length)
    result, log_sum = attend(query_ref[...], key_refs, value_refs, kv_head, bounds)
    out_ref[:stacked] = result.astype(jnp.bfloat16)
    lane = lax.broadcasted_iota(jnp.int32, (rows, LANES), 1)
    logs = jnp.zeros((rows, LANES), jnp.float32)
    for g in range(G):
        logs = jnp.where(lane == g, log_sum[g * rows : (g + 1) * rows], logs)
    logs = logs.T[:LOG_ROWS]
    high = logs.astype(jnp.bfloat16).astype(jnp.float32)
    middle = (logs - high).astype(jnp.bfloat16).astype(jnp.float32)
    low = logs - high - middle
    rest = jnp.zeros((LOG_SPACE - 3 * LOG_ROWS, rows), jnp.float32)
    out_ref[stacked:] = jnp.concatenate([high, middle, low, rest], axis=0).astype(jnp.bfloat16)


def block_columns(group, slot, block_width):
    xs, lower, width = group
    return pl.ds(pl.multiple_of((lax.axis_index("tp") ^ xs[slot]) * block_width + lower, LANES), width)


def projected_block(att_refs, w_refs, columns):
    return sum(
        jnp.dot(att_ref[...], w_ref[0, :, columns], preferred_element_type=jnp.float32)
        for att_ref, w_ref in zip(att_refs, w_refs)
    )


def combine_kernel(kv_head, group, block_width, near_ref, log_ref, far_ref, w_ref, *refs):
    *before_refs, att_ref, send_ref = refs
    rows = att_ref.shape[0]
    stacked = G * rows
    parts = far_ref[stacked:].astype(jnp.float32)
    logs = sum(parts[i * LOG_ROWS : (i + 1) * LOG_ROWS] for i in range(3))
    logs = jnp.concatenate([logs, jnp.zeros((LANES - LOG_ROWS, rows), jnp.float32)], axis=0).T
    for g in range(G):
        span = slice(g * rows, (g + 1) * rows)
        near_log, far_log = log_ref[kv_head, span, :1], logs[:, g : g + 1]
        top = jnp.maximum(near_log, far_log)
        near_weight, far_weight = jnp.exp2(near_log - top), jnp.exp2(far_log - top)
        scale = 1.0 / (near_weight + far_weight)
        mixed = near_ref[kv_head, span] * (near_weight * scale)
        mixed += far_ref[span].astype(jnp.float32) * (far_weight * scale)
        att_ref[:, g * HD : (g + 1) * HD] = mixed.astype(jnp.bfloat16)
    for slot in range(len(group[0])):
        block = projected_block([att_ref], [w_ref], block_columns(group, slot, block_width))
        for before_ref in before_refs:
            block += before_ref[slot]
        send_ref[slot] = block.astype(send_ref.dtype)


def own_kernel(count, group, block_width, *refs):
    att_refs, w_refs, (residual_ref, own_ref) = refs[:count], refs[count : 2 * count], refs[2 * count :]
    own = projected_block(att_refs, w_refs, block_columns(group, 0, block_width))
    own_ref[...] = (residual_ref[0, :, : own_ref.shape[1]].astype(jnp.float32) + own).astype(jnp.bfloat16)


def project_kernel(count, groups, block_width, *refs):
    att_refs, w_refs, out_refs = refs[:count], refs[count : 2 * count], refs[2 * count :]
    for group, out_ref in zip(groups, out_refs):
        for slot in range(len(group[0])):
            block = projected_block(att_refs, w_refs, block_columns(group, slot, block_width))
            out_ref[slot] = block.astype(jnp.bfloat16)


def total_kernel(count, *refs):
    *term_refs, out_ref, total_ref, sems = refs
    lower = term_refs[0].shape[1]
    half = out_ref.shape[0] // 2
    copies = []
    for i, rows in enumerate((slice(0, half), slice(half, 2 * half))):
        for group, columns in ((term_refs[:count], slice(0, lower)), (term_refs[count:], slice(lower, None))):
            total_ref[rows, columns] = sum(ref[rows].astype(jnp.float32) for ref in group).astype(jnp.bfloat16)
        copies.append(pltpu.make_async_copy(total_ref.at[rows], out_ref.at[rows], sems.at[i]))
        copies[-1].start()
    for copy in copies:
        copy.wait()


def xor_order(lowest, size):
    if lowest >= size:
        return [0]
    rest = xor_order(lowest * 2, size)
    return [x + lowest for x in rest] + rest


def cross_first_width(width):
    return max(1, (2 * (width // LANES)) // 10) * LANES


def on_device(row_offsets, queries, cache_keys, cache_values, residual, out_weight):
    n_ctx, n_tp = lax.axis_size("ctx"), lax.axis_size("tp")
    rows = queries.shape[1]
    kv_local = cache_keys.shape[2] // HD
    stacked = G * rows
    top_bit = n_ctx // 2
    block_width = out_weight.shape[2] // n_tp
    bf16, f32 = jnp.bfloat16, jnp.float32

    in_hbm = [pltpu.with_memory_space_constraint(a, pltpu.HBM) for a in (queries, cache_keys, cache_values, out_weight)]
    own_queries = local_call(
        query_kernel,
        [IN_HBM],
        [((stacked, HD), bf16)] * kv_local,
        16 * MIB,
        0,
        [pltpu.VMEM(queries.shape, bf16), pltpu.SemaphoreType.DMA],
    )(in_hbm[0])
    far_queries = [exchange(query, "ctx", top_bit) for query in own_queries]
    near = [(0, cache_keys, cache_values)]
    bit = top_bit // 2
    while bit:
        near += [(m | bit, exchange(k, "ctx", bit), exchange(v, "ctx", bit)) for m, k, v in near]
        bit //= 2
    w_shape = (1, G * HD, out_weight.shape[2])
    own_keys, own_values, first_weight = local_call(
        cache_kernel,
        [IN_HBM] * 3,
        [(cache_keys.shape, bf16), (cache_values.shape, bf16), (w_shape, bf16)],
        16 * MIB,
        0,
        [pltpu.SemaphoreType.DMA((3,))],
    )(*in_hbm[1:])
    masks, near_keys, near_values = zip(*near)
    cached = [in_vmem(a) for a in (own_keys, *near_keys[1:], own_values, *near_values[1:])]
    far_results = []
    for kv_head in range(kv_local):
        query = far_queries[kv_head]
        if kv_head:
            query, _ = lax.optimization_barrier((query, result))
        (result,) = local_call(
            functools.partial(far_kernel, masks, top_bit, kv_head),
            [SCALARS] + [WHOLE] * (1 + len(cached)),
            [((stacked + LOG_SPACE, HD), bf16)],
            24 * MIB,
            0,
        )(row_offsets, in_vmem(query), *cached)
        far_results.append(exchange(result, "ctx", top_bit))
    near_result, near_log, *weights = local_call(
        functools.partial(near_kernel, masks, kv_local),
        [SCALARS, IN_HBM] + [WHOLE] * (kv_local + len(cached)),
        [((kv_local, stacked, HD), f32)] * 2 + [(w_shape, bf16)] * (kv_local - 1),
        24 * MIB,
        0,
        [pltpu.SemaphoreType.DMA((kv_local,))],
    )(row_offsets, in_hbm[3], *own_queries, *cached)
    weights = [first_weight, *weights]

    across = xor_order(2, n_tp)[:-1]
    cross_width = cross_first_width(block_width)
    pair_width = block_width - cross_width
    block_flops = 2 * rows * out_weight.shape[1]
    relay = ([1 ^ x for x in across], 0, pair_width)
    attended, sent = [], []
    for kv_head, result in enumerate(far_results):
        kind = bf16 if kv_head + 1 == kv_local else f32
        head, *sent = local_call(
            functools.partial(combine_kernel, kv_head, relay, block_width),
            [WHOLE] * (4 + len(sent)),
            [((rows, G * HD), bf16), ((len(across), rows, pair_width), kind)],
            24 * MIB,
            0,
        )(near_result, near_log, in_vmem(result), weights[kv_head], *sent)
        attended.append(head)
    (send_a,) = sent
    (own_a,) = local_call(
        functools.partial(own_kernel, kv_local, ([0], 0, pair_width), block_width),
        [WHOLE] * (2 * kv_local + 1),
        [((rows, pair_width), bf16)],
        16 * MIB,
        block_flops * pair_width,
    )(*attended, *weights, in_vmem(residual))

    def projected(*groups):
        return local_call(
            functools.partial(project_kernel, kv_local, groups, block_width),
            [WHOLE] * (2 * kv_local),
            [((len(xs), rows, width), bf16) for xs, _, width in groups],
            16 * MIB,
            block_flops * sum(len(xs) * width for xs, _, width in groups),
        )(*attended, *weights)

    half = n_tp // 2
    own_a = handed(own_a, 0)
    send_b, pair_a = projected((list(range(half, n_tp)), pair_width, cross_width), ([1], 0, pair_width))
    kept_a, kept_b = projected((across, 0, pair_width), (list(range(half)), pair_width, cross_width))
    got_a = exchange(send_a, "tp", 1)
    got_b = exchange(send_b, "tp", half)
    pair_a = handed(pair_a[0], 1)

    part = [kept_a[i].astype(jnp.float32) + got_a[i].astype(jnp.float32) for i in range(len(across))]
    own_a, *part = lax.optimization_barrier((own_a, *[a.astype(jnp.bfloat16) for a in part]))
    terms_a = [own_a, pair_a]
    bit = 2
    while bit < n_tp:
        count = (len(part) + 1) // 2
        sends = part[:count]
        received = [exchange(a, "tp", bit) for a in sends[:-1]]
        terms_a.append(handed(sends[-1], bit))
        part = [(a.astype(jnp.float32) + r.astype(jnp.float32)).astype(jnp.bfloat16) for a, r in zip(part[count:], received)]
        bit *= 2

    part = [kept_b[i].astype(jnp.float32) + got_b[i].astype(jnp.float32) for i in range(half)]
    while len(part) > 2:
        count = len(part) // 2
        received = [exchange(a.astype(jnp.bfloat16), "tp", count) for a in part[count:]]
        part = [a + r.astype(jnp.float32) for a, r in zip(part[:count], received)]
    part[0] = part[0] + residual[0, :, pair_width:].astype(jnp.float32)
    part = [a.astype(jnp.bfloat16) for a in part]
    terms_b = [handed(a, x) for x, a in enumerate(part)]

    terms = [*terms_a, *terms_b]
    (out,) = pl.pallas_call(
        functools.partial(total_kernel, len(terms_a)),
        in_specs=[WHOLE] * len(terms),
        out_shape=[pltpu.HBM((rows, block_width), jnp.bfloat16)],
        out_specs=[IN_HBM],
        scratch_shapes=[pltpu.VMEM((rows, block_width), jnp.bfloat16), pltpu.SemaphoreType.DMA((2,))],
        compiler_params=pltpu.CompilerParams(vmem_limit_bytes=16 * MIB),
    )(*[in_vmem(term) for term in terms])
    return out[None]


def solution(mesh):
    placed = (
        P("section"),
        P("section", "ctx", "tp"),
        P("section", "ctx", "tp"),
        P("section", "ctx", "tp"),
        P("section", "ctx", "tp"),
        P("section", "tp", None),
    )
    return jax.shard_map(
        on_device, mesh=mesh, in_specs=placed, out_specs=P("section", "ctx", "tp"), check_vma=False
    )
```

time: 48.5 us -> 46.2 us (0.953)
  waiting for transfers between devices: 17.9 us -> 6.77 us
  starting transfers between devices: 18.9 us -> 25.1 us
  Pallas kernels: 10.7 us -> 13.4 us
    ppermute x8, waiting for transfers between devices: 10.4 us -> 2.15 us  [exchange(): return lax.ppermute(block, axis, route)]
    ppermute x5, starting transfers between devices: 10.4 us -> 14.7 us  [handed(): return lax.ppermute(block, ('section', 'tp'), route)]
    ppermute x5, waiting for transfers between devices: 7.5 us -> 4.63 us  [handed(): return lax.ppermute(block, ('section', 'tp'), route)]
    pallas_call x7 -> x10, Pallas kernels: 9.94 us -> 12.6 us  [the longest x2 2.88 us: on_device(): local_call(functools.partial(far_kernel, masks, top_bit, kv_head), [SCALA...]
    ppermute x8, starting transfers between devices: 8.49 us -> 10.4 us  [exchange(): return lax.ppermute(block, axis, route)]
  transfers between devices with their start and end apart: 13 -> 13, of which waited for: 5 -> 6; matrix products, arithmetic and copies ran while one was open for 0% -> 0% of each run, Pallas kernels for 18% -> 25%
where the time goes in v5:
time: 46.2 us; the launch traced here: 46.1 us
  starting transfers between devices  25.1 us (54%)
  Pallas kernels  13.4 us (29%)
  waiting for transfers between devices  6.77 us (15%)
  between operations  0.76 us (2%)
    ppermute x5, starting transfers between devices, handed(): return lax.ppermute(block, ('section', 'tp'), route)  14.7 us
    ppermute x8, starting transfers between devices, exchange(): return lax.ppermute(block, axis, route)  10.4 us
    ppermute x5, waiting for transfers between devices, handed(): return lax.ppermute(block, ('section', 'tp'), route)  4.63 us
    pallas_call x2, Pallas kernels, on_device(): local_call(functools.partial(far_kernel, masks, top_bit, kv_head), [SCALA...  2.88 us
    pallas_call x1, Pallas kernels, on_device(): local_call(cache_kernel, [IN_HBM] * 3, [(cache_keys.shape, bf16), (cache_...  2.73 us
    pallas_call x1, Pallas kernels, on_device(): local_call(functools.partial(near_kernel, masks, kv_local), [SCALARS, IN_...  2.56 us
    ppermute x8, waiting for transfers between devices, exchange(): return lax.ppermute(block, axis, route)  2.15 us
    pallas_call x2, Pallas kernels, on_device(): local_call(functools.partial(combine_kernel, kv_head, relay, block_width)...  1.71 us
  transfers between devices with their start and end apart: 13, of which 6 were waited for; matrix products, arithmetic and copies ran while one was open for 0% of the time, Pallas kernels for 25%

profile of v5, /device:TPU:0, one launch (start us, length us, event | category | flops | bytes accessed | tf_op | source)
XLA Modules:
  0.0 46.1 jit_solution(8252394312108404353)
XLA Ops:
  0.0 0.5 collective-permute-start
  0.5 0.1 collective-permute-start.1
  0.5 1.0 %shard_map.64 = (bf16[512,128]{1,0:T(8,128)(2,1)S(1)}, bf16[512,128]{1,0:T(8,128)(2,1)S(1)}) custom-call(bf16[1,128,1024]{2,1,0:T(8,128)(2,1)} %q_hbm.1), custom_call_target="tpu_custom_call" | custom-call | tf_op jit(solution)/shard_map/pallas_call | solution.py:232
  1.5 3.0 %collective-permute-start.2 = (bf16[512,128]{1,0:T(8,128)(2,1)S(1)}, bf16[512,128]{1,0:T(8,128)(2,1)S(1)}, u32[]{:S(2)}, u32[]{:S(2)}) collective-permute-start(bf16[512,128]{1,0:T(8,128)(2,1)S(1)} %get-tuple-element.24.refs_0_), channel_id=1, source_target_pairs={{0,16},{8,24},{16,0},{24,8},{1,17},{9,25},{17,1},{25,9},{2,18},{10... | collective-permute-start | bytes 393224 | tf_op jit(solution)/shard_map/ppermute | solution.py:29
  4.6 0.1 collective-permute-start.4
  5.3 2.7 %shard_map.65 = (bf16[1,640,256]{2,1,0:T(8,128)(2,1)S(1)}, bf16[1,640,256]{2,1,0:T(8,128)(2,1)S(1)}, bf16[1,512,5120]{2,1,0:T(8,128)(2,1)S(1)}) custom-call(bf16[1,640,256]{2,1,0:T(8,128)(2,1)} %key_hbm.1, bf16[1,640,256]{2,1,0:T(8,128)(2,1)} %value_hbm.1, bf16[1,1024,5120]{2,1,0:T(8,128)(2,1)} %w_hbm.3), custom_call_target="tpu_custom_call" | custom-call | tf_op jit(solution)/shard_map/pallas_call | solution.py:247
  8.0 0.8 %collective-permute-done.2.query_ref = bf16[512,128]{1,0:T(8,128)(2,1)S(1)} collective-permute-done((bf16[512,128]{1,0:T(8,128)(2,1)S(1)}, bf16[512,128]{1,0:T(8,128)(2,1)S(1)}, u32[]{:S(2)}, u32[]{:S(2)}) %collective-permute-start.2) | collective-permute-done | bytes 131104 | tf_op jit(solution)/shard_map/ppermute | solution.py:29
  8.9 0.0 collective-permute-done.refs_3_.refs_1_
  8.9 0.0 collective-permute-done.1.refs_5_.refs_3_
  8.9 1.5 %shard_map.67 = bf16[544,128]{1,0:T(8,128)(2,1)S(1)} custom-call(s32[1]{0:T(128)S(6)} %copy.7.offset_ref, bf16[512,128]{1,0:T(8,128)(2,1)S(1)} %collective-permute-done.2.query_ref, bf16[1,640,256]{2,1,0:T(8,128)(2,1)S(1)} %get-tuple-element.26.refs_2_.refs_0_, bf16[1,640,256]{2,1,0:T(8,128)(2,1)S(1)} %collective-permute-done.refs_3_.refs_1_, ...), custom_call_target="tpu_custom_call" | custom-call | tf_op jit(solution)/shard_map/pallas_call | solution.py:262
  10.3 2.1 %collective-permute-start.3 = (bf16[544,128]{1,0:T(8,128)(2,1)S(1)}, bf16[544,128]{1,0:T(8,128)(2,1)S(1)}, u32[]{:S(2)}, u32[]{:S(2)}) collective-permute-start(bf16[544,128]{1,0:T(8,128)(2,1)S(1)} %shard_map.67), channel_id=1, source_target_pairs={{0,16},{8,24},{16,0},{24,8},{1,17},{9,25},{17,1},{25,9},{2,18},{10... | collective-permute-start | bytes 417800 | tf_op jit(solution)/shard_map/ppermute | solution.py:29
  12.5 0.0 collective-permute-done.4.query_ref
  12.5 1.4 %shard_map.69 = bf16[544,128]{1,0:T(8,128)(2,1)S(1)} custom-call(s32[1]{0:T(128)S(6)} %copy.7.offset_ref, bf16[512,128]{1,0:T(8,128)(2,1)S(1)} %collective-permute-done.4.query_ref, bf16[1,640,256]{2,1,0:T(8,128)(2,1)S(1)} %get-tuple-element.26.refs_2_.refs_0_, bf16[1,640,256]{2,1,0:T(8,128)(2,1)S(1)} %collective-permute-done.refs_3_.refs_1_, ...), custom_call_target="tpu_custom_call" | custom-call | tf_op jit(solution)/shard_map/pallas_call | solution.py:262
  13.9 0.4 collective-permute-start.5
  14.3 2.6 %shard_map.66 = (f32[2,512,128]{2,1,0:T(8,128)S(1)}, f32[2,512,128]{2,1,0:T(8,128)S(1)}, bf16[1,512,5120]{2,1,0:T(8,128)(2,1)S(1)}) custom-call(s32[1]{0:T(128)S(6)} %copy.7.offset_ref, bf16[1,1024,5120]{2,1,0:T(8,128)(2,1)} %w_hbm.3, bf16[512,128]{1,0:T(8,128)(2,1)S(1)} %get-tuple-element.24.refs_0_, bf16[512,128]{1,0:T(8,128)(2,1)S(1)} %get-tuple-element.25.refs_1_, ...), custom_call_target="tpu_custom_call" | custom-call | tf_op jit(solution)/shard_map/pallas_call | solution.py:270
  16.8 0.0 collective-permute-done.3.far_ref
  16.9 0.0 copy-start
  16.9 0.9 %shard_map.68 = (bf16[128,512]{1,0:T(8,128)(2,1)S(1)}, f32[1,128,1024]{2,1,0:T(8,128)S(1)}) custom-call(f32[2,512,128]{2,1,0:T(8,128)S(1)} %get-tuple-element.28.near_ref, f32[2,512,128]{2,1,0:T(8,128)S(1)} %get-tuple-element.29.log_ref, bf16[544,128]{1,0:T(8,128)(2,1)S(1)} %collective-permute-done.3.far_ref, ...), custom_call_target="tpu_custom_call" | custom-call | tf_op jit(solution)/shard_map/pallas_call | solution.py:288
  17.7 1.3 %collective-permute-done.5.far_ref = bf16[544,128]{1,0:T(8,128)(2,1)S(1)} collective-permute-done((bf16[544,128]{1,0:T(8,128)(2,1)S(1)}, bf16[544,128]{1,0:T(8,128)(2,1)S(1)}, u32[]{:S(2)}, u32[]{:S(2)}) %collective-permute-start.5) | collective-permute-done | bytes 139296 | tf_op jit(solution)/shard_map/ppermute | solution.py:29
  19.0 0.9 %shard_map.70 = (bf16[128,512]{1,0:T(8,128)(2,1)S(1)}, bf16[1,128,1024]{2,1,0:T(8,128)(2,1)S(1)}) custom-call(f32[2,512,128]{2,1,0:T(8,128)S(1)} %get-tuple-element.28.near_ref, f32[2,512,128]{2,1,0:T(8,128)S(1)} %get-tuple-element.29.log_ref, bf16[544,128]{1,0:T(8,128)(2,1)S(1)} %collective-permute-done.5.far_ref, ...), custom_call_target="tpu_custom_call" | custom-call | tf_op jit(solution)/shard_map/pallas_call | solution.py:288
  19.9 1.6 %collective-permute-start.7 = (bf16[1,128,1024]{2,1,0:T(8,128)(2,1)S(1)}, bf16[1,128,1024]{2,1,0:T(8,128)(2,1)S(1)}, u32[]{:S(2)}, u32[]{:S(2)}) collective-permute-start(bf16[1,128,1024]{2,1,0:T(8,128)(2,1)S(1)} %get-tuple-element.37), channel_id=1, source_target_pairs={{0,1},{1,0},{2,3},{3,2},{4,5},{5,4},{6,7},{7,6},{8,9},{9,8},{10,11... | collective-permute-start | bytes 786440 | tf_op jit(solution)/shard_map/ppermute | solution.py:29
  21.5 0.0 copy-done
  21.5 0.5 shard_map.71
  22.0 1.5 %collective-permute-start.6 = (bf16[128,1024]{1,0:T(8,128)(2,1)S(1)}, bf16[128,1024]{1,0:T(8,128)(2,1)S(1)}, u32[]{:S(2)}, u32[]{:S(2)}) collective-permute-start(bf16[128,1024]{1,0:T(8,128)(2,1)S(1)} %shard_map.71), channel_id=1, source_target_pairs={{0,4},{1,5},{2,6},{3,7},{4,0},{5,1},{6,2},{7,3},{8,12},{9,13},{10,... | collective-permute-start | bytes 786440 | tf_op jit(solution)/shard_map/ppermute | solution.py:35
  23.5 0.6 %shard_map.73 = (bf16[2,128,256]{2,1,0:T(8,128)(2,1)S(1)}, bf16[1,128,1024]{2,1,0:T(8,128)(2,1)S(1)}) custom-call(bf16[128,512]{1,0:T(8,128)(2,1)S(1)} %get-tuple-element.31.refs_0_, bf16[128,512]{1,0:T(8,128)(2,1)S(1)} %get-tuple-element.35.refs_1_, bf16[1,512,5120]{2,1,0:T(8,128)(2,1)S(1)} %get-tuple-element.30.w_ref.refs_2_, ...), custom_call_target="tpu_custom_call" | custom-call | flops 402653184 | tf_op jit(solution)/shard_map/pallas_call | solution.py:306
  24.1 0.6 %shard_map.72 = (bf16[1,128,1024]{2,1,0:T(8,128)(2,1)S(1)}, bf16[2,128,256]{2,1,0:T(8,128)(2,1)S(1)}) custom-call(bf16[128,512]{1,0:T(8,128)(2,1)S(1)} %get-tuple-element.31.refs_0_, bf16[128,512]{1,0:T(8,128)(2,1)S(1)} %get-tuple-element.35.refs_1_, bf16[1,512,5120]{2,1,0:T(8,128)(2,1)S(1)} %get-tuple-element.30.w_ref.refs_2_, ...), custom_call_target="tpu_custom_call" | custom-call | flops 402653184 | tf_op jit(solution)/shard_map/pallas_call | solution.py:306
  24.8 2.7 %collective-permute-start.10 = (bf16[2,128,256]{2,1,0:T(8,128)(2,1)S(1)}, bf16[2,128,256]{2,1,0:T(8,128)(2,1)S(1)}, u32[]{:S(2)}, u32[]{:S(2)}) collective-permute-start(bf16[2,128,256]{2,1,0:T(8,128)(2,1)S(1)} %get-tuple-element.42), channel_id=1, source_target_pairs={{0,2},{1,3},{2,0},{3,1},{4,6},{5,7},{6,4},{7,5},{8,10},{9,11},{10,... | collective-permute-start | bytes 393224 | tf_op jit(solution)/shard_map/ppermute | solution.py:29
  27.4 0.5 %collective-permute-start.8 = (bf16[128,1024]{1,0:T(8,128)(2,1)S(1)}, bf16[128,1024]{1,0:T(8,128)(2,1)S(1)}, u32[]{:S(2)}, u32[]{:S(2)}) collective-permute-start(bf16[128,1024]{1,0:T(8,128)(2,1)S(1)} %bitcast.8), channel_id=1, source_target_pairs={{0,5},{1,4},{2,7},{3,6},{4,1},{5,0},{6,3},{7,2},{8,13},{9,12},{10,... | collective-permute-start | bytes 786440 | tf_op jit(solution)/shard_map/ppermute | solution.py:35
  27.9 0.0 collective-permute-done.7
  27.9 0.1 fusion
  27.9 0.6 %collective-permute-done.6.refs_0_ = bf16[128,1024]{1,0:T(8,128)(2,1)S(1)} collective-permute-done((bf16[128,1024]{1,0:T(8,128)(2,1)S(1)}, bf16[128,1024]{1,0:T(8,128)(2,1)S(1)}, u32[]{:S(2)}, u32[]{:S(2)}) %collective-permute-start.6) | collective-permute-done | bytes 262176 | tf_op jit(solution)/shard_map/ppermute | solution.py:35
  28.6 8.5 %collective-permute-start.9 = (bf16[128,1024]{1,0:T(8,128)(2,1)S(1)}, bf16[128,1024]{1,0:T(8,128)(2,1)S(1)}, u32[]{:S(2)}, u32[]{:S(2)}) collective-permute-start(bf16[128,1024]{1,0:T(8,128)(2,1)S(1)} %fusion), channel_id=1, source_target_pairs={{0,6},{1,7},{2,4},{3,5},{4,2},{5,3},{6,0},{7,1},{8,14},{9,15},{10,... | collective-permute-start | bytes 786440 | tf_op jit(solution)/shard_map/ppermute | solution.py:35
  37.1 0.0 collective-permute-done.10
  37.1 1.2 %collective-permute-start.12 = (bf16[128,256]{1,0:T(8,128)(2,1)S(1)}, bf16[128,256]{1,0:T(8,128)(2,1)S(1)}, u32[]{:S(2)}, u32[]{:S(2)}) collective-permute-start(bf16[128,256]{1,0:T(8,128)(2,1)S(1)} %get-tuple-element.43), channel_id=1, source_target_pairs={{0,5},{1,4},{2,7},{3,6},{4,1},{5,0},{6,3},{7,2},{8,13},{9,12},{10,... | collective-permute-start | bytes 196616 | tf_op jit(solution)/shard_map/ppermute | solution.py:35
  38.3 3.0 %collective-permute-start.11 = (bf16[128,256]{1,0:T(8,128)(2,1)S(1)}, bf16[128,256]{1,0:T(8,128)(2,1)S(1)}, u32[]{:S(2)}, u32[]{:S(2)}) collective-permute-start(bf16[128,256]{1,0:T(8,128)(2,1)S(1)} %get-tuple-element.44), channel_id=1, source_target_pairs={{0,4},{1,5},{2,6},{3,7},{4,0},{5,1},{6,2},{7,3},{8,12},{9,13},{10,... | collective-permute-start | bytes 196616 | tf_op jit(solution)/shard_map/ppermute | solution.py:35
  41.3 1.2 %collective-permute-done.12.refs_4_ = bf16[128,256]{1,0:T(8,128)(2,1)S(1)} collective-permute-done((bf16[128,256]{1,0:T(8,128)(2,1)S(1)}, bf16[128,256]{1,0:T(8,128)(2,1)S(1)}, u32[]{:S(2)}, u32[]{:S(2)}) %collective-permute-start.12) | collective-permute-done | bytes 65568 | tf_op jit(solution)/shard_map/ppermute | solution.py:35
  42.5 1.0 %collective-permute-done.11.refs_3_ = bf16[128,256]{1,0:T(8,128)(2,1)S(1)} collective-permute-done((bf16[128,256]{1,0:T(8,128)(2,1)S(1)}, bf16[128,256]{1,0:T(8,128)(2,1)S(1)}, u32[]{:S(2)}, u32[]{:S(2)}) %collective-permute-start.11) | collective-permute-done | bytes 65568 | tf_op jit(solution)/shard_map/ppermute | solution.py:35
  43.5 0.0 collective-permute-done.8.refs_1_
  43.5 1.7 %collective-permute-done.9.refs_2_ = bf16[128,1024]{1,0:T(8,128)(2,1)S(1)} collective-permute-done((bf16[128,1024]{1,0:T(8,128)(2,1)S(1)}, bf16[128,1024]{1,0:T(8,128)(2,1)S(1)}, u32[]{:S(2)}, u32[]{:S(2)}) %collective-permute-start.9) | collective-permute-done | bytes 262176 | tf_op jit(solution)/shard_map/ppermute | solution.py:35
  45.3 0.8 %shard_map.74 = bf16[128,1280]{1,0:T(8,128)(2,1)} custom-call(bf16[128,1024]{1,0:T(8,128)(2,1)S(1)} %collective-permute-done.6.refs_0_, bf16[128,1024]{1,0:T(8,128)(2,1)S(1)} %collective-permute-done.8.refs_1_, bf16[128,1024]{1,0:T(8,128)(2,1)S(1)} %collective-permute-done.9.refs_2_, bf16[128,256]{1,0:T(8,128)(2,1)S(1)} %collective-permute-done.11.refs_3_, ...), custom_call_target="tpu_custom_call" | custom-call | tf_op jit(solution)/shard_map/pallas_call | solution.py:344
  (1 shorter events, 0.0 us)
Async XLA Ops:
  0.0 8.9 %collective-permute-start = (bf16[1,640,256]{2,1,0:T(8,128)(2,1)}, bf16[1,640,256]{2,1,0:T(8,128)(2,1)S(1)}, u32[]{:S(2)}, u32[]{:S(2)}) collective-permute-start(bf16[1,640,256]{2,1,0:T(8,128)(2,1)} %key_hbm.1), channel_id=1, source_target_pairs={{0,8},{8,0},{16,24},{24,16},{1,9},{9,1},{17,25},{25,17},{2,10},{10... | collective-permute-start | bytes 983048 | tf_op jit(solution)/shard_map/ppermute | solution.py:29
  0.5 8.4 %collective-permute-start.1 = (bf16[1,640,256]{2,1,0:T(8,128)(2,1)}, bf16[1,640,256]{2,1,0:T(8,128)(2,1)S(1)}, u32[]{:S(2)}, u32[]{:S(2)}) collective-permute-start(bf16[1,640,256]{2,1,0:T(8,128)(2,1)} %value_hbm.1), channel_id=1, source_target_pairs={{0,8},{8,0},{16,24},{24,16},{1,9},{9,1},{17,25},{25,17},{2,10},{10... | collective-permute-start | bytes 983048 | tf_op jit(solution)/shard_map/ppermute | solution.py:29
  1.5 7.3 %collective-permute-start.2 = (bf16[512,128]{1,0:T(8,128)(2,1)S(1)}, bf16[512,128]{1,0:T(8,128)(2,1)S(1)}, u32[]{:S(2)}, u32[]{:S(2)}) collective-permute-start(bf16[512,128]{1,0:T(8,128)(2,1)S(1)} %get-tuple-element.24.refs_0_), channel_id=1, source_target_pairs={{0,16},{8,24},{16,0},{24,8},{1,17},{9,25},{17,1},{25,9},{2,18},{10... | collective-permute-start | bytes 393224 | tf_op jit(solution)/shard_map/ppermute | solution.py:29
  4.6 7.9 %collective-permute-start.4 = (bf16[512,128]{1,0:T(8,128)(2,1)S(1)}, bf16[512,128]{1,0:T(8,128)(2,1)S(1)}, u32[]{:S(2)}, u32[]{:S(2)}) collective-permute-start(bf16[512,128]{1,0:T(8,128)(2,1)S(1)} %get-tuple-element.25.refs_1_), channel_id=1, source_target_pairs={{0,16},{8,24},{16,0},{24,8},{1,17},{9,25},{17,1},{25,9},{2,18},{10... | collective-permute-start | bytes 393224 | tf_op jit(solution)/shard_map/ppermute | solution.py:29
  10.3 6.5 %collective-permute-start.3 = (bf16[544,128]{1,0:T(8,128)(2,1)S(1)}, bf16[544,128]{1,0:T(8,128)(2,1)S(1)}, u32[]{:S(2)}, u32[]{:S(2)}) collective-permute-start(bf16[544,128]{1,0:T(8,128)(2,1)S(1)} %shard_map.67), channel_id=1, source_target_pairs={{0,16},{8,24},{16,0},{24,8},{1,17},{9,25},{17,1},{25,9},{2,18},{10... | collective-permute-start | bytes 417800 | tf_op jit(solution)/shard_map/ppermute | solution.py:29
  13.9 5.1 %collective-permute-start.5 = (bf16[544,128]{1,0:T(8,128)(2,1)S(1)}, bf16[544,128]{1,0:T(8,128)(2,1)S(1)}, u32[]{:S(2)}, u32[]{:S(2)}) collective-permute-start(bf16[544,128]{1,0:T(8,128)(2,1)S(1)} %shard_map.69), channel_id=1, source_target_pairs={{0,16},{8,24},{16,0},{24,8},{1,17},{9,25},{17,1},{25,9},{2,18},{10... | collective-permute-start | bytes 417800 | tf_op jit(solution)/shard_map/ppermute | solution.py:29
  16.9 4.7 %copy-start = (bf16[1,128,1280]{2,1,0:T(8,128)(2,1)S(1)}, bf16[1,128,1280]{2,1,0:T(8,128)(2,1)}, u32[]{:S(2)}) copy-start(bf16[1,128,1280]{2,1,0:T(8,128)(2,1)} %refs_4_.1) | copy-start | bytes 983044
  19.9 8.0 %collective-permute-start.7 = (bf16[1,128,1024]{2,1,0:T(8,128)(2,1)S(1)}, bf16[1,128,1024]{2,1,0:T(8,128)(2,1)S(1)}, u32[]{:S(2)}, u32[]{:S(2)}) collective-permute-start(bf16[1,128,1024]{2,1,0:T(8,128)(2,1)S(1)} %get-tuple-element.37), channel_id=1, source_target_pairs={{0,1},{1,0},{2,3},{3,2},{4,5},{5,4},{6,7},{7,6},{8,9},{9,8},{10,11... | collective-permute-start | bytes 786440 | tf_op jit(solution)/shard_map/ppermute | solution.py:29
  22.0 6.6 %collective-permute-start.6 = (bf16[128,1024]{1,0:T(8,128)(2,1)S(1)}, bf16[128,1024]{1,0:T(8,128)(2,1)S(1)}, u32[]{:S(2)}, u32[]{:S(2)}) collective-permute-start(bf16[128,1024]{1,0:T(8,128)(2,1)S(1)} %shard_map.71), channel_id=1, source_target_pairs={{0,4},{1,5},{2,6},{3,7},{4,0},{5,1},{6,2},{7,3},{8,12},{9,13},{10,... | collective-permute-start | bytes 786440 | tf_op jit(solution)/shard_map/ppermute | solution.py:35
  24.8 12.3 %collective-permute-start.10 = (bf16[2,128,256]{2,1,0:T(8,128)(2,1)S(1)}, bf16[2,128,256]{2,1,0:T(8,128)(2,1)S(1)}, u32[]{:S(2)}, u32[]{:S(2)}) collective-permute-start(bf16[2,128,256]{2,1,0:T(8,128)(2,1)S(1)} %get-tuple-element.42), channel_id=1, source_target_pairs={{0,2},{1,3},{2,0},{3,1},{4,6},{5,7},{6,4},{7,5},{8,10},{9,11},{10,... | collective-permute-start | bytes 393224 | tf_op jit(solution)/shard_map/ppermute | solution.py:29
  27.4 16.1 %collective-permute-start.8 = (bf16[128,1024]{1,0:T(8,128)(2,1)S(1)}, bf16[128,1024]{1,0:T(8,128)(2,1)S(1)}, u32[]{:S(2)}, u32[]{:S(2)}) collective-permute-start(bf16[128,1024]{1,0:T(8,128)(2,1)S(1)} %bitcast.8), channel_id=1, source_target_pairs={{0,5},{1,4},{2,7},{3,6},{4,1},{5,0},{6,3},{7,2},{8,13},{9,12},{10,... | collective-permute-start | bytes 786440 | tf_op jit(solution)/shard_map/ppermute | solution.py:35
  28.6 16.7 %collective-permute-start.9 = (bf16[128,1024]{1,0:T(8,128)(2,1)S(1)}, bf16[128,1024]{1,0:T(8,128)(2,1)S(1)}, u32[]{:S(2)}, u32[]{:S(2)}) collective-permute-start(bf16[128,1024]{1,0:T(8,128)(2,1)S(1)} %fusion), channel_id=1, source_target_pairs={{0,6},{1,7},{2,4},{3,5},{4,2},{5,3},{6,0},{7,1},{8,14},{9,15},{10,... | collective-permute-start | bytes 786440 | tf_op jit(solution)/shard_map/ppermute | solution.py:35
  37.1 5.4 %collective-permute-start.12 = (bf16[128,256]{1,0:T(8,128)(2,1)S(1)}, bf16[128,256]{1,0:T(8,128)(2,1)S(1)}, u32[]{:S(2)}, u32[]{:S(2)}) collective-permute-start(bf16[128,256]{1,0:T(8,128)(2,1)S(1)} %get-tuple-element.43), channel_id=1, source_target_pairs={{0,5},{1,4},{2,7},{3,6},{4,1},{5,0},{6,3},{7,2},{8,13},{9,12},{10,... | collective-permute-start | bytes 196616 | tf_op jit(solution)/shard_map/ppermute | solution.py:35
  38.3 5.2 %collective-permute-start.11 = (bf16[128,256]{1,0:T(8,128)(2,1)S(1)}, bf16[128,256]{1,0:T(8,128)(2,1)S(1)}, u32[]{:S(2)}, u32[]{:S(2)}) collective-permute-start(bf16[128,256]{1,0:T(8,128)(2,1)S(1)} %get-tuple-element.44), channel_id=1, source_target_pairs={{0,4},{1,5},{2,6},{3,7},{4,0},{5,1},{6,2},{7,3},{8,12},{9,13},{10,... | collective-permute-start | bytes 196616 | tf_op jit(solution)/shard_map/ppermute | solution.py:35

commit v6 on v5

--- a/solution.py
+++ b/solution.py
@@ -15,8 +15,8 @@
 MAX_FLOOR = -1e29
 EXP_SCALE = HD ** (-0.5) * math.log2(math.e)
 LOG2_E = math.log2(math.e)
-LOG_ROWS = 8
-LOG_SPACE = 32
+LOG_ROWS = G
+LOG_SPACE = 16
 MIB = 1 << 20
 
 WHOLE = pl.BlockSpec(memory_space=pltpu.VMEM)
@@ -59,9 +59,10 @@
 def masked_scores(query, key_ref, kv_head, bound):
     keys = key_ref[0, :, kv_head * HD : (kv_head + 1) * HD]
     scores = lax.dot_general(query, keys, (((1,), (1,)), ((), ())), preferred_element_type=jnp.float32)
-    rows = query.shape[0] // G
-    ahead = lax.broadcasted_iota(jnp.int32, scores.shape, 1) - lax.broadcasted_iota(jnp.int32, scores.shape, 0) % rows
-    return jnp.where(ahead <= bound, scores, NEG_FILL)
+    stacked, length = scores.shape
+    row = lax.rem(lax.broadcasted_iota(jnp.int32, (stacked, 1), 0), jnp.int32(stacked // G))
+    visible = lax.broadcasted_iota(jnp.int32, (1, length), 1) <= row + bound
+    return jnp.where(visible, scores, NEG_FILL)
 
 
 def attend(query, key_refs, value_refs, kv_head, bounds):
@@ -88,12 +89,12 @@
 
 
 def query_kernel(q_hbm, *refs):
-    *query_refs, q_ref, sem = refs
-    copy = pltpu.make_async_copy(q_hbm, q_ref, sem)
-    copy.start()
-    copy.wait()
-    for kv_head, query_ref in enumerate(query_refs):
-        query_ref[...] = stacked_query(q_ref, kv_head)
+    *query_refs, sems = refs
+    rows = q_hbm.shape[1]
+    heads = [(query_ref, g) for query_ref in query_refs for g in range(G)]
+    parts = [(q_hbm.at[0, :, pl.ds(h * HD, HD)], ref.at[pl.ds(g * rows, rows)]) for h, (ref, g) in enumerate(heads)]
+    for copy in copy_all(parts, sems):
+        copy.wait()
 
 
 def cache_kernel(key_hbm, value_hbm, w_hbm, key_ref, value_ref, w_ref, sems):
@@ -235,9 +236,8 @@
         [((stacked, HD), bf16)] * kv_local,
         16 * MIB,
         0,
-        [pltpu.VMEM(queries.shape, bf16), pltpu.SemaphoreType.DMA],
+        [pltpu.SemaphoreType.DMA((kv_local * G,))],
     )(in_hbm[0])
-    far_queries = [exchange(query, "ctx", top_bit) for query in own_queries]
     near = [(0, cache_keys, cache_values)]
     bit = top_bit // 2
     while bit:
@@ -252,6 +252,9 @@
         0,
         [pltpu.SemaphoreType.DMA((3,))],
     )(*in_hbm[1:])
+    sent_queries = list(own_queries)
+    sent_queries[1:], first_weight = lax.optimization_barrier((sent_queries[1:], first_weight))
+    far_queries = [exchange(query, "ctx", top_bit) for query in sent_queries]
     masks, near_keys, near_values = zip(*near)
     cached = [in_vmem(a) for a in (own_keys, *near_keys[1:], own_values, *near_values[1:])]
     far_results = []

time: 46.2 us -> 45.6 us (0.987)
  starting transfers between devices: 25.1 us -> 23.4 us
  waiting for transfers between devices: 6.77 us -> 7.74 us
    ppermute x8, waiting for transfers between devices: 2.15 us -> 3.77 us  [exchange(): return lax.ppermute(block, axis, route)]
    ppermute x5, starting transfers between devices: 14.7 us -> 13.7 us  [handed(): return lax.ppermute(block, ('section', 'tp'), route)]
    ppermute x8, starting transfers between devices: 10.4 us -> 9.71 us  [exchange(): return lax.ppermute(block, axis, route)]
    ppermute x5, waiting for transfers between devices: 4.63 us -> 3.97 us  [handed(): return lax.ppermute(block, ('section', 'tp'), route)]
  transfers between devices with their start and end apart: 13 -> 13, of which waited for: 6 -> 8; matrix products, arithmetic and copies ran while one was open for 0% -> 0% of each run, Pallas kernels for 25% -> 26%
where the time goes in v6:
time: 45.6 us; the launch traced here: 45.4 us
  starting transfers between devices  23.4 us (51%)
  Pallas kernels  13.3 us (29%)
  waiting for transfers between devices  7.74 us (17%)
  between operations  0.77 us (2%)
    ppermute x5, starting transfers between devices, handed(): return lax.ppermute(block, ('section', 'tp'), route)  13.7 us
    ppermute x8, starting transfers between devices, exchange(): return lax.ppermute(block, axis, route)  9.71 us
    ppermute x5, waiting for transfers between devices, handed(): return lax.ppermute(block, ('section', 'tp'), route)  3.97 us
    ppermute x8, waiting for transfers between devices, exchange(): return lax.ppermute(block, axis, route)  3.77 us
    pallas_call x2, Pallas kernels, on_device(): local_call(functools.partial(far_kernel, masks, top_bit, kv_head), [SCALA...  2.85 us
    pallas_call x1, Pallas kernels, on_device(): local_call(cache_kernel, [IN_HBM] * 3, [(cache_keys.shape, bf16), (cache_...  2.73 us
    pallas_call x1, Pallas kernels, on_device(): local_call(functools.partial(near_kernel, masks, kv_local), [SCALARS, IN_...  2.68 us
    pallas_call x2, Pallas kernels, on_device(): local_call(functools.partial(combine_kernel, kv_head, relay, block_width)...  1.67 us
  transfers between devices with their start and end apart: 13, of which 8 were waited for; matrix products, arithmetic and copies ran while one was open for 0% of the time, Pallas kernels for 26%

profile of v6, /device:TPU:0, one launch (start us, length us, event | category | flops | bytes accessed | tf_op | source)
XLA Modules:
  0.0 45.4 jit_solution(3866398120389250446)
XLA Ops:
  0.0 0.5 collective-permute-start
  0.5 0.1 collective-permute-start.1
  0.5 0.9 %shard_map.64 = (bf16[512,128]{1,0:T(8,128)(2,1)S(1)}, bf16[512,128]{1,0:T(8,128)(2,1)S(1)}) custom-call(bf16[1,128,1024]{2,1,0:T(8,128)(2,1)} %q_hbm.1), custom_call_target="tpu_custom_call" | custom-call | tf_op jit(solution)/shard_map/pallas_call | solution.py:233
  1.5 3.0 %collective-permute-start.2 = (bf16[512,128]{1,0:T(8,128)(2,1)S(1)}, bf16[512,128]{1,0:T(8,128)(2,1)S(1)}, u32[]{:S(2)}, u32[]{:S(2)}) collective-permute-start(bf16[512,128]{1,0:T(8,128)(2,1)S(1)} %get-tuple-element.26.refs_0_), channel_id=1, source_target_pairs={{0,16},{8,24},{16,0},{24,8},{1,17},{9,25},{17,1},{25,9},{2,18},{10... | collective-permute-start | bytes 393224 | tf_op jit(solution)/shard_map/ppermute | solution.py:29
  4.5 2.7 %shard_map.65 = (bf16[1,640,256]{2,1,0:T(8,128)(2,1)S(1)}, bf16[1,640,256]{2,1,0:T(8,128)(2,1)S(1)}, bf16[1,512,5120]{2,1,0:T(8,128)(2,1)S(1)}) custom-call(bf16[1,640,256]{2,1,0:T(8,128)(2,1)} %key_hbm.1, bf16[1,640,256]{2,1,0:T(8,128)(2,1)} %value_hbm.1, bf16[1,1024,5120]{2,1,0:T(8,128)(2,1)} %w_hbm.3), custom_call_target="tpu_custom_call" | custom-call | tf_op jit(solution)/shard_map/pallas_call | solution.py:247
  7.2 0.1 collective-permute-start.4
  8.0 0.2 collective-permute-done.2.query_ref
  8.2 0.0 collective-permute-done.refs_3_.refs_1_
  8.2 0.0 collective-permute-done.1.refs_5_.refs_3_
  8.2 1.4 %shard_map.67 = bf16[528,128]{1,0:T(8,128)(2,1)S(1)} custom-call(s32[1]{0:T(128)S(6)} %copy.7.offset_ref, bf16[512,128]{1,0:T(8,128)(2,1)S(1)} %collective-permute-done.2.query_ref, bf16[1,640,256]{2,1,0:T(8,128)(2,1)S(1)} %get-tuple-element.28.refs_2_.refs_0_, bf16[1,640,256]{2,1,0:T(8,128)(2,1)S(1)} %collective-permute-done.refs_3_.refs_1_, ...), custom_call_target="tpu_custom_call" | custom-call | tf_op jit(solution)/shard_map/pallas_call | solution.py:265
  9.6 1.9 %collective-permute-start.3 = (bf16[528,128]{1,0:T(8,128)(2,1)S(1)}, bf16[528,128]{1,0:T(8,128)(2,1)S(1)}, u32[]{:S(2)}, u32[]{:S(2)}) collective-permute-start(bf16[528,128]{1,0:T(8,128)(2,1)S(1)} %shard_map.67), channel_id=1, source_target_pairs={{0,16},{8,24},{16,0},{24,8},{1,17},{9,25},{17,1},{25,9},{2,18},{10... | collective-permute-start | bytes 405512 | tf_op jit(solution)/shard_map/ppermute | solution.py:29
  11.5 1.5 %collective-permute-done.4.query_ref = bf16[512,128]{1,0:T(8,128)(2,1)S(1)} collective-permute-done((bf16[512,128]{1,0:T(8,128)(2,1)S(1)}, bf16[512,128]{1,0:T(8,128)(2,1)S(1)}, u32[]{:S(2)}, u32[]{:S(2)}) %collective-permute-start.4) | collective-permute-done | bytes 131104 | tf_op jit(solution)/shard_map/ppermute | solution.py:29
  13.0 1.4 %shard_map.69 = bf16[528,128]{1,0:T(8,128)(2,1)S(1)} custom-call(s32[1]{0:T(128)S(6)} %copy.7.offset_ref, bf16[512,128]{1,0:T(8,128)(2,1)S(1)} %collective-permute-done.4.query_ref, bf16[1,640,256]{2,1,0:T(8,128)(2,1)S(1)} %get-tuple-element.28.refs_2_.refs_0_, bf16[1,640,256]{2,1,0:T(8,128)(2,1)S(1)} %collective-permute-done.refs_3_.refs_1_, ...), custom_call_target="tpu_custom_call" | custom-call | tf_op jit(solution)/shard_map/pallas_call | solution.py:265
  14.5 0.1 collective-permute-start.5
  14.5 2.7 %shard_map.66 = (f32[2,512,128]{2,1,0:T(8,128)S(1)}, f32[2,512,128]{2,1,0:T(8,128)S(1)}, bf16[1,512,5120]{2,1,0:T(8,128)(2,1)S(1)}) custom-call(s32[1]{0:T(128)S(6)} %copy.7.offset_ref, bf16[1,1024,5120]{2,1,0:T(8,128)(2,1)} %w_hbm.3, bf16[512,128]{1,0:T(8,128)(2,1)S(1)} %get-tuple-element.26.refs_0_, bf16[512,128]{1,0:T(8,128)(2,1)S(1)} %get-tuple-element.35.refs_1_, ...), custom_call_target="tpu_custom_call" | custom-call | tf_op jit(solution)/shard_map/pallas_call | solution.py:273
  17.2 0.0 collective-permute-done.3.far_ref
  17.2 0.0 copy-start
  17.2 0.8 %shard_map.68 = (bf16[128,512]{1,0:T(8,128)(2,1)S(1)}, f32[1,128,1024]{2,1,0:T(8,128)S(1)}) custom-call(f32[2,512,128]{2,1,0:T(8,128)S(1)} %get-tuple-element.30.near_ref, f32[2,512,128]{2,1,0:T(8,128)S(1)} %get-tuple-element.31.log_ref, bf16[528,128]{1,0:T(8,128)(2,1)S(1)} %collective-permute-done.3.far_ref, ...), custom_call_target="tpu_custom_call" | custom-call | tf_op jit(solution)/shard_map/pallas_call | solution.py:291
  18.1 1.4 %collective-permute-done.5.far_ref = bf16[528,128]{1,0:T(8,128)(2,1)S(1)} collective-permute-done((bf16[528,128]{1,0:T(8,128)(2,1)S(1)}, bf16[528,128]{1,0:T(8,128)(2,1)S(1)}, u32[]{:S(2)}, u32[]{:S(2)}) %collective-permute-start.5) | collective-permute-done | bytes 135200 | tf_op jit(solution)/shard_map/ppermute | solution.py:29
  19.5 0.8 %shard_map.70 = (bf16[128,512]{1,0:T(8,128)(2,1)S(1)}, bf16[1,128,1024]{2,1,0:T(8,128)(2,1)S(1)}) custom-call(f32[2,512,128]{2,1,0:T(8,128)S(1)} %get-tuple-element.30.near_ref, f32[2,512,128]{2,1,0:T(8,128)S(1)} %get-tuple-element.31.log_ref, bf16[528,128]{1,0:T(8,128)(2,1)S(1)} %collective-permute-done.5.far_ref, ...), custom_call_target="tpu_custom_call" | custom-call | tf_op jit(solution)/shard_map/pallas_call | solution.py:291
  20.4 1.4 %collective-permute-start.7 = (bf16[1,128,1024]{2,1,0:T(8,128)(2,1)S(1)}, bf16[1,128,1024]{2,1,0:T(8,128)(2,1)S(1)}, u32[]{:S(2)}, u32[]{:S(2)}) collective-permute-start(bf16[1,128,1024]{2,1,0:T(8,128)(2,1)S(1)} %get-tuple-element.41), channel_id=1, source_target_pairs={{0,1},{1,0},{2,3},{3,2},{4,5},{5,4},{6,7},{7,6},{8,9},{9,8},{10,11... | collective-permute-start | bytes 786440 | tf_op jit(solution)/shard_map/ppermute | solution.py:29
  21.8 0.0 copy-done
  21.8 0.5 %shard_map.71 = bf16[128,1024]{1,0:T(8,128)(2,1)S(1)} custom-call(bf16[128,512]{1,0:T(8,128)(2,1)S(1)} %get-tuple-element.34.refs_0_, bf16[128,512]{1,0:T(8,128)(2,1)S(1)} %get-tuple-element.39.refs_1_, bf16[1,512,5120]{2,1,0:T(8,128)(2,1)S(1)} %get-tuple-element.33.w_ref.refs_2_, bf16[1,512,5120]{2,1,0:T(8,128)(2,1)S(1)} %get-tuple-element.37.w_ref.refs_3_, ...), custom_call_target="tpu_custom_call" | custom-call | flops 268435456 | tf_op jit(solution)/shard_map/pallas_call | solution.py:300
  22.3 1.6 %collective-permute-start.6 = (bf16[128,1024]{1,0:T(8,128)(2,1)S(1)}, bf16[128,1024]{1,0:T(8,128)(2,1)S(1)}, u32[]{:S(2)}, u32[]{:S(2)}) collective-permute-start(bf16[128,1024]{1,0:T(8,128)(2,1)S(1)} %shard_map.71), channel_id=1, source_target_pairs={{0,4},{1,5},{2,6},{3,7},{4,0},{5,1},{6,2},{7,3},{8,12},{9,13},{10,... | collective-permute-start | bytes 786440 | tf_op jit(solution)/shard_map/ppermute | solution.py:35
  23.8 0.6 %shard_map.73 = (bf16[2,128,256]{2,1,0:T(8,128)(2,1)S(1)}, bf16[1,128,1024]{2,1,0:T(8,128)(2,1)S(1)}) custom-call(bf16[128,512]{1,0:T(8,128)(2,1)S(1)} %get-tuple-element.34.refs_0_, bf16[128,512]{1,0:T(8,128)(2,1)S(1)} %get-tuple-element.39.refs_1_, bf16[1,512,5120]{2,1,0:T(8,128)(2,1)S(1)} %get-tuple-element.33.w_ref.refs_2_, ...), custom_call_target="tpu_custom_call" | custom-call | flops 402653184 | tf_op jit(solution)/shard_map/pallas_call | solution.py:309
  24.4 0.6 %shard_map.72 = (bf16[1,128,1024]{2,1,0:T(8,128)(2,1)S(1)}, bf16[2,128,256]{2,1,0:T(8,128)(2,1)S(1)}) custom-call(bf16[128,512]{1,0:T(8,128)(2,1)S(1)} %get-tuple-element.34.refs_0_, bf16[128,512]{1,0:T(8,128)(2,1)S(1)} %get-tuple-element.39.refs_1_, bf16[1,512,5120]{2,1,0:T(8,128)(2,1)S(1)} %get-tuple-element.33.w_ref.refs_2_, ...), custom_call_target="tpu_custom_call" | custom-call | flops 402653184 | tf_op jit(solution)/shard_map/pallas_call | solution.py:309
  25.0 2.7 %collective-permute-start.10 = (bf16[2,128,256]{2,1,0:T(8,128)(2,1)S(1)}, bf16[2,128,256]{2,1,0:T(8,128)(2,1)S(1)}, u32[]{:S(2)}, u32[]{:S(2)}) collective-permute-start(bf16[2,128,256]{2,1,0:T(8,128)(2,1)S(1)} %get-tuple-element.46), channel_id=1, source_target_pairs={{0,2},{1,3},{2,0},{3,1},{4,6},{5,7},{6,4},{7,5},{8,10},{9,11},{10,... | collective-permute-start | bytes 393224 | tf_op jit(solution)/shard_map/ppermute | solution.py:29
  27.7 0.4 collective-permute-start.8
  28.1 0.6 %collective-permute-done.7 = bf16[1,128,1024]{2,1,0:T(8,128)(2,1)S(1)} collective-permute-done((bf16[1,128,1024]{2,1,0:T(8,128)(2,1)S(1)}, bf16[1,128,1024]{2,1,0:T(8,128)(2,1)S(1)}, u32[]{:S(2)}, u32[]{:S(2)}) %collective-permute-start.7) | collective-permute-done | bytes 262176 | tf_op jit(solution)/shard_map/ppermute | solution.py:29
  28.7 0.1 fusion
  28.8 0.7 %collective-permute-done.6.refs_0_ = bf16[128,1024]{1,0:T(8,128)(2,1)S(1)} collective-permute-done((bf16[128,1024]{1,0:T(8,128)(2,1)S(1)}, bf16[128,1024]{1,0:T(8,128)(2,1)S(1)}, u32[]{:S(2)}, u32[]{:S(2)}) %collective-permute-start.6) | collective-permute-done | bytes 262176 | tf_op jit(solution)/shard_map/ppermute | solution.py:35
  29.5 7.8 %collective-permute-start.9 = (bf16[128,1024]{1,0:T(8,128)(2,1)S(1)}, bf16[128,1024]{1,0:T(8,128)(2,1)S(1)}, u32[]{:S(2)}, u32[]{:S(2)}) collective-permute-start(bf16[128,1024]{1,0:T(8,128)(2,1)S(1)} %fusion), channel_id=1, source_target_pairs={{0,6},{1,7},{2,4},{3,5},{4,2},{5,3},{6,0},{7,1},{8,14},{9,15},{10,... | collective-permute-start | bytes 786440 | tf_op jit(solution)/shard_map/ppermute | solution.py:35
  37.3 0.0 collective-permute-done.10
  37.3 1.3 %collective-permute-start.12 = (bf16[128,256]{1,0:T(8,128)(2,1)S(1)}, bf16[128,256]{1,0:T(8,128)(2,1)S(1)}, u32[]{:S(2)}, u32[]{:S(2)}) collective-permute-start(bf16[128,256]{1,0:T(8,128)(2,1)S(1)} %get-tuple-element.47), channel_id=1, source_target_pairs={{0,5},{1,4},{2,7},{3,6},{4,1},{5,0},{6,3},{7,2},{8,13},{9,12},{10,... | collective-permute-start | bytes 196616 | tf_op jit(solution)/shard_map/ppermute | solution.py:35
  38.6 2.8 %collective-permute-start.11 = (bf16[128,256]{1,0:T(8,128)(2,1)S(1)}, bf16[128,256]{1,0:T(8,128)(2,1)S(1)}, u32[]{:S(2)}, u32[]{:S(2)}) collective-permute-start(bf16[128,256]{1,0:T(8,128)(2,1)S(1)} %get-tuple-element.48), channel_id=1, source_target_pairs={{0,4},{1,5},{2,6},{3,7},{4,0},{5,1},{6,2},{7,3},{8,12},{9,13},{10,... | collective-permute-start | bytes 196616 | tf_op jit(solution)/shard_map/ppermute | solution.py:35
  41.3 1.4 %collective-permute-done.12.refs_4_ = bf16[128,256]{1,0:T(8,128)(2,1)S(1)} collective-permute-done((bf16[128,256]{1,0:T(8,128)(2,1)S(1)}, bf16[128,256]{1,0:T(8,128)(2,1)S(1)}, u32[]{:S(2)}, u32[]{:S(2)}) %collective-permute-start.12) | collective-permute-done | bytes 65568 | tf_op jit(solution)/shard_map/ppermute | solution.py:35
  42.8 0.9 %collective-permute-done.11.refs_3_ = bf16[128,256]{1,0:T(8,128)(2,1)S(1)} collective-permute-done((bf16[128,256]{1,0:T(8,128)(2,1)S(1)}, bf16[128,256]{1,0:T(8,128)(2,1)S(1)}, u32[]{:S(2)}, u32[]{:S(2)}) %collective-permute-start.11) | collective-permute-done | bytes 65568 | tf_op jit(solution)/shard_map/ppermute | solution.py:35
  43.7 0.0 collective-permute-done.8.refs_1_
  43.7 0.9 %collective-permute-done.9.refs_2_ = bf16[128,1024]{1,0:T(8,128)(2,1)S(1)} collective-permute-done((bf16[128,1024]{1,0:T(8,128)(2,1)S(1)}, bf16[128,1024]{1,0:T(8,128)(2,1)S(1)}, u32[]{:S(2)}, u32[]{:S(2)}) %collective-permute-start.9) | collective-permute-done | bytes 262176 | tf_op jit(solution)/shard_map/ppermute | solution.py:35
  44.6 0.8 %shard_map.74 = bf16[128,1280]{1,0:T(8,128)(2,1)} custom-call(bf16[128,1024]{1,0:T(8,128)(2,1)S(1)} %collective-permute-done.6.refs_0_, bf16[128,1024]{1,0:T(8,128)(2,1)S(1)} %collective-permute-done.8.refs_1_, bf16[128,1024]{1,0:T(8,128)(2,1)S(1)} %collective-permute-done.9.refs_2_, bf16[128,256]{1,0:T(8,128)(2,1)S(1)} %collective-permute-done.11.refs_3_, ...), custom_call_target="tpu_custom_call" | custom-call | tf_op jit(solution)/shard_map/pallas_call | solution.py:347
  (1 shorter events, 0.0 us)
Async XLA Ops:
  0.0 8.2 %collective-permute-start = (bf16[1,640,256]{2,1,0:T(8,128)(2,1)}, bf16[1,640,256]{2,1,0:T(8,128)(2,1)S(1)}, u32[]{:S(2)}, u32[]{:S(2)}) collective-permute-start(bf16[1,640,256]{2,1,0:T(8,128)(2,1)} %key_hbm.1), channel_id=1, source_target_pairs={{0,8},{8,0},{16,24},{24,16},{1,9},{9,1},{17,25},{25,17},{2,10},{10... | collective-permute-start | bytes 983048 | tf_op jit(solution)/shard_map/ppermute | solution.py:29
  0.5 7.7 %collective-permute-start.1 = (bf16[1,640,256]{2,1,0:T(8,128)(2,1)}, bf16[1,640,256]{2,1,0:T(8,128)(2,1)S(1)}, u32[]{:S(2)}, u32[]{:S(2)}) collective-permute-start(bf16[1,640,256]{2,1,0:T(8,128)(2,1)} %value_hbm.1), channel_id=1, source_target_pairs={{0,8},{8,0},{16,24},{24,16},{1,9},{9,1},{17,25},{25,17},{2,10},{10... | collective-permute-start | bytes 983048 | tf_op jit(solution)/shard_map/ppermute | solution.py:29
  1.5 6.7 %collective-permute-start.2 = (bf16[512,128]{1,0:T(8,128)(2,1)S(1)}, bf16[512,128]{1,0:T(8,128)(2,1)S(1)}, u32[]{:S(2)}, u32[]{:S(2)}) collective-permute-start(bf16[512,128]{1,0:T(8,128)(2,1)S(1)} %get-tuple-element.26.refs_0_), channel_id=1, source_target_pairs={{0,16},{8,24},{16,0},{24,8},{1,17},{9,25},{17,1},{25,9},{2,18},{10... | collective-permute-start | bytes 393224 | tf_op jit(solution)/shard_map/ppermute | solution.py:29
  7.2 5.8 %collective-permute-start.4 = (bf16[512,128]{1,0:T(8,128)(2,1)S(1)}, bf16[512,128]{1,0:T(8,128)(2,1)S(1)}, u32[]{:S(2)}, u32[]{:S(2)}) collective-permute-start(bf16[512,128]{1,0:T(8,128)(2,1)S(1)} %get-tuple-element.35.refs_1_), channel_id=1, source_target_pairs={{0,16},{8,24},{16,0},{24,8},{1,17},{9,25},{17,1},{25,9},{2,18},{10... | collective-permute-start | bytes 393224 | tf_op jit(solution)/shard_map/ppermute | solution.py:29
  9.6 7.6 %collective-permute-start.3 = (bf16[528,128]{1,0:T(8,128)(2,1)S(1)}, bf16[528,128]{1,0:T(8,128)(2,1)S(1)}, u32[]{:S(2)}, u32[]{:S(2)}) collective-permute-start(bf16[528,128]{1,0:T(8,128)(2,1)S(1)} %shard_map.67), channel_id=1, source_target_pairs={{0,16},{8,24},{16,0},{24,8},{1,17},{9,25},{17,1},{25,9},{2,18},{10... | collective-permute-start | bytes 405512 | tf_op jit(solution)/shard_map/ppermute | solution.py:29
  14.5 5.1 %collective-permute-start.5 = (bf16[528,128]{1,0:T(8,128)(2,1)S(1)}, bf16[528,128]{1,0:T(8,128)(2,1)S(1)}, u32[]{:S(2)}, u32[]{:S(2)}) collective-permute-start(bf16[528,128]{1,0:T(8,128)(2,1)S(1)} %shard_map.69), channel_id=1, source_target_pairs={{0,16},{8,24},{16,0},{24,8},{1,17},{9,25},{17,1},{25,9},{2,18},{10... | collective-permute-start | bytes 405512 | tf_op jit(solution)/shard_map/ppermute | solution.py:29
  17.2 4.6 %copy-start = (bf16[1,128,1280]{2,1,0:T(8,128)(2,1)S(1)}, bf16[1,128,1280]{2,1,0:T(8,128)(2,1)}, u32[]{:S(2)}) copy-start(bf16[1,128,1280]{2,1,0:T(8,128)(2,1)} %refs_4_.1) | copy-start | bytes 983044
  20.4 8.3 %collective-permute-start.7 = (bf16[1,128,1024]{2,1,0:T(8,128)(2,1)S(1)}, bf16[1,128,1024]{2,1,0:T(8,128)(2,1)S(1)}, u32[]{:S(2)}, u32[]{:S(2)}) collective-permute-start(bf16[1,128,1024]{2,1,0:T(8,128)(2,1)S(1)} %get-tuple-element.41), channel_id=1, source_target_pairs={{0,1},{1,0},{2,3},{3,2},{4,5},{5,4},{6,7},{7,6},{8,9},{9,8},{10,11... | collective-permute-start | bytes 786440 | tf_op jit(solution)/shard_map/ppermute | solution.py:29
  22.3 7.2 %collective-permute-start.6 = (bf16[128,1024]{1,0:T(8,128)(2,1)S(1)}, bf16[128,1024]{1,0:T(8,128)(2,1)S(1)}, u32[]{:S(2)}, u32[]{:S(2)}) collective-permute-start(bf16[128,1024]{1,0:T(8,128)(2,1)S(1)} %shard_map.71), channel_id=1, source_target_pairs={{0,4},{1,5},{2,6},{3,7},{4,0},{5,1},{6,2},{7,3},{8,12},{9,13},{10,... | collective-permute-start | bytes 786440 | tf_op jit(solution)/shard_map/ppermute | solution.py:35
  25.0 12.2 %collective-permute-start.10 = (bf16[2,128,256]{2,1,0:T(8,128)(2,1)S(1)}, bf16[2,128,256]{2,1,0:T(8,128)(2,1)S(1)}, u32[]{:S(2)}, u32[]{:S(2)}) collective-permute-start(bf16[2,128,256]{2,1,0:T(8,128)(2,1)S(1)} %get-tuple-element.46), channel_id=1, source_target_pairs={{0,2},{1,3},{2,0},{3,1},{4,6},{5,7},{6,4},{7,5},{8,10},{9,11},{10,... | collective-permute-start | bytes 393224 | tf_op jit(solution)/shard_map/ppermute | solution.py:29
  27.7 16.0 %collective-permute-start.8 = (bf16[128,1024]{1,0:T(8,128)(2,1)S(1)}, bf16[128,1024]{1,0:T(8,128)(2,1)S(1)}, u32[]{:S(2)}, u32[]{:S(2)}) collective-permute-start(bf16[128,1024]{1,0:T(8,128)(2,1)S(1)} %bitcast.8), channel_id=1, source_target_pairs={{0,5},{1,4},{2,7},{3,6},{4,1},{5,0},{6,3},{7,2},{8,13},{9,12},{10,... | collective-permute-start | bytes 786440 | tf_op jit(solution)/shard_map/ppermute | solution.py:35
  29.5 15.1 %collective-permute-start.9 = (bf16[128,1024]{1,0:T(8,128)(2,1)S(1)}, bf16[128,1024]{1,0:T(8,128)(2,1)S(1)}, u32[]{:S(2)}, u32[]{:S(2)}) collective-permute-start(bf16[128,1024]{1,0:T(8,128)(2,1)S(1)} %fusion), channel_id=1, source_target_pairs={{0,6},{1,7},{2,4},{3,5},{4,2},{5,3},{6,0},{7,1},{8,14},{9,15},{10,... | collective-permute-start | bytes 786440 | tf_op jit(solution)/shard_map/ppermute | solution.py:35
  37.3 5.4 %collective-permute-start.12 = (bf16[128,256]{1,0:T(8,128)(2,1)S(1)}, bf16[128,256]{1,0:T(8,128)(2,1)S(1)}, u32[]{:S(2)}, u32[]{:S(2)}) collective-permute-start(bf16[128,256]{1,0:T(8,128)(2,1)S(1)} %get-tuple-element.47), channel_id=1, source_target_pairs={{0,5},{1,4},{2,7},{3,6},{4,1},{5,0},{6,3},{7,2},{8,13},{9,12},{10,... | collective-permute-start | bytes 196616 | tf_op jit(solution)/shard_map/ppermute | solution.py:35
  38.6 5.1 %collective-permute-start.11 = (bf16[128,256]{1,0:T(8,128)(2,1)S(1)}, bf16[128,256]{1,0:T(8,128)(2,1)S(1)}, u32[]{:S(2)}, u32[]{:S(2)}) collective-permute-start(bf16[128,256]{1,0:T(8,128)(2,1)S(1)} %get-tuple-element.48), channel_id=1, source_target_pairs={{0,4},{1,5},{2,6},{3,7},{4,0},{5,1},{6,2},{7,3},{8,12},{9,13},{10,... | collective-permute-start | bytes 196616 | tf_op jit(solution)/shard_map/ppermute | solution.py:35

commit v7 on v6

--- a/solution.py
+++ b/solution.py
@@ -217,7 +217,7 @@
 
 
 def cross_first_width(width):
-    return max(1, (2 * (width // LANES)) // 10) * LANES
+    return max(1, (3 * (width // LANES)) // 10) * LANES
 
 
 def on_device(row_offsets, queries, cache_keys, cache_values, residual, out_weight):

time: 45.6 us -> 45.4 us (level)
  starting transfers between devices: 23.4 us -> 21.6 us
  waiting for transfers between devices: 7.74 us -> 9.02 us
    ppermute x5, starting transfers between devices: 13.7 us -> 12 us  [handed(): return lax.ppermute(block, ('section', 'tp'), route)]
    ppermute x8, waiting for transfers between devices: 3.77 us -> 4.9 us  [exchange(): return lax.ppermute(block, axis, route)]
  transfers between devices with their start and end apart: 13 -> 13, of which waited for: 8 -> 8; matrix products, arithmetic and copies ran while one was open for 0% -> 0% of each run, Pallas kernels for 26% -> 27%
where the time goes in v7:
time: 45.4 us; the launch traced here: 45.2 us
  starting transfers between devices  21.6 us (48%)
  Pallas kernels  13.6 us (30%)
  waiting for transfers between devices  9.02 us (20%)
  between operations  0.78 us (2%)
    ppermute x5, starting transfers between devices, handed(): return lax.ppermute(block, ('section', 'tp'), route)  12 us
    ppermute x8, starting transfers between devices, exchange(): return lax.ppermute(block, axis, route)  9.66 us
    ppermute x8, waiting for transfers between devices, exchange(): return lax.ppermute(block, axis, route)  4.9 us
    ppermute x5, waiting for transfers between devices, handed(): return lax.ppermute(block, ('section', 'tp'), route)  4.12 us
    pallas_call x2, Pallas kernels, on_device(): local_call(functools.partial(far_kernel, masks, top_bit, kv_head), [SCALA...  2.86 us
    pallas_call x1, Pallas kernels, on_device(): local_call(cache_kernel, [IN_HBM] * 3, [(cache_keys.shape, bf16), (cache_...  2.73 us
    pallas_call x1, Pallas kernels, on_device(): local_call(functools.partial(near_kernel, masks, kv_local), [SCALARS, IN_...  2.69 us
    pallas_call x2, Pallas kernels, on_device(): local_call(functools.partial(combine_kernel, kv_head, relay, block_width)...  1.69 us
  transfers between devices with their start and end apart: 13, of which 8 were waited for; matrix products, arithmetic and copies ran while one was open for 0% of the time, Pallas kernels for 27%

profile of v7, /device:TPU:0, one launch (start us, length us, event | category | flops | bytes accessed | tf_op | source)
XLA Modules:
  0.0 45.2 jit_solution(8066843984761650195)
XLA Ops:
  0.0 0.5 %collective-permute-start = (bf16[1,640,256]{2,1,0:T(8,128)(2,1)}, bf16[1,640,256]{2,1,0:T(8,128)(2,1)S(1)}, u32[]{:S(2)}, u32[]{:S(2)}) collective-permute-start(bf16[1,640,256]{2,1,0:T(8,128)(2,1)} %key_hbm.1), channel_id=1, source_target_pairs={{0,8},{8,0},{16,24},{24,16},{1,9},{9,1},{17,25},{25,17},{2,10},{10... | collective-permute-start | bytes 983048 | tf_op jit(solution)/shard_map/ppermute | solution.py:29
  0.5 0.1 collective-permute-start.1
  0.5 0.9 %shard_map.64 = (bf16[512,128]{1,0:T(8,128)(2,1)S(1)}, bf16[512,128]{1,0:T(8,128)(2,1)S(1)}) custom-call(bf16[1,128,1024]{2,1,0:T(8,128)(2,1)} %q_hbm.1), custom_call_target="tpu_custom_call" | custom-call | tf_op jit(solution)/shard_map/pallas_call | solution.py:233
  1.5 3.0 %collective-permute-start.2 = (bf16[512,128]{1,0:T(8,128)(2,1)S(1)}, bf16[512,128]{1,0:T(8,128)(2,1)S(1)}, u32[]{:S(2)}, u32[]{:S(2)}) collective-permute-start(bf16[512,128]{1,0:T(8,128)(2,1)S(1)} %get-tuple-element.26.refs_0_), channel_id=1, source_target_pairs={{0,16},{8,24},{16,0},{24,8},{1,17},{9,25},{17,1},{25,9},{2,18},{10... | collective-permute-start | bytes 393224 | tf_op jit(solution)/shard_map/ppermute | solution.py:29
  4.5 2.7 %shard_map.65 = (bf16[1,640,256]{2,1,0:T(8,128)(2,1)S(1)}, bf16[1,640,256]{2,1,0:T(8,128)(2,1)S(1)}, bf16[1,512,5120]{2,1,0:T(8,128)(2,1)S(1)}) custom-call(bf16[1,640,256]{2,1,0:T(8,128)(2,1)} %key_hbm.1, bf16[1,640,256]{2,1,0:T(8,128)(2,1)} %value_hbm.1, bf16[1,1024,5120]{2,1,0:T(8,128)(2,1)} %w_hbm.3), custom_call_target="tpu_custom_call" | custom-call | tf_op jit(solution)/shard_map/pallas_call | solution.py:247
  7.2 0.1 collective-permute-start.4
  8.0 0.2 collective-permute-done.2.query_ref
  8.2 0.0 collective-permute-done.refs_3_.refs_1_
  8.2 0.0 collective-permute-done.1.refs_5_.refs_3_
  8.2 1.4 %shard_map.67 = bf16[528,128]{1,0:T(8,128)(2,1)S(1)} custom-call(s32[1]{0:T(128)S(6)} %copy.7.offset_ref, bf16[512,128]{1,0:T(8,128)(2,1)S(1)} %collective-permute-done.2.query_ref, bf16[1,640,256]{2,1,0:T(8,128)(2,1)S(1)} %get-tuple-element.28.refs_2_.refs_0_, bf16[1,640,256]{2,1,0:T(8,128)(2,1)S(1)} %collective-permute-done.refs_3_.refs_1_, ...), custom_call_target="tpu_custom_call" | custom-call | tf_op jit(solution)/shard_map/pallas_call | solution.py:265
  9.6 1.9 %collective-permute-start.3 = (bf16[528,128]{1,0:T(8,128)(2,1)S(1)}, bf16[528,128]{1,0:T(8,128)(2,1)S(1)}, u32[]{:S(2)}, u32[]{:S(2)}) collective-permute-start(bf16[528,128]{1,0:T(8,128)(2,1)S(1)} %shard_map.67), channel_id=1, source_target_pairs={{0,16},{8,24},{16,0},{24,8},{1,17},{9,25},{17,1},{25,9},{2,18},{10... | collective-permute-start | bytes 405512 | tf_op jit(solution)/shard_map/ppermute | solution.py:29
  11.5 1.5 %collective-permute-done.4.query_ref = bf16[512,128]{1,0:T(8,128)(2,1)S(1)} collective-permute-done((bf16[512,128]{1,0:T(8,128)(2,1)S(1)}, bf16[512,128]{1,0:T(8,128)(2,1)S(1)}, u32[]{:S(2)}, u32[]{:S(2)}) %collective-permute-start.4) | collective-permute-done | bytes 131104 | tf_op jit(solution)/shard_map/ppermute | solution.py:29
  13.0 1.4 %shard_map.69 = bf16[528,128]{1,0:T(8,128)(2,1)S(1)} custom-call(s32[1]{0:T(128)S(6)} %copy.7.offset_ref, bf16[512,128]{1,0:T(8,128)(2,1)S(1)} %collective-permute-done.4.query_ref, bf16[1,640,256]{2,1,0:T(8,128)(2,1)S(1)} %get-tuple-element.28.refs_2_.refs_0_, bf16[1,640,256]{2,1,0:T(8,128)(2,1)S(1)} %collective-permute-done.refs_3_.refs_1_, ...), custom_call_target="tpu_custom_call" | custom-call | tf_op jit(solution)/shard_map/pallas_call | solution.py:265
  14.5 0.1 collective-permute-start.5
  14.6 2.7 %shard_map.66 = (f32[2,512,128]{2,1,0:T(8,128)S(1)}, f32[2,512,128]{2,1,0:T(8,128)S(1)}, bf16[1,512,5120]{2,1,0:T(8,128)(2,1)S(1)}) custom-call(s32[1]{0:T(128)S(6)} %copy.7.offset_ref, bf16[1,1024,5120]{2,1,0:T(8,128)(2,1)} %w_hbm.3, bf16[512,128]{1,0:T(8,128)(2,1)S(1)} %get-tuple-element.26.refs_0_, bf16[512,128]{1,0:T(8,128)(2,1)S(1)} %get-tuple-element.35.refs_1_, ...), custom_call_target="tpu_custom_call" | custom-call | tf_op jit(solution)/shard_map/pallas_call | solution.py:273
  17.3 0.0 collective-permute-done.3.far_ref
  17.3 0.0 copy-start
  17.3 0.8 %shard_map.68 = (bf16[128,512]{1,0:T(8,128)(2,1)S(1)}, f32[1,128,896]{2,1,0:T(8,128)S(1)}) custom-call(f32[2,512,128]{2,1,0:T(8,128)S(1)} %get-tuple-element.30.near_ref, f32[2,512,128]{2,1,0:T(8,128)S(1)} %get-tuple-element.31.log_ref, bf16[528,128]{1,0:T(8,128)(2,1)S(1)} %collective-permute-done.3.far_ref, ...), custom_call_target="tpu_custom_call" | custom-call | tf_op jit(solution)/shard_map/pallas_call | solution.py:291
  18.1 1.4 %collective-permute-done.5.far_ref = bf16[528,128]{1,0:T(8,128)(2,1)S(1)} collective-permute-done((bf16[528,128]{1,0:T(8,128)(2,1)S(1)}, bf16[528,128]{1,0:T(8,128)(2,1)S(1)}, u32[]{:S(2)}, u32[]{:S(2)}) %collective-permute-start.5) | collective-permute-done | bytes 135200 | tf_op jit(solution)/shard_map/ppermute | solution.py:29
  19.5 0.8 %shard_map.70 = (bf16[128,512]{1,0:T(8,128)(2,1)S(1)}, bf16[1,128,896]{2,1,0:T(8,128)(2,1)S(1)}) custom-call(f32[2,512,128]{2,1,0:T(8,128)S(1)} %get-tuple-element.30.near_ref, f32[2,512,128]{2,1,0:T(8,128)S(1)} %get-tuple-element.31.log_ref, bf16[528,128]{1,0:T(8,128)(2,1)S(1)} %collective-permute-done.5.far_ref, ...), custom_call_target="tpu_custom_call" | custom-call | tf_op jit(solution)/shard_map/pallas_call | solution.py:291
  20.4 1.4 %collective-permute-start.7 = (bf16[1,128,896]{2,1,0:T(8,128)(2,1)S(1)}, bf16[1,128,896]{2,1,0:T(8,128)(2,1)S(1)}, u32[]{:S(2)}, u32[]{:S(2)}) collective-permute-start(bf16[1,128,896]{2,1,0:T(8,128)(2,1)S(1)} %get-tuple-element.41), channel_id=1, source_target_pairs={{0,1},{1,0},{2,3},{3,2},{4,5},{5,4},{6,7},{7,6},{8,9},{9,8},{10,11... | collective-permute-start | bytes 688136 | tf_op jit(solution)/shard_map/ppermute | solution.py:29
  21.8 0.0 copy-done
  21.8 0.5 %shard_map.71 = bf16[128,896]{1,0:T(8,128)(2,1)S(1)} custom-call(bf16[128,512]{1,0:T(8,128)(2,1)S(1)} %get-tuple-element.34.refs_0_, bf16[128,512]{1,0:T(8,128)(2,1)S(1)} %get-tuple-element.39.refs_1_, bf16[1,512,5120]{2,1,0:T(8,128)(2,1)S(1)} %get-tuple-element.33.w_ref.refs_2_, bf16[1,512,5120]{2,1,0:T(8,128)(2,1)S(1)} %get-tuple-element.37.w_ref.refs_3_, ...), custom_call_target="tpu_custom_call" | custom-call | flops 234881024 | tf_op jit(solution)/shard_map/pallas_call | solution.py:300
  22.3 1.6 %collective-permute-start.6 = (bf16[128,896]{1,0:T(8,128)(2,1)S(1)}, bf16[128,896]{1,0:T(8,128)(2,1)S(1)}, u32[]{:S(2)}, u32[]{:S(2)}) collective-permute-start(bf16[128,896]{1,0:T(8,128)(2,1)S(1)} %shard_map.71), channel_id=1, source_target_pairs={{0,4},{1,5},{2,6},{3,7},{4,0},{5,1},{6,2},{7,3},{8,12},{9,13},{10,... | collective-permute-start | bytes 688136 | tf_op jit(solution)/shard_map/ppermute | solution.py:35
  23.8 0.7 %shard_map.73 = (bf16[2,128,384]{2,1,0:T(8,128)(2,1)S(1)}, bf16[1,128,896]{2,1,0:T(8,128)(2,1)S(1)}) custom-call(bf16[128,512]{1,0:T(8,128)(2,1)S(1)} %get-tuple-element.34.refs_0_, bf16[128,512]{1,0:T(8,128)(2,1)S(1)} %get-tuple-element.39.refs_1_, bf16[1,512,5120]{2,1,0:T(8,128)(2,1)S(1)} %get-tuple-element.33.w_ref.refs_2_, ...), custom_call_target="tpu_custom_call" | custom-call | flops 436207616 | tf_op jit(solution)/shard_map/pallas_call | solution.py:309
  24.6 2.6 %collective-permute-start.10 = (bf16[2,128,384]{2,1,0:T(8,128)(2,1)S(1)}, bf16[2,128,384]{2,1,0:T(8,128)(2,1)S(1)}, u32[]{:S(2)}, u32[]{:S(2)}) collective-permute-start(bf16[2,128,384]{2,1,0:T(8,128)(2,1)S(1)} %get-tuple-element.46), channel_id=1, source_target_pairs={{0,2},{1,3},{2,0},{3,1},{4,6},{5,7},{6,4},{7,5},{8,10},{9,11},{10,... | collective-permute-start | bytes 589832 | tf_op jit(solution)/shard_map/ppermute | solution.py:29
  27.2 0.4 collective-permute-start.8
  27.6 0.7 %shard_map.72 = (bf16[1,128,896]{2,1,0:T(8,128)(2,1)S(1)}, bf16[2,128,384]{2,1,0:T(8,128)(2,1)S(1)}) custom-call(bf16[128,512]{1,0:T(8,128)(2,1)S(1)} %get-tuple-element.34.refs_0_, bf16[128,512]{1,0:T(8,128)(2,1)S(1)} %get-tuple-element.39.refs_1_, bf16[1,512,5120]{2,1,0:T(8,128)(2,1)S(1)} %get-tuple-element.33.w_ref.refs_2_, ...), custom_call_target="tpu_custom_call" | custom-call | flops 436207616 | tf_op jit(solution)/shard_map/pallas_call | solution.py:309
  28.4 0.0 collective-permute-done.7
  28.4 0.1 fusion
  28.5 0.3 collective-permute-done.6.refs_0_
  28.7 7.4 %collective-permute-start.9 = (bf16[128,896]{1,0:T(8,128)(2,1)S(1)}, bf16[128,896]{1,0:T(8,128)(2,1)S(1)}, u32[]{:S(2)}, u32[]{:S(2)}) collective-permute-start(bf16[128,896]{1,0:T(8,128)(2,1)S(1)} %fusion), channel_id=1, source_target_pairs={{0,6},{1,7},{2,4},{3,5},{4,2},{5,3},{6,0},{7,1},{8,14},{9,15},{10,... | collective-permute-start | bytes 688136 | tf_op jit(solution)/shard_map/ppermute | solution.py:35
  36.2 1.8 %collective-permute-done.10 = bf16[2,128,384]{2,1,0:T(8,128)(2,1)S(1)} collective-permute-done((bf16[2,128,384]{2,1,0:T(8,128)(2,1)S(1)}, bf16[2,128,384]{2,1,0:T(8,128)(2,1)S(1)}, u32[]{:S(2)}, u32[]{:S(2)}) %collective-permute-start.10) | collective-permute-done | bytes 196640 | tf_op jit(solution)/shard_map/ppermute | solution.py:29
  37.9 0.1 fusion.2
  38.0 0.7 %collective-permute-start.12 = (bf16[128,384]{1,0:T(8,128)(2,1)S(1)}, bf16[128,384]{1,0:T(8,128)(2,1)S(1)}, u32[]{:S(2)}, u32[]{:S(2)}) collective-permute-start(bf16[128,384]{1,0:T(8,128)(2,1)S(1)} %get-tuple-element.47), channel_id=1, source_target_pairs={{0,5},{1,4},{2,7},{3,6},{4,1},{5,0},{6,3},{7,2},{8,13},{9,12},{10,... | collective-permute-start | bytes 294920 | tf_op jit(solution)/shard_map/ppermute | solution.py:35
  38.7 1.9 %collective-permute-start.11 = (bf16[128,384]{1,0:T(8,128)(2,1)S(1)}, bf16[128,384]{1,0:T(8,128)(2,1)S(1)}, u32[]{:S(2)}, u32[]{:S(2)}) collective-permute-start(bf16[128,384]{1,0:T(8,128)(2,1)S(1)} %get-tuple-element.48), channel_id=1, source_target_pairs={{0,4},{1,5},{2,6},{3,7},{4,0},{5,1},{6,2},{7,3},{8,12},{9,13},{10,... | collective-permute-start | bytes 294920 | tf_op jit(solution)/shard_map/ppermute | solution.py:35
  40.5 1.6 %collective-permute-done.8.refs_1_ = bf16[128,896]{1,0:T(8,128)(2,1)S(1)} collective-permute-done((bf16[128,896]{1,0:T(8,128)(2,1)S(1)}, bf16[128,896]{1,0:T(8,128)(2,1)S(1)}, u32[]{:S(2)}, u32[]{:S(2)}) %collective-permute-start.8) | collective-permute-done | bytes 229408 | tf_op jit(solution)/shard_map/ppermute | solution.py:35
  42.1 1.5 %collective-permute-done.12.refs_4_ = bf16[128,384]{1,0:T(8,128)(2,1)S(1)} collective-permute-done((bf16[128,384]{1,0:T(8,128)(2,1)S(1)}, bf16[128,384]{1,0:T(8,128)(2,1)S(1)}, u32[]{:S(2)}, u32[]{:S(2)}) %collective-permute-start.12) | collective-permute-done | bytes 98336 | tf_op jit(solution)/shard_map/ppermute | solution.py:35
  43.6 0.8 %collective-permute-done.11.refs_3_ = bf16[128,384]{1,0:T(8,128)(2,1)S(1)} collective-permute-done((bf16[128,384]{1,0:T(8,128)(2,1)S(1)}, bf16[128,384]{1,0:T(8,128)(2,1)S(1)}, u32[]{:S(2)}, u32[]{:S(2)}) %collective-permute-start.11) | collective-permute-done | bytes 98336 | tf_op jit(solution)/shard_map/ppermute | solution.py:35
  44.4 0.0 collective-permute-done.9.refs_2_
  44.4 0.8 %shard_map.74 = bf16[128,1280]{1,0:T(8,128)(2,1)} custom-call(bf16[128,896]{1,0:T(8,128)(2,1)S(1)} %collective-permute-done.6.refs_0_, bf16[128,896]{1,0:T(8,128)(2,1)S(1)} %collective-permute-done.8.refs_1_, bf16[128,896]{1,0:T(8,128)(2,1)S(1)} %collective-permute-done.9.refs_2_, bf16[128,384]{1,0:T(8,128)(2,1)S(1)} %collective-permute-done.11.refs_3_, ...), custom_call_target="tpu_custom_call" | custom-call | tf_op jit(solution)/shard_map/pallas_call | solution.py:347
Async XLA Ops:
  0.0 8.2 %collective-permute-start = (bf16[1,640,256]{2,1,0:T(8,128)(2,1)}, bf16[1,640,256]{2,1,0:T(8,128)(2,1)S(1)}, u32[]{:S(2)}, u32[]{:S(2)}) collective-permute-start(bf16[1,640,256]{2,1,0:T(8,128)(2,1)} %key_hbm.1), channel_id=1, source_target_pairs={{0,8},{8,0},{16,24},{24,16},{1,9},{9,1},{17,25},{25,17},{2,10},{10... | collective-permute-start | bytes 983048 | tf_op jit(solution)/shard_map/ppermute | solution.py:29
  0.5 7.7 %collective-permute-start.1 = (bf16[1,640,256]{2,1,0:T(8,128)(2,1)}, bf16[1,640,256]{2,1,0:T(8,128)(2,1)S(1)}, u32[]{:S(2)}, u32[]{:S(2)}) collective-permute-start(bf16[1,640,256]{2,1,0:T(8,128)(2,1)} %value_hbm.1), channel_id=1, source_target_pairs={{0,8},{8,0},{16,24},{24,16},{1,9},{9,1},{17,25},{25,17},{2,10},{10... | collective-permute-start | bytes 983048 | tf_op jit(solution)/shard_map/ppermute | solution.py:29
  1.5 6.7 %collective-permute-start.2 = (bf16[512,128]{1,0:T(8,128)(2,1)S(1)}, bf16[512,128]{1,0:T(8,128)(2,1)S(1)}, u32[]{:S(2)}, u32[]{:S(2)}) collective-permute-start(bf16[512,128]{1,0:T(8,128)(2,1)S(1)} %get-tuple-element.26.refs_0_), channel_id=1, source_target_pairs={{0,16},{8,24},{16,0},{24,8},{1,17},{9,25},{17,1},{25,9},{2,18},{10... | collective-permute-start | bytes 393224 | tf_op jit(solution)/shard_map/ppermute | solution.py:29
  7.2 5.8 %collective-permute-start.4 = (bf16[512,128]{1,0:T(8,128)(2,1)S(1)}, bf16[512,128]{1,0:T(8,128)(2,1)S(1)}, u32[]{:S(2)}, u32[]{:S(2)}) collective-permute-start(bf16[512,128]{1,0:T(8,128)(2,1)S(1)} %get-tuple-element.35.refs_1_), channel_id=1, source_target_pairs={{0,16},{8,24},{16,0},{24,8},{1,17},{9,25},{17,1},{25,9},{2,18},{10... | collective-permute-start | bytes 393224 | tf_op jit(solution)/shard_map/ppermute | solution.py:29
  9.6 7.7 %collective-permute-start.3 = (bf16[528,128]{1,0:T(8,128)(2,1)S(1)}, bf16[528,128]{1,0:T(8,128)(2,1)S(1)}, u32[]{:S(2)}, u32[]{:S(2)}) collective-permute-start(bf16[528,128]{1,0:T(8,128)(2,1)S(1)} %shard_map.67), channel_id=1, source_target_pairs={{0,16},{8,24},{16,0},{24,8},{1,17},{9,25},{17,1},{25,9},{2,18},{10... | collective-permute-start | bytes 405512 | tf_op jit(solution)/shard_map/ppermute | solution.py:29
  14.5 5.1 %collective-permute-start.5 = (bf16[528,128]{1,0:T(8,128)(2,1)S(1)}, bf16[528,128]{1,0:T(8,128)(2,1)S(1)}, u32[]{:S(2)}, u32[]{:S(2)}) collective-permute-start(bf16[528,128]{1,0:T(8,128)(2,1)S(1)} %shard_map.69), channel_id=1, source_target_pairs={{0,16},{8,24},{16,0},{24,8},{1,17},{9,25},{17,1},{25,9},{2,18},{10... | collective-permute-start | bytes 405512 | tf_op jit(solution)/shard_map/ppermute | solution.py:29
  17.3 4.6 %copy-start = (bf16[1,128,1280]{2,1,0:T(8,128)(2,1)S(1)}, bf16[1,128,1280]{2,1,0:T(8,128)(2,1)}, u32[]{:S(2)}) copy-start(bf16[1,128,1280]{2,1,0:T(8,128)(2,1)} %refs_4_.1) | copy-start | bytes 983044
  20.4 8.0 %collective-permute-start.7 = (bf16[1,128,896]{2,1,0:T(8,128)(2,1)S(1)}, bf16[1,128,896]{2,1,0:T(8,128)(2,1)S(1)}, u32[]{:S(2)}, u32[]{:S(2)}) collective-permute-start(bf16[1,128,896]{2,1,0:T(8,128)(2,1)S(1)} %get-tuple-element.41), channel_id=1, source_target_pairs={{0,1},{1,0},{2,3},{3,2},{4,5},{5,4},{6,7},{7,6},{8,9},{9,8},{10,11... | collective-permute-start | bytes 688136 | tf_op jit(solution)/shard_map/ppermute | solution.py:29
  22.3 6.5 %collective-permute-start.6 = (bf16[128,896]{1,0:T(8,128)(2,1)S(1)}, bf16[128,896]{1,0:T(8,128)(2,1)S(1)}, u32[]{:S(2)}, u32[]{:S(2)}) collective-permute-start(bf16[128,896]{1,0:T(8,128)(2,1)S(1)} %shard_map.71), channel_id=1, source_target_pairs={{0,4},{1,5},{2,6},{3,7},{4,0},{5,1},{6,2},{7,3},{8,12},{9,13},{10,... | collective-permute-start | bytes 688136 | tf_op jit(solution)/shard_map/ppermute | solution.py:35
  24.6 13.3 %collective-permute-start.10 = (bf16[2,128,384]{2,1,0:T(8,128)(2,1)S(1)}, bf16[2,128,384]{2,1,0:T(8,128)(2,1)S(1)}, u32[]{:S(2)}, u32[]{:S(2)}) collective-permute-start(bf16[2,128,384]{2,1,0:T(8,128)(2,1)S(1)} %get-tuple-element.46), channel_id=1, source_target_pairs={{0,2},{1,3},{2,0},{3,1},{4,6},{5,7},{6,4},{7,5},{8,10},{9,11},{10,... | collective-permute-start | bytes 589832 | tf_op jit(solution)/shard_map/ppermute | solution.py:29
  27.2 14.9 %collective-permute-start.8 = (bf16[128,896]{1,0:T(8,128)(2,1)S(1)}, bf16[128,896]{1,0:T(8,128)(2,1)S(1)}, u32[]{:S(2)}, u32[]{:S(2)}) collective-permute-start(bf16[128,896]{1,0:T(8,128)(2,1)S(1)} %bitcast.8), channel_id=1, source_target_pairs={{0,5},{1,4},{2,7},{3,6},{4,1},{5,0},{6,3},{7,2},{8,13},{9,12},{10,... | collective-permute-start | bytes 688136 | tf_op jit(solution)/shard_map/ppermute | solution.py:35
  28.7 15.7 %collective-permute-start.9 = (bf16[128,896]{1,0:T(8,128)(2,1)S(1)}, bf16[128,896]{1,0:T(8,128)(2,1)S(1)}, u32[]{:S(2)}, u32[]{:S(2)}) collective-permute-start(bf16[128,896]{1,0:T(8,128)(2,1)S(1)} %fusion), channel_id=1, source_target_pairs={{0,6},{1,7},{2,4},{3,5},{4,2},{5,3},{6,0},{7,1},{8,14},{9,15},{10,... | collective-permute-start | bytes 688136 | tf_op jit(solution)/shard_map/ppermute | solution.py:35
  38.0 5.6 %collective-permute-start.12 = (bf16[128,384]{1,0:T(8,128)(2,1)S(1)}, bf16[128,384]{1,0:T(8,128)(2,1)S(1)}, u32[]{:S(2)}, u32[]{:S(2)}) collective-permute-start(bf16[128,384]{1,0:T(8,128)(2,1)S(1)} %get-tuple-element.47), channel_id=1, source_target_pairs={{0,5},{1,4},{2,7},{3,6},{4,1},{5,0},{6,3},{7,2},{8,13},{9,12},{10,... | collective-permute-start | bytes 294920 | tf_op jit(solution)/shard_map/ppermute | solution.py:35
  38.7 5.7 %collective-permute-start.11 = (bf16[128,384]{1,0:T(8,128)(2,1)S(1)}, bf16[128,384]{1,0:T(8,128)(2,1)S(1)}, u32[]{:S(2)}, u32[]{:S(2)}) collective-permute-start(bf16[128,384]{1,0:T(8,128)(2,1)S(1)} %get-tuple-element.48), channel_id=1, source_target_pairs={{0,4},{1,5},{2,6},{3,7},{4,0},{5,1},{6,2},{7,3},{8,12},{9,13},{10,... | collective-permute-start | bytes 294920 | tf_op jit(solution)/shard_map/ppermute | solution.py:35

commit v8 on v7

--- a/solution.py
+++ b/solution.py
@@ -49,11 +49,6 @@
         compiler_params=pltpu.CompilerParams(vmem_limit_bytes=limit),
         cost_estimate=pl.CostEstimate(flops=flops, bytes_accessed=0, transcendentals=0),
     )
-
-
-def stacked_query(q_ref, kv_head):
-    heads = range(kv_head * G, (kv_head + 1) * G)
-    return jnp.concatenate([q_ref[0, :, h * HD : (h + 1) * HD] for h in heads], axis=0)
 
 
 def masked_scores(query, key_ref, kv_head, bound):

time: 45.4 us -> 45.4 us (level)
  no operation moved by 1% of the time
where the time goes in v8:
time: 45.4 us; the launch traced here: 45.2 us
  starting transfers between devices  21.6 us (48%)
  Pallas kernels  13.6 us (30%)
  waiting for transfers between devices  9.02 us (20%)
  between operations  0.78 us (2%)
    ppermute x5, starting transfers between devices, handed(): return lax.ppermute(block, ('section', 'tp'), route)  12 us
    ppermute x8, starting transfers between devices, exchange(): return lax.ppermute(block, axis, route)  9.66 us
    ppermute x8, waiting for transfers between devices, exchange(): return lax.ppermute(block, axis, route)  4.9 us
    ppermute x5, waiting for transfers between devices, handed(): return lax.ppermute(block, ('section', 'tp'), route)  4.12 us
    pallas_call x2, Pallas kernels, on_device(): local_call(functools.partial(far_kernel, masks, top_bit, kv_head), [SCALA...  2.86 us
    pallas_call x1, Pallas kernels, on_device(): local_call(cache_kernel, [IN_HBM] * 3, [(cache_keys.shape, bf16), (cache_...  2.73 us
    pallas_call x1, Pallas kernels, on_device(): local_call(functools.partial(near_kernel, masks, kv_local), [SCALARS, IN_...  2.69 us
    pallas_call x2, Pallas kernels, on_device(): local_call(functools.partial(combine_kernel, kv_head, relay, block_width)...  1.69 us
  transfers between devices with their start and end apart: 13, of which 8 were waited for; matrix products, arithmetic and copies ran while one was open for 0% of the time, Pallas kernels for 27%

profile of v8, /device:TPU:0, one launch (start us, length us, event | category | flops | bytes accessed | tf_op | source)
XLA Modules:
  0.0 45.2 jit_solution(8066843984761650195)
XLA Ops:
  0.0 0.5 %collective-permute-start = (bf16[1,640,256]{2,1,0:T(8,128)(2,1)}, bf16[1,640,256]{2,1,0:T(8,128)(2,1)S(1)}, u32[]{:S(2)}, u32[]{:S(2)}) collective-permute-start(bf16[1,640,256]{2,1,0:T(8,128)(2,1)} %key_hbm.1), channel_id=1, source_target_pairs={{0,8},{8,0},{16,24},{24,16},{1,9},{9,1},{17,25},{25,17},{2,10},{10... | collective-permute-start | bytes 983048 | tf_op jit(solution)/shard_map/ppermute | solution.py:29
  0.5 0.1 collective-permute-start.1
  0.5 0.9 %shard_map.64 = (bf16[512,128]{1,0:T(8,128)(2,1)S(1)}, bf16[512,128]{1,0:T(8,128)(2,1)S(1)}) custom-call(bf16[1,128,1024]{2,1,0:T(8,128)(2,1)} %q_hbm.1), custom_call_target="tpu_custom_call" | custom-call | tf_op jit(solution)/shard_map/pallas_call | solution.py:228
  1.5 3.0 %collective-permute-start.2 = (bf16[512,128]{1,0:T(8,128)(2,1)S(1)}, bf16[512,128]{1,0:T(8,128)(2,1)S(1)}, u32[]{:S(2)}, u32[]{:S(2)}) collective-permute-start(bf16[512,128]{1,0:T(8,128)(2,1)S(1)} %get-tuple-element.26.refs_0_), channel_id=1, source_target_pairs={{0,16},{8,24},{16,0},{24,8},{1,17},{9,25},{17,1},{25,9},{2,18},{10... | collective-permute-start | bytes 393224 | tf_op jit(solution)/shard_map/ppermute | solution.py:29
  4.5 2.7 %shard_map.65 = (bf16[1,640,256]{2,1,0:T(8,128)(2,1)S(1)}, bf16[1,640,256]{2,1,0:T(8,128)(2,1)S(1)}, bf16[1,512,5120]{2,1,0:T(8,128)(2,1)S(1)}) custom-call(bf16[1,640,256]{2,1,0:T(8,128)(2,1)} %key_hbm.1, bf16[1,640,256]{2,1,0:T(8,128)(2,1)} %value_hbm.1, bf16[1,1024,5120]{2,1,0:T(8,128)(2,1)} %w_hbm.3), custom_call_target="tpu_custom_call" | custom-call | tf_op jit(solution)/shard_map/pallas_call | solution.py:242
  7.2 0.1 collective-permute-start.4
  8.0 0.2 collective-permute-done.2.query_ref
  8.2 0.0 collective-permute-done.refs_3_.refs_1_
  8.2 0.0 collective-permute-done.1.refs_5_.refs_3_
  8.2 1.4 %shard_map.67 = bf16[528,128]{1,0:T(8,128)(2,1)S(1)} custom-call(s32[1]{0:T(128)S(6)} %copy.7.offset_ref, bf16[512,128]{1,0:T(8,128)(2,1)S(1)} %collective-permute-done.2.query_ref, bf16[1,640,256]{2,1,0:T(8,128)(2,1)S(1)} %get-tuple-element.28.refs_2_.refs_0_, bf16[1,640,256]{2,1,0:T(8,128)(2,1)S(1)} %collective-permute-done.refs_3_.refs_1_, ...), custom_call_target="tpu_custom_call" | custom-call | tf_op jit(solution)/shard_map/pallas_call | solution.py:260
  9.6 1.9 %collective-permute-start.3 = (bf16[528,128]{1,0:T(8,128)(2,1)S(1)}, bf16[528,128]{1,0:T(8,128)(2,1)S(1)}, u32[]{:S(2)}, u32[]{:S(2)}) collective-permute-start(bf16[528,128]{1,0:T(8,128)(2,1)S(1)} %shard_map.67), channel_id=1, source_target_pairs={{0,16},{8,24},{16,0},{24,8},{1,17},{9,25},{17,1},{25,9},{2,18},{10... | collective-permute-start | bytes 405512 | tf_op jit(solution)/shard_map/ppermute | solution.py:29
  11.5 1.5 %collective-permute-done.4.query_ref = bf16[512,128]{1,0:T(8,128)(2,1)S(1)} collective-permute-done((bf16[512,128]{1,0:T(8,128)(2,1)S(1)}, bf16[512,128]{1,0:T(8,128)(2,1)S(1)}, u32[]{:S(2)}, u32[]{:S(2)}) %collective-permute-start.4) | collective-permute-done | bytes 131104 | tf_op jit(solution)/shard_map/ppermute | solution.py:29
  13.0 1.4 %shard_map.69 = bf16[528,128]{1,0:T(8,128)(2,1)S(1)} custom-call(s32[1]{0:T(128)S(6)} %copy.7.offset_ref, bf16[512,128]{1,0:T(8,128)(2,1)S(1)} %collective-permute-done.4.query_ref, bf16[1,640,256]{2,1,0:T(8,128)(2,1)S(1)} %get-tuple-element.28.refs_2_.refs_0_, bf16[1,640,256]{2,1,0:T(8,128)(2,1)S(1)} %collective-permute-done.refs_3_.refs_1_, ...), custom_call_target="tpu_custom_call" | custom-call | tf_op jit(solution)/shard_map/pallas_call | solution.py:260
  14.5 0.1 collective-permute-start.5
  14.6 2.7 %shard_map.66 = (f32[2,512,128]{2,1,0:T(8,128)S(1)}, f32[2,512,128]{2,1,0:T(8,128)S(1)}, bf16[1,512,5120]{2,1,0:T(8,128)(2,1)S(1)}) custom-call(s32[1]{0:T(128)S(6)} %copy.7.offset_ref, bf16[1,1024,5120]{2,1,0:T(8,128)(2,1)} %w_hbm.3, bf16[512,128]{1,0:T(8,128)(2,1)S(1)} %get-tuple-element.26.refs_0_, bf16[512,128]{1,0:T(8,128)(2,1)S(1)} %get-tuple-element.35.refs_1_, ...), custom_call_target="tpu_custom_call" | custom-call | tf_op jit(solution)/shard_map/pallas_call | solution.py:268
  17.3 0.0 collective-permute-done.3.far_ref
  17.3 0.0 copy-start
  17.3 0.8 %shard_map.68 = (bf16[128,512]{1,0:T(8,128)(2,1)S(1)}, f32[1,128,896]{2,1,0:T(8,128)S(1)}) custom-call(f32[2,512,128]{2,1,0:T(8,128)S(1)} %get-tuple-element.30.near_ref, f32[2,512,128]{2,1,0:T(8,128)S(1)} %get-tuple-element.31.log_ref, bf16[528,128]{1,0:T(8,128)(2,1)S(1)} %collective-permute-done.3.far_ref, ...), custom_call_target="tpu_custom_call" | custom-call | tf_op jit(solution)/shard_map/pallas_call | solution.py:286
  18.1 1.4 %collective-permute-done.5.far_ref = bf16[528,128]{1,0:T(8,128)(2,1)S(1)} collective-permute-done((bf16[528,128]{1,0:T(8,128)(2,1)S(1)}, bf16[528,128]{1,0:T(8,128)(2,1)S(1)}, u32[]{:S(2)}, u32[]{:S(2)}) %collective-permute-start.5) | collective-permute-done | bytes 135200 | tf_op jit(solution)/shard_map/ppermute | solution.py:29
  19.5 0.8 %shard_map.70 = (bf16[128,512]{1,0:T(8,128)(2,1)S(1)}, bf16[1,128,896]{2,1,0:T(8,128)(2,1)S(1)}) custom-call(f32[2,512,128]{2,1,0:T(8,128)S(1)} %get-tuple-element.30.near_ref, f32[2,512,128]{2,1,0:T(8,128)S(1)} %get-tuple-element.31.log_ref, bf16[528,128]{1,0:T(8,128)(2,1)S(1)} %collective-permute-done.5.far_ref, ...), custom_call_target="tpu_custom_call" | custom-call | tf_op jit(solution)/shard_map/pallas_call | solution.py:286
  20.4 1.4 %collective-permute-start.7 = (bf16[1,128,896]{2,1,0:T(8,128)(2,1)S(1)}, bf16[1,128,896]{2,1,0:T(8,128)(2,1)S(1)}, u32[]{:S(2)}, u32[]{:S(2)}) collective-permute-start(bf16[1,128,896]{2,1,0:T(8,128)(2,1)S(1)} %get-tuple-element.41), channel_id=1, source_target_pairs={{0,1},{1,0},{2,3},{3,2},{4,5},{5,4},{6,7},{7,6},{8,9},{9,8},{10,11... | collective-permute-start | bytes 688136 | tf_op jit(solution)/shard_map/ppermute | solution.py:29
  21.8 0.0 copy-done
  21.8 0.5 %shard_map.71 = bf16[128,896]{1,0:T(8,128)(2,1)S(1)} custom-call(bf16[128,512]{1,0:T(8,128)(2,1)S(1)} %get-tuple-element.34.refs_0_, bf16[128,512]{1,0:T(8,128)(2,1)S(1)} %get-tuple-element.39.refs_1_, bf16[1,512,5120]{2,1,0:T(8,128)(2,1)S(1)} %get-tuple-element.33.w_ref.refs_2_, bf16[1,512,5120]{2,1,0:T(8,128)(2,1)S(1)} %get-tuple-element.37.w_ref.refs_3_, ...), custom_call_target="tpu_custom_call" | custom-call | flops 234881024 | tf_op jit(solution)/shard_map/pallas_call | solution.py:295
  22.3 1.6 %collective-permute-start.6 = (bf16[128,896]{1,0:T(8,128)(2,1)S(1)}, bf16[128,896]{1,0:T(8,128)(2,1)S(1)}, u32[]{:S(2)}, u32[]{:S(2)}) collective-permute-start(bf16[128,896]{1,0:T(8,128)(2,1)S(1)} %shard_map.71), channel_id=1, source_target_pairs={{0,4},{1,5},{2,6},{3,7},{4,0},{5,1},{6,2},{7,3},{8,12},{9,13},{10,... | collective-permute-start | bytes 688136 | tf_op jit(solution)/shard_map/ppermute | solution.py:35
  23.8 0.7 %shard_map.73 = (bf16[2,128,384]{2,1,0:T(8,128)(2,1)S(1)}, bf16[1,128,896]{2,1,0:T(8,128)(2,1)S(1)}) custom-call(bf16[128,512]{1,0:T(8,128)(2,1)S(1)} %get-tuple-element.34.refs_0_, bf16[128,512]{1,0:T(8,128)(2,1)S(1)} %get-tuple-element.39.refs_1_, bf16[1,512,5120]{2,1,0:T(8,128)(2,1)S(1)} %get-tuple-element.33.w_ref.refs_2_, ...), custom_call_target="tpu_custom_call" | custom-call | flops 436207616 | tf_op jit(solution)/shard_map/pallas_call | solution.py:304
  24.6 2.6 %collective-permute-start.10 = (bf16[2,128,384]{2,1,0:T(8,128)(2,1)S(1)}, bf16[2,128,384]{2,1,0:T(8,128)(2,1)S(1)}, u32[]{:S(2)}, u32[]{:S(2)}) collective-permute-start(bf16[2,128,384]{2,1,0:T(8,128)(2,1)S(1)} %get-tuple-element.46), channel_id=1, source_target_pairs={{0,2},{1,3},{2,0},{3,1},{4,6},{5,7},{6,4},{7,5},{8,10},{9,11},{10,... | collective-permute-start | bytes 589832 | tf_op jit(solution)/shard_map/ppermute | solution.py:29
  27.2 0.4 collective-permute-start.8
  27.6 0.7 %shard_map.72 = (bf16[1,128,896]{2,1,0:T(8,128)(2,1)S(1)}, bf16[2,128,384]{2,1,0:T(8,128)(2,1)S(1)}) custom-call(bf16[128,512]{1,0:T(8,128)(2,1)S(1)} %get-tuple-element.34.refs_0_, bf16[128,512]{1,0:T(8,128)(2,1)S(1)} %get-tuple-element.39.refs_1_, bf16[1,512,5120]{2,1,0:T(8,128)(2,1)S(1)} %get-tuple-element.33.w_ref.refs_2_, ...), custom_call_target="tpu_custom_call" | custom-call | flops 436207616 | tf_op jit(solution)/shard_map/pallas_call | solution.py:304
  28.4 0.0 collective-permute-done.7
  28.4 0.1 fusion
  28.5 0.3 collective-permute-done.6.refs_0_
  28.7 7.4 %collective-permute-start.9 = (bf16[128,896]{1,0:T(8,128)(2,1)S(1)}, bf16[128,896]{1,0:T(8,128)(2,1)S(1)}, u32[]{:S(2)}, u32[]{:S(2)}) collective-permute-start(bf16[128,896]{1,0:T(8,128)(2,1)S(1)} %fusion), channel_id=1, source_target_pairs={{0,6},{1,7},{2,4},{3,5},{4,2},{5,3},{6,0},{7,1},{8,14},{9,15},{10,... | collective-permute-start | bytes 688136 | tf_op jit(solution)/shard_map/ppermute | solution.py:35
  36.2 1.8 %collective-permute-done.10 = bf16[2,128,384]{2,1,0:T(8,128)(2,1)S(1)} collective-permute-done((bf16[2,128,384]{2,1,0:T(8,128)(2,1)S(1)}, bf16[2,128,384]{2,1,0:T(8,128)(2,1)S(1)}, u32[]{:S(2)}, u32[]{:S(2)}) %collective-permute-start.10) | collective-permute-done | bytes 196640 | tf_op jit(solution)/shard_map/ppermute | solution.py:29
  37.9 0.1 fusion.2
  38.0 0.7 %collective-permute-start.12 = (bf16[128,384]{1,0:T(8,128)(2,1)S(1)}, bf16[128,384]{1,0:T(8,128)(2,1)S(1)}, u32[]{:S(2)}, u32[]{:S(2)}) collective-permute-start(bf16[128,384]{1,0:T(8,128)(2,1)S(1)} %get-tuple-element.47), channel_id=1, source_target_pairs={{0,5},{1,4},{2,7},{3,6},{4,1},{5,0},{6,3},{7,2},{8,13},{9,12},{10,... | collective-permute-start | bytes 294920 | tf_op jit(solution)/shard_map/ppermute | solution.py:35
  38.7 1.9 %collective-permute-start.11 = (bf16[128,384]{1,0:T(8,128)(2,1)S(1)}, bf16[128,384]{1,0:T(8,128)(2,1)S(1)}, u32[]{:S(2)}, u32[]{:S(2)}) collective-permute-start(bf16[128,384]{1,0:T(8,128)(2,1)S(1)} %get-tuple-element.48), channel_id=1, source_target_pairs={{0,4},{1,5},{2,6},{3,7},{4,0},{5,1},{6,2},{7,3},{8,12},{9,13},{10,... | collective-permute-start | bytes 294920 | tf_op jit(solution)/shard_map/ppermute | solution.py:35
  40.5 1.6 %collective-permute-done.8.refs_1_ = bf16[128,896]{1,0:T(8,128)(2,1)S(1)} collective-permute-done((bf16[128,896]{1,0:T(8,128)(2,1)S(1)}, bf16[128,896]{1,0:T(8,128)(2,1)S(1)}, u32[]{:S(2)}, u32[]{:S(2)}) %collective-permute-start.8) | collective-permute-done | bytes 229408 | tf_op jit(solution)/shard_map/ppermute | solution.py:35
  42.1 1.5 %collective-permute-done.12.refs_4_ = bf16[128,384]{1,0:T(8,128)(2,1)S(1)} collective-permute-done((bf16[128,384]{1,0:T(8,128)(2,1)S(1)}, bf16[128,384]{1,0:T(8,128)(2,1)S(1)}, u32[]{:S(2)}, u32[]{:S(2)}) %collective-permute-start.12) | collective-permute-done | bytes 98336 | tf_op jit(solution)/shard_map/ppermute | solution.py:35
  43.6 0.8 %collective-permute-done.11.refs_3_ = bf16[128,384]{1,0:T(8,128)(2,1)S(1)} collective-permute-done((bf16[128,384]{1,0:T(8,128)(2,1)S(1)}, bf16[128,384]{1,0:T(8,128)(2,1)S(1)}, u32[]{:S(2)}, u32[]{:S(2)}) %collective-permute-start.11) | collective-permute-done | bytes 98336 | tf_op jit(solution)/shard_map/ppermute | solution.py:35
  44.4 0.0 collective-permute-done.9.refs_2_
  44.4 0.8 %shard_map.74 = bf16[128,1280]{1,0:T(8,128)(2,1)} custom-call(bf16[128,896]{1,0:T(8,128)(2,1)S(1)} %collective-permute-done.6.refs_0_, bf16[128,896]{1,0:T(8,128)(2,1)S(1)} %collective-permute-done.8.refs_1_, bf16[128,896]{1,0:T(8,128)(2,1)S(1)} %collective-permute-done.9.refs_2_, bf16[128,384]{1,0:T(8,128)(2,1)S(1)} %collective-permute-done.11.refs_3_, ...), custom_call_target="tpu_custom_call" | custom-call | tf_op jit(solution)/shard_map/pallas_call | solution.py:342
Async XLA Ops:
  0.0 8.2 %collective-permute-start = (bf16[1,640,256]{2,1,0:T(8,128)(2,1)}, bf16[1,640,256]{2,1,0:T(8,128)(2,1)S(1)}, u32[]{:S(2)}, u32[]{:S(2)}) collective-permute-start(bf16[1,640,256]{2,1,0:T(8,128)(2,1)} %key_hbm.1), channel_id=1, source_target_pairs={{0,8},{8,0},{16,24},{24,16},{1,9},{9,1},{17,25},{25,17},{2,10},{10... | collective-permute-start | bytes 983048 | tf_op jit(solution)/shard_map/ppermute | solution.py:29
  0.5 7.7 %collective-permute-start.1 = (bf16[1,640,256]{2,1,0:T(8,128)(2,1)}, bf16[1,640,256]{2,1,0:T(8,128)(2,1)S(1)}, u32[]{:S(2)}, u32[]{:S(2)}) collective-permute-start(bf16[1,640,256]{2,1,0:T(8,128)(2,1)} %value_hbm.1), channel_id=1, source_target_pairs={{0,8},{8,0},{16,24},{24,16},{1,9},{9,1},{17,25},{25,17},{2,10},{10... | collective-permute-start | bytes 983048 | tf_op jit(solution)/shard_map/ppermute | solution.py:29
  1.5 6.7 %collective-permute-start.2 = (bf16[512,128]{1,0:T(8,128)(2,1)S(1)}, bf16[512,128]{1,0:T(8,128)(2,1)S(1)}, u32[]{:S(2)}, u32[]{:S(2)}) collective-permute-start(bf16[512,128]{1,0:T(8,128)(2,1)S(1)} %get-tuple-element.26.refs_0_), channel_id=1, source_target_pairs={{0,16},{8,24},{16,0},{24,8},{1,17},{9,25},{17,1},{25,9},{2,18},{10... | collective-permute-start | bytes 393224 | tf_op jit(solution)/shard_map/ppermute | solution.py:29
  7.2 5.8 %collective-permute-start.4 = (bf16[512,128]{1,0:T(8,128)(2,1)S(1)}, bf16[512,128]{1,0:T(8,128)(2,1)S(1)}, u32[]{:S(2)}, u32[]{:S(2)}) collective-permute-start(bf16[512,128]{1,0:T(8,128)(2,1)S(1)} %get-tuple-element.35.refs_1_), channel_id=1, source_target_pairs={{0,16},{8,24},{16,0},{24,8},{1,17},{9,25},{17,1},{25,9},{2,18},{10... | collective-permute-start | bytes 393224 | tf_op jit(solution)/shard_map/ppermute | solution.py:29
  9.6 7.7 %collective-permute-start.3 = (bf16[528,128]{1,0:T(8,128)(2,1)S(1)}, bf16[528,128]{1,0:T(8,128)(2,1)S(1)}, u32[]{:S(2)}, u32[]{:S(2)}) collective-permute-start(bf16[528,128]{1,0:T(8,128)(2,1)S(1)} %shard_map.67), channel_id=1, source_target_pairs={{0,16},{8,24},{16,0},{24,8},{1,17},{9,25},{17,1},{25,9},{2,18},{10... | collective-permute-start | bytes 405512 | tf_op jit(solution)/shard_map/ppermute | solution.py:29
  14.5 5.1 %collective-permute-start.5 = (bf16[528,128]{1,0:T(8,128)(2,1)S(1)}, bf16[528,128]{1,0:T(8,128)(2,1)S(1)}, u32[]{:S(2)}, u32[]{:S(2)}) collective-permute-start(bf16[528,128]{1,0:T(8,128)(2,1)S(1)} %shard_map.69), channel_id=1, source_target_pairs={{0,16},{8,24},{16,0},{24,8},{1,17},{9,25},{17,1},{25,9},{2,18},{10... | collective-permute-start | bytes 405512 | tf_op jit(solution)/shard_map/ppermute | solution.py:29
  17.3 4.6 %copy-start = (bf16[1,128,1280]{2,1,0:T(8,128)(2,1)S(1)}, bf16[1,128,1280]{2,1,0:T(8,128)(2,1)}, u32[]{:S(2)}) copy-start(bf16[1,128,1280]{2,1,0:T(8,128)(2,1)} %refs_4_.1) | copy-start | bytes 983044
  20.4 8.0 %collective-permute-start.7 = (bf16[1,128,896]{2,1,0:T(8,128)(2,1)S(1)}, bf16[1,128,896]{2,1,0:T(8,128)(2,1)S(1)}, u32[]{:S(2)}, u32[]{:S(2)}) collective-permute-start(bf16[1,128,896]{2,1,0:T(8,128)(2,1)S(1)} %get-tuple-element.41), channel_id=1, source_target_pairs={{0,1},{1,0},{2,3},{3,2},{4,5},{5,4},{6,7},{7,6},{8,9},{9,8},{10,11... | collective-permute-start | bytes 688136 | tf_op jit(solution)/shard_map/ppermute | solution.py:29
  22.3 6.5 %collective-permute-start.6 = (bf16[128,896]{1,0:T(8,128)(2,1)S(1)}, bf16[128,896]{1,0:T(8,128)(2,1)S(1)}, u32[]{:S(2)}, u32[]{:S(2)}) collective-permute-start(bf16[128,896]{1,0:T(8,128)(2,1)S(1)} %shard_map.71), channel_id=1, source_target_pairs={{0,4},{1,5},{2,6},{3,7},{4,0},{5,1},{6,2},{7,3},{8,12},{9,13},{10,... | collective-permute-start | bytes 688136 | tf_op jit(solution)/shard_map/ppermute | solution.py:35
  24.6 13.3 %collective-permute-start.10 = (bf16[2,128,384]{2,1,0:T(8,128)(2,1)S(1)}, bf16[2,128,384]{2,1,0:T(8,128)(2,1)S(1)}, u32[]{:S(2)}, u32[]{:S(2)}) collective-permute-start(bf16[2,128,384]{2,1,0:T(8,128)(2,1)S(1)} %get-tuple-element.46), channel_id=1, source_target_pairs={{0,2},{1,3},{2,0},{3,1},{4,6},{5,7},{6,4},{7,5},{8,10},{9,11},{10,... | collective-permute-start | bytes 589832 | tf_op jit(solution)/shard_map/ppermute | solution.py:29
  27.2 14.9 %collective-permute-start.8 = (bf16[128,896]{1,0:T(8,128)(2,1)S(1)}, bf16[128,896]{1,0:T(8,128)(2,1)S(1)}, u32[]{:S(2)}, u32[]{:S(2)}) collective-permute-start(bf16[128,896]{1,0:T(8,128)(2,1)S(1)} %bitcast.8), channel_id=1, source_target_pairs={{0,5},{1,4},{2,7},{3,6},{4,1},{5,0},{6,3},{7,2},{8,13},{9,12},{10,... | collective-permute-start | bytes 688136 | tf_op jit(solution)/shard_map/ppermute | solution.py:35
  28.7 15.7 %collective-permute-start.9 = (bf16[128,896]{1,0:T(8,128)(2,1)S(1)}, bf16[128,896]{1,0:T(8,128)(2,1)S(1)}, u32[]{:S(2)}, u32[]{:S(2)}) collective-permute-start(bf16[128,896]{1,0:T(8,128)(2,1)S(1)} %fusion), channel_id=1, source_target_pairs={{0,6},{1,7},{2,4},{3,5},{4,2},{5,3},{6,0},{7,1},{8,14},{9,15},{10,... | collective-permute-start | bytes 688136 | tf_op jit(solution)/shard_map/ppermute | solution.py:35
  38.0 5.6 %collective-permute-start.12 = (bf16[128,384]{1,0:T(8,128)(2,1)S(1)}, bf16[128,384]{1,0:T(8,128)(2,1)S(1)}, u32[]{:S(2)}, u32[]{:S(2)}) collective-permute-start(bf16[128,384]{1,0:T(8,128)(2,1)S(1)} %get-tuple-element.47), channel_id=1, source_target_pairs={{0,5},{1,4},{2,7},{3,6},{4,1},{5,0},{6,3},{7,2},{8,13},{9,12},{10,... | collective-permute-start | bytes 294920 | tf_op jit(solution)/shard_map/ppermute | solution.py:35
  38.7 5.7 %collective-permute-start.11 = (bf16[128,384]{1,0:T(8,128)(2,1)S(1)}, bf16[128,384]{1,0:T(8,128)(2,1)S(1)}, u32[]{:S(2)}, u32[]{:S(2)}) collective-permute-start(bf16[128,384]{1,0:T(8,128)(2,1)S(1)} %get-tuple-element.48), channel_id=1, source_target_pairs={{0,4},{1,5},{2,6},{3,7},{4,0},{5,1},{6,2},{7,3},{8,12},{9,13},{10,... | collective-permute-start | bytes 294920 | tf_op jit(solution)/shard_map/ppermute | solution.py:35

commit v9 on v8

--- a/solution.py
+++ b/solution.py
@@ -83,18 +83,23 @@
     return copies
 
 
-def query_kernel(q_hbm, *refs):
-    *query_refs, sems = refs
+def stacking(q_hbm, head, query_refs):
     rows = q_hbm.shape[1]
-    heads = [(query_ref, g) for query_ref in query_refs for g in range(G)]
-    parts = [(q_hbm.at[0, :, pl.ds(h * HD, HD)], ref.at[pl.ds(g * rows, rows)]) for h, (ref, g) in enumerate(heads)]
-    for copy in copy_all(parts, sems):
+    places = [(query_ref, g) for query_ref in query_refs for g in range(G)]
+    return [
+        (q_hbm.at[0, :, pl.ds((head + i) * HD, HD)], ref.at[pl.ds(g * rows, rows)]) for i, (ref, g) in enumerate(places)
+    ]
+
+
+def query_kernel(q_hbm, query_ref, sems):
+    for copy in copy_all(stacking(q_hbm, 0, [query_ref]), sems):
         copy.wait()
 
 
-def cache_kernel(key_hbm, value_hbm, w_hbm, key_ref, value_ref, w_ref, sems):
-    span = pl.ds(0, w_ref.shape[1])
-    for copy in copy_all(((key_hbm, key_ref), (value_hbm, value_ref), (w_hbm.at[:, span], w_ref)), sems):
+def cache_kernel(q_hbm, key_hbm, value_hbm, w_hbm, *refs):
+    *query_refs, key_ref, value_ref, w_ref, sems = refs
+    pairs = stacking(q_hbm, G, query_refs) + [(key_hbm, key_ref), (value_hbm, value_ref)]
+    for copy in copy_all(pairs + [(w_hbm.at[:, pl.ds(0, w_ref.shape[1])], w_ref)], sems):
         copy.wait()
 
 
@@ -193,9 +198,9 @@
 def total_kernel(count, *refs):
     *term_refs, out_ref, total_ref, sems = refs
     lower = term_refs[0].shape[1]
-    half = out_ref.shape[0] // 2
+    part = out_ref.shape[0] // 4
     copies = []
-    for i, rows in enumerate((slice(0, half), slice(half, 2 * half))):
+    for i, rows in enumerate([slice(k * part, (k + 1) * part) for k in range(4)]):
         for group, columns in ((term_refs[:count], slice(0, lower)), (term_refs[count:], slice(lower, None))):
             total_ref[rows, columns] = sum(ref[rows].astype(jnp.float32) for ref in group).astype(jnp.bfloat16)
         copies.append(pltpu.make_async_copy(total_ref.at[rows], out_ref.at[rows], sems.at[i]))
@@ -225,13 +230,8 @@
     bf16, f32 = jnp.bfloat16, jnp.float32
 
     in_hbm = [pltpu.with_memory_space_constraint(a, pltpu.HBM) for a in (queries, cache_keys, cache_values, out_weight)]
-    own_queries = local_call(
-        query_kernel,
-        [IN_HBM],
-        [((stacked, HD), bf16)] * kv_local,
-        16 * MIB,
-        0,
-        [pltpu.SemaphoreType.DMA((kv_local * G,))],
+    first_query = local_call(
+        query_kernel, [IN_HBM], [((stacked, HD), bf16)], 16 * MIB, 0, [pltpu.SemaphoreType.DMA((G,))]
     )(in_hbm[0])
     near = [(0, cache_keys, cache_values)]
     bit = top_bit // 2
@@ -239,17 +239,17 @@
         near += [(m | bit, exchange(k, "ctx", bit), exchange(v, "ctx", bit)) for m, k, v in near]
         bit //= 2
     w_shape = (1, G * HD, out_weight.shape[2])
-    own_keys, own_values, first_weight = local_call(
+    *more_queries, own_keys, own_values, first_weight = local_call(
         cache_kernel,
-        [IN_HBM] * 3,
-        [(cache_keys.shape, bf16), (cache_values.shape, bf16), (w_shape, bf16)],
+        [IN_HBM] * 4,
+        [((stacked, HD), bf16)] * (kv_local - 1)
+        + [(cache_keys.shape, bf16), (cache_values.shape, bf16), (w_shape, bf16)],
         16 * MIB,
         0,
-        [pltpu.SemaphoreType.DMA((3,))],
-    )(*in_hbm[1:])
-    sent_queries = list(own_queries)
-    sent_queries[1:], first_weight = lax.optimization_barrier((sent_queries[1:], first_weight))
-    far_queries = [exchange(query, "ctx", top_bit) for query in sent_queries]
+        [pltpu.SemaphoreType.DMA(((kv_local - 1) * G + 3,))],
+    )(*in_hbm)
+    own_queries = [*first_query, *more_queries]
+    far_queries = [exchange(query, "ctx", top_bit) for query in own_queries]
     masks, near_keys, near_values = zip(*near)
     cached = [in_vmem(a) for a in (own_keys, *near_keys[1:], own_values, *near_values[1:])]
     far_results = []
@@ -338,13 +338,14 @@
     part = [a.astype(jnp.bfloat16) for a in part]
     terms_b = [handed(a, x) for x, a in enumerate(part)]
 
+    terms_b, terms_a[-1] = lax.optimization_barrier((terms_b, terms_a[-1]))
     terms = [*terms_a, *terms_b]
     (out,) = pl.pallas_call(
         functools.partial(total_kernel, len(terms_a)),
         in_specs=[WHOLE] * len(terms),
         out_shape=[pltpu.HBM((rows, block_width), jnp.bfloat16)],
         out_specs=[IN_HBM],
-        scratch_shapes=[pltpu.VMEM((rows, block_width), jnp.bfloat16), pltpu.SemaphoreType.DMA((2,))],
+        scratch_shapes=[pltpu.VMEM((rows, block_width), jnp.bfloat16), pltpu.SemaphoreType.DMA((4,))],
         compiler_params=pltpu.CompilerParams(vmem_limit_bytes=16 * MIB),
     )(*[in_vmem(term) for term in terms])
     return out[None]

time: 45.4 us -> 45.4 us (level)
  transfers between devices with their start and end apart: 13 -> 13, of which waited for: 8 -> 7; matrix products, arithmetic and copies ran while one was open for 0% -> 0% of each run, Pallas kernels for 27% -> 26%
where the time goes in v9:
time: 45.4 us; the launch traced here: 45.2 us
  starting transfers between devices  21.8 us (48%)
  Pallas kernels  13.6 us (30%)
  waiting for transfers between devices  8.84 us (19%)
  between operations  0.78 us (2%)
    ppermute x5, starting transfers between devices, handed(): return lax.ppermute(block, ('section', 'tp'), route)  12.1 us
    ppermute x8, starting transfers between devices, exchange(): return lax.ppermute(block, axis, route)  9.75 us
    ppermute x8, waiting for transfers between devices, exchange(): return lax.ppermute(block, axis, route)  4.7 us
    ppermute x5, waiting for transfers between devices, handed(): return lax.ppermute(block, ('section', 'tp'), route)  4.14 us
    pallas_call x2, Pallas kernels, on_device(): local_call(functools.partial(far_kernel, masks, top_bit, kv_head), [SCALA...  2.86 us
    pallas_call x1, Pallas kernels, on_device(): local_call(cache_kernel, [IN_HBM] * 4, [((stacked, HD), bf16)] * (kv_loca...  2.83 us
    pallas_call x1, Pallas kernels, on_device(): local_call(functools.partial(near_kernel, masks, kv_local), [SCALARS, IN_...  2.68 us
    pallas_call x2, Pallas kernels, on_device(): local_call(functools.partial(combine_kernel, kv_head, relay, block_width)...  1.69 us
  transfers between devices with their start and end apart: 13, of which 7 were waited for; matrix products, arithmetic and copies ran while one was open for 0% of the time, Pallas kernels for 26%

profile of v9, /device:TPU:0, one launch (start us, length us, event | category | flops | bytes accessed | tf_op | source)
XLA Modules:
  0.0 45.2 jit_solution(2687622562493029414)
XLA Ops:
  0.0 0.5 %collective-permute-start = (bf16[1,640,256]{2,1,0:T(8,128)(2,1)}, bf16[1,640,256]{2,1,0:T(8,128)(2,1)S(1)}, u32[]{:S(2)}, u32[]{:S(2)}) collective-permute-start(bf16[1,640,256]{2,1,0:T(8,128)(2,1)} %key_hbm.1), channel_id=1, source_target_pairs={{0,8},{8,0},{16,24},{24,16},{1,9},{9,1},{17,25},{25,17},{2,10},{10... | collective-permute-start | bytes 983048 | tf_op jit(solution)/shard_map/ppermute | solution.py:29
  0.5 0.1 collective-permute-start.1
  0.5 0.8 %shard_map.64.refs_0_ = bf16[512,128]{1,0:T(8,128)(2,1)S(1)} custom-call(bf16[1,128,1024]{2,1,0:T(8,128)(2,1)} %q_hbm.3), custom_call_target="tpu_custom_call" | custom-call | tf_op jit(solution)/shard_map/pallas_call | solution.py:233
  1.4 3.0 %collective-permute-start.2 = (bf16[512,128]{1,0:T(8,128)(2,1)S(1)}, bf16[512,128]{1,0:T(8,128)(2,1)S(1)}, u32[]{:S(2)}, u32[]{:S(2)}) collective-permute-start(bf16[512,128]{1,0:T(8,128)(2,1)S(1)} %shard_map.64.refs_0_), channel_id=1, source_target_pairs={{0,16},{8,24},{16,0},{24,8},{1,17},{9,25},{17,1},{25,9},{2,18},{10... | collective-permute-start | bytes 393224 | tf_op jit(solution)/shard_map/ppermute | solution.py:29
  4.4 2.8 %shard_map.65 = (bf16[512,128]{1,0:T(8,128)(2,1)S(1)}, bf16[1,640,256]{2,1,0:T(8,128)(2,1)S(1)}, bf16[1,640,256]{2,1,0:T(8,128)(2,1)S(1)}, bf16[1,512,5120]{2,1,0:T(8,128)(2,1)S(1)}) custom-call(bf16[1,128,1024]{2,1,0:T(8,128)(2,1)} %q_hbm.3, bf16[1,640,256]{2,1,0:T(8,128)(2,1)} %key_hbm.1, bf16[1,640,256]{2,1,0:T(8,128)(2,1)} %value_hbm.1, ...), custom_call_target="tpu_custom_call" | custom-call | tf_op jit(solution)/shard_map/pallas_call | solution.py:242
  7.2 0.1 collective-permute-start.4
  8.0 0.1 collective-permute-done.2.query_ref
  8.1 0.0 collective-permute-done.refs_3_.refs_1_
  8.1 0.0 collective-permute-done.1.refs_5_.refs_3_
  8.1 1.4 %shard_map.67 = bf16[528,128]{1,0:T(8,128)(2,1)S(1)} custom-call(s32[1]{0:T(128)S(6)} %copy.7.offset_ref, bf16[512,128]{1,0:T(8,128)(2,1)S(1)} %collective-permute-done.2.query_ref, bf16[1,640,256]{2,1,0:T(8,128)(2,1)S(1)} %get-tuple-element.27.refs_2_.refs_0_, bf16[1,640,256]{2,1,0:T(8,128)(2,1)S(1)} %collective-permute-done.refs_3_.refs_1_, ...), custom_call_target="tpu_custom_call" | custom-call | tf_op jit(solution)/shard_map/pallas_call | solution.py:260
  9.5 2.0 %collective-permute-start.3 = (bf16[528,128]{1,0:T(8,128)(2,1)S(1)}, bf16[528,128]{1,0:T(8,128)(2,1)S(1)}, u32[]{:S(2)}, u32[]{:S(2)}) collective-permute-start(bf16[528,128]{1,0:T(8,128)(2,1)S(1)} %shard_map.67), channel_id=1, source_target_pairs={{0,16},{8,24},{16,0},{24,8},{1,17},{9,25},{17,1},{25,9},{2,18},{10... | collective-permute-start | bytes 405512 | tf_op jit(solution)/shard_map/ppermute | solution.py:29
  11.5 1.5 %collective-permute-done.4.query_ref = bf16[512,128]{1,0:T(8,128)(2,1)S(1)} collective-permute-done((bf16[512,128]{1,0:T(8,128)(2,1)S(1)}, bf16[512,128]{1,0:T(8,128)(2,1)S(1)}, u32[]{:S(2)}, u32[]{:S(2)}) %collective-permute-start.4) | collective-permute-done | bytes 131104 | tf_op jit(solution)/shard_map/ppermute | solution.py:29
  13.0 1.4 %shard_map.69 = bf16[528,128]{1,0:T(8,128)(2,1)S(1)} custom-call(s32[1]{0:T(128)S(6)} %copy.7.offset_ref, bf16[512,128]{1,0:T(8,128)(2,1)S(1)} %collective-permute-done.4.query_ref, bf16[1,640,256]{2,1,0:T(8,128)(2,1)S(1)} %get-tuple-element.27.refs_2_.refs_0_, bf16[1,640,256]{2,1,0:T(8,128)(2,1)S(1)} %collective-permute-done.refs_3_.refs_1_, ...), custom_call_target="tpu_custom_call" | custom-call | tf_op jit(solution)/shard_map/pallas_call | solution.py:260
  14.5 0.1 collective-permute-start.5
  14.5 2.7 %shard_map.66 = (f32[2,512,128]{2,1,0:T(8,128)S(1)}, f32[2,512,128]{2,1,0:T(8,128)S(1)}, bf16[1,512,5120]{2,1,0:T(8,128)(2,1)S(1)}) custom-call(s32[1]{0:T(128)S(6)} %copy.7.offset_ref, bf16[1,1024,5120]{2,1,0:T(8,128)(2,1)} %w_hbm.3, bf16[512,128]{1,0:T(8,128)(2,1)S(1)} %shard_map.64.refs_0_, bf16[512,128]{1,0:T(8,128)(2,1)S(1)} %get-tuple-element.26.refs_1_, ...), custom_call_target="tpu_custom_call" | custom-call | tf_op jit(solution)/shard_map/pallas_call | solution.py:268
  17.2 0.0 collective-permute-done.3.far_ref
  17.2 0.0 copy-start
  17.3 0.8 %shard_map.68 = (bf16[128,512]{1,0:T(8,128)(2,1)S(1)}, f32[1,128,896]{2,1,0:T(8,128)S(1)}) custom-call(f32[2,512,128]{2,1,0:T(8,128)S(1)} %get-tuple-element.29.near_ref, f32[2,512,128]{2,1,0:T(8,128)S(1)} %get-tuple-element.30.log_ref, bf16[528,128]{1,0:T(8,128)(2,1)S(1)} %collective-permute-done.3.far_ref, ...), custom_call_target="tpu_custom_call" | custom-call | tf_op jit(solution)/shard_map/pallas_call | solution.py:286
  18.1 1.4 %collective-permute-done.5.far_ref = bf16[528,128]{1,0:T(8,128)(2,1)S(1)} collective-permute-done((bf16[528,128]{1,0:T(8,128)(2,1)S(1)}, bf16[528,128]{1,0:T(8,128)(2,1)S(1)}, u32[]{:S(2)}, u32[]{:S(2)}) %collective-permute-start.5) | collective-permute-done | bytes 135200 | tf_op jit(solution)/shard_map/ppermute | solution.py:29
  19.5 0.8 %shard_map.70 = (bf16[128,512]{1,0:T(8,128)(2,1)S(1)}, bf16[1,128,896]{2,1,0:T(8,128)(2,1)S(1)}) custom-call(f32[2,512,128]{2,1,0:T(8,128)S(1)} %get-tuple-element.29.near_ref, f32[2,512,128]{2,1,0:T(8,128)S(1)} %get-tuple-element.30.log_ref, bf16[528,128]{1,0:T(8,128)(2,1)S(1)} %collective-permute-done.5.far_ref, ...), custom_call_target="tpu_custom_call" | custom-call | tf_op jit(solution)/shard_map/pallas_call | solution.py:286
  20.4 1.4 %collective-permute-start.7 = (bf16[1,128,896]{2,1,0:T(8,128)(2,1)S(1)}, bf16[1,128,896]{2,1,0:T(8,128)(2,1)S(1)}, u32[]{:S(2)}, u32[]{:S(2)}) collective-permute-start(bf16[1,128,896]{2,1,0:T(8,128)(2,1)S(1)} %get-tuple-element.38), channel_id=1, source_target_pairs={{0,1},{1,0},{2,3},{3,2},{4,5},{5,4},{6,7},{7,6},{8,9},{9,8},{10,11... | collective-permute-start | bytes 688136 | tf_op jit(solution)/shard_map/ppermute | solution.py:29
  21.8 0.0 copy-done
  21.8 0.5 %shard_map.71 = bf16[128,896]{1,0:T(8,128)(2,1)S(1)} custom-call(bf16[128,512]{1,0:T(8,128)(2,1)S(1)} %get-tuple-element.32.refs_0_, bf16[128,512]{1,0:T(8,128)(2,1)S(1)} %get-tuple-element.36.refs_1_, bf16[1,512,5120]{2,1,0:T(8,128)(2,1)S(1)} %get-tuple-element.31.w_ref.refs_2_, bf16[1,512,5120]{2,1,0:T(8,128)(2,1)S(1)} %get-tuple-element.34.w_ref.refs_3_, ...), custom_call_target="tpu_custom_call" | custom-call | flops 234881024 | tf_op jit(solution)/shard_map/pallas_call | solution.py:295
  22.3 1.6 %collective-permute-start.6 = (bf16[128,896]{1,0:T(8,128)(2,1)S(1)}, bf16[128,896]{1,0:T(8,128)(2,1)S(1)}, u32[]{:S(2)}, u32[]{:S(2)}) collective-permute-start(bf16[128,896]{1,0:T(8,128)(2,1)S(1)} %shard_map.71), channel_id=1, source_target_pairs={{0,4},{1,5},{2,6},{3,7},{4,0},{5,1},{6,2},{7,3},{8,12},{9,13},{10,... | collective-permute-start | bytes 688136 | tf_op jit(solution)/shard_map/ppermute | solution.py:35
  23.8 0.7 %shard_map.73 = (bf16[2,128,384]{2,1,0:T(8,128)(2,1)S(1)}, bf16[1,128,896]{2,1,0:T(8,128)(2,1)S(1)}) custom-call(bf16[128,512]{1,0:T(8,128)(2,1)S(1)} %get-tuple-element.32.refs_0_, bf16[128,512]{1,0:T(8,128)(2,1)S(1)} %get-tuple-element.36.refs_1_, bf16[1,512,5120]{2,1,0:T(8,128)(2,1)S(1)} %get-tuple-element.31.w_ref.refs_2_, ...), custom_call_target="tpu_custom_call" | custom-call | flops 436207616 | tf_op jit(solution)/shard_map/pallas_call | solution.py:304
  24.5 2.7 %collective-permute-start.9 = (bf16[2,128,384]{2,1,0:T(8,128)(2,1)S(1)}, bf16[2,128,384]{2,1,0:T(8,128)(2,1)S(1)}, u32[]{:S(2)}, u32[]{:S(2)}) collective-permute-start(bf16[2,128,384]{2,1,0:T(8,128)(2,1)S(1)} %get-tuple-element.42), channel_id=1, source_target_pairs={{0,2},{1,3},{2,0},{3,1},{4,6},{5,7},{6,4},{7,5},{8,10},{9,11},{10,... | collective-permute-start | bytes 589832 | tf_op jit(solution)/shard_map/ppermute | solution.py:29
  27.2 0.4 collective-permute-start.8
  27.6 0.7 %shard_map.72 = (bf16[1,128,896]{2,1,0:T(8,128)(2,1)S(1)}, bf16[2,128,384]{2,1,0:T(8,128)(2,1)S(1)}) custom-call(bf16[128,512]{1,0:T(8,128)(2,1)S(1)} %get-tuple-element.32.refs_0_, bf16[128,512]{1,0:T(8,128)(2,1)S(1)} %get-tuple-element.36.refs_1_, bf16[1,512,5120]{2,1,0:T(8,128)(2,1)S(1)} %get-tuple-element.31.w_ref.refs_2_, ...), custom_call_target="tpu_custom_call" | custom-call | flops 436207616 | tf_op jit(solution)/shard_map/pallas_call | solution.py:304
  28.4 0.0 collective-permute-done.7
  28.4 0.1 fusion
  28.4 0.3 collective-permute-done.6.refs_0_
  28.7 7.4 %collective-permute-start.12 = (bf16[128,896]{1,0:T(8,128)(2,1)S(1)}, bf16[128,896]{1,0:T(8,128)(2,1)S(1)}, u32[]{:S(2)}, u32[]{:S(2)}) collective-permute-start(bf16[128,896]{1,0:T(8,128)(2,1)S(1)} %fusion), channel_id=1, source_target_pairs={{0,6},{1,7},{2,4},{3,5},{4,2},{5,3},{6,0},{7,1},{8,14},{9,15},{10,... | collective-permute-start | bytes 688136 | tf_op jit(solution)/shard_map/ppermute | solution.py:35
  36.1 1.6 %collective-permute-done.9 = bf16[2,128,384]{2,1,0:T(8,128)(2,1)S(1)} collective-permute-done((bf16[2,128,384]{2,1,0:T(8,128)(2,1)S(1)}, bf16[2,128,384]{2,1,0:T(8,128)(2,1)S(1)}, u32[]{:S(2)}, u32[]{:S(2)}) %collective-permute-start.9) | collective-permute-done | bytes 196640 | tf_op jit(solution)/shard_map/ppermute | solution.py:29
  37.8 0.1 fusion.2
  37.8 0.8 %collective-permute-start.11 = (bf16[128,384]{1,0:T(8,128)(2,1)S(1)}, bf16[128,384]{1,0:T(8,128)(2,1)S(1)}, u32[]{:S(2)}, u32[]{:S(2)}) collective-permute-start(bf16[128,384]{1,0:T(8,128)(2,1)S(1)} %get-tuple-element.47), channel_id=1, source_target_pairs={{0,5},{1,4},{2,7},{3,6},{4,1},{5,0},{6,3},{7,2},{8,13},{9,12},{10,... | collective-permute-start | bytes 294920 | tf_op jit(solution)/shard_map/ppermute | solution.py:35
  38.7 1.9 %collective-permute-start.10 = (bf16[128,384]{1,0:T(8,128)(2,1)S(1)}, bf16[128,384]{1,0:T(8,128)(2,1)S(1)}, u32[]{:S(2)}, u32[]{:S(2)}) collective-permute-start(bf16[128,384]{1,0:T(8,128)(2,1)S(1)} %get-tuple-element.48), channel_id=1, source_target_pairs={{0,4},{1,5},{2,6},{3,7},{4,0},{5,1},{6,2},{7,3},{8,12},{9,13},{10,... | collective-permute-start | bytes 294920 | tf_op jit(solution)/shard_map/ppermute | solution.py:35
  40.5 3.0 %collective-permute-done.11.refs_4_ = bf16[128,384]{1,0:T(8,128)(2,1)S(1)} collective-permute-done((bf16[128,384]{1,0:T(8,128)(2,1)S(1)}, bf16[128,384]{1,0:T(8,128)(2,1)S(1)}, u32[]{:S(2)}, u32[]{:S(2)}) %collective-permute-start.11) | collective-permute-done | bytes 98336 | tf_op jit(solution)/shard_map/ppermute | solution.py:35
  43.5 0.9 %collective-permute-done.10.refs_3_ = bf16[128,384]{1,0:T(8,128)(2,1)S(1)} collective-permute-done((bf16[128,384]{1,0:T(8,128)(2,1)S(1)}, bf16[128,384]{1,0:T(8,128)(2,1)S(1)}, u32[]{:S(2)}, u32[]{:S(2)}) %collective-permute-start.10) | collective-permute-done | bytes 98336 | tf_op jit(solution)/shard_map/ppermute | solution.py:35
  44.4 0.0 collective-permute-done.12.refs_2_
  44.4 0.0 collective-permute-done.8.refs_1_
  44.4 0.8 %shard_map.74 = bf16[128,1280]{1,0:T(8,128)(2,1)} custom-call(bf16[128,896]{1,0:T(8,128)(2,1)S(1)} %collective-permute-done.6.refs_0_, bf16[128,896]{1,0:T(8,128)(2,1)S(1)} %collective-permute-done.8.refs_1_, bf16[128,896]{1,0:T(8,128)(2,1)S(1)} %collective-permute-done.12.refs_2_, bf16[128,384]{1,0:T(8,128)(2,1)S(1)} %collective-permute-done.10.refs_3_, ...), custom_call_target="tpu_custom_call" | custom-call | tf_op jit(solution)/shard_map/pallas_call | solution.py:343
Async XLA Ops:
  0.0 8.1 %collective-permute-start = (bf16[1,640,256]{2,1,0:T(8,128)(2,1)}, bf16[1,640,256]{2,1,0:T(8,128)(2,1)S(1)}, u32[]{:S(2)}, u32[]{:S(2)}) collective-permute-start(bf16[1,640,256]{2,1,0:T(8,128)(2,1)} %key_hbm.1), channel_id=1, source_target_pairs={{0,8},{8,0},{16,24},{24,16},{1,9},{9,1},{17,25},{25,17},{2,10},{10... | collective-permute-start | bytes 983048 | tf_op jit(solution)/shard_map/ppermute | solution.py:29
  0.5 7.6 %collective-permute-start.1 = (bf16[1,640,256]{2,1,0:T(8,128)(2,1)}, bf16[1,640,256]{2,1,0:T(8,128)(2,1)S(1)}, u32[]{:S(2)}, u32[]{:S(2)}) collective-permute-start(bf16[1,640,256]{2,1,0:T(8,128)(2,1)} %value_hbm.1), channel_id=1, source_target_pairs={{0,8},{8,0},{16,24},{24,16},{1,9},{9,1},{17,25},{25,17},{2,10},{10... | collective-permute-start | bytes 983048 | tf_op jit(solution)/shard_map/ppermute | solution.py:29
  1.4 6.7 %collective-permute-start.2 = (bf16[512,128]{1,0:T(8,128)(2,1)S(1)}, bf16[512,128]{1,0:T(8,128)(2,1)S(1)}, u32[]{:S(2)}, u32[]{:S(2)}) collective-permute-start(bf16[512,128]{1,0:T(8,128)(2,1)S(1)} %shard_map.64.refs_0_), channel_id=1, source_target_pairs={{0,16},{8,24},{16,0},{24,8},{1,17},{9,25},{17,1},{25,9},{2,18},{10... | collective-permute-start | bytes 393224 | tf_op jit(solution)/shard_map/ppermute | solution.py:29
  7.2 5.8 %collective-permute-start.4 = (bf16[512,128]{1,0:T(8,128)(2,1)S(1)}, bf16[512,128]{1,0:T(8,128)(2,1)S(1)}, u32[]{:S(2)}, u32[]{:S(2)}) collective-permute-start(bf16[512,128]{1,0:T(8,128)(2,1)S(1)} %get-tuple-element.26.refs_1_), channel_id=1, source_target_pairs={{0,16},{8,24},{16,0},{24,8},{1,17},{9,25},{17,1},{25,9},{2,18},{10... | collective-permute-start | bytes 393224 | tf_op jit(solution)/shard_map/ppermute | solution.py:29
  9.5 7.7 %collective-permute-start.3 = (bf16[528,128]{1,0:T(8,128)(2,1)S(1)}, bf16[528,128]{1,0:T(8,128)(2,1)S(1)}, u32[]{:S(2)}, u32[]{:S(2)}) collective-permute-start(bf16[528,128]{1,0:T(8,128)(2,1)S(1)} %shard_map.67), channel_id=1, source_target_pairs={{0,16},{8,24},{16,0},{24,8},{1,17},{9,25},{17,1},{25,9},{2,18},{10... | collective-permute-start | bytes 405512 | tf_op jit(solution)/shard_map/ppermute | solution.py:29
  14.5 5.1 %collective-permute-start.5 = (bf16[528,128]{1,0:T(8,128)(2,1)S(1)}, bf16[528,128]{1,0:T(8,128)(2,1)S(1)}, u32[]{:S(2)}, u32[]{:S(2)}) collective-permute-start(bf16[528,128]{1,0:T(8,128)(2,1)S(1)} %shard_map.69), channel_id=1, source_target_pairs={{0,16},{8,24},{16,0},{24,8},{1,17},{9,25},{17,1},{25,9},{2,18},{10... | collective-permute-start | bytes 405512 | tf_op jit(solution)/shard_map/ppermute | solution.py:29
  17.2 4.6 %copy-start = (bf16[1,128,1280]{2,1,0:T(8,128)(2,1)S(1)}, bf16[1,128,1280]{2,1,0:T(8,128)(2,1)}, u32[]{:S(2)}) copy-start(bf16[1,128,1280]{2,1,0:T(8,128)(2,1)} %refs_4_.1) | copy-start | bytes 983044
  20.4 8.0 %collective-permute-start.7 = (bf16[1,128,896]{2,1,0:T(8,128)(2,1)S(1)}, bf16[1,128,896]{2,1,0:T(8,128)(2,1)S(1)}, u32[]{:S(2)}, u32[]{:S(2)}) collective-permute-start(bf16[1,128,896]{2,1,0:T(8,128)(2,1)S(1)} %get-tuple-element.38), channel_id=1, source_target_pairs={{0,1},{1,0},{2,3},{3,2},{4,5},{5,4},{6,7},{7,6},{8,9},{9,8},{10,11... | collective-permute-start | bytes 688136 | tf_op jit(solution)/shard_map/ppermute | solution.py:29
  22.3 6.5 %collective-permute-start.6 = (bf16[128,896]{1,0:T(8,128)(2,1)S(1)}, bf16[128,896]{1,0:T(8,128)(2,1)S(1)}, u32[]{:S(2)}, u32[]{:S(2)}) collective-permute-start(bf16[128,896]{1,0:T(8,128)(2,1)S(1)} %shard_map.71), channel_id=1, source_target_pairs={{0,4},{1,5},{2,6},{3,7},{4,0},{5,1},{6,2},{7,3},{8,12},{9,13},{10,... | collective-permute-start | bytes 688136 | tf_op jit(solution)/shard_map/ppermute | solution.py:35
  24.5 13.2 %collective-permute-start.9 = (bf16[2,128,384]{2,1,0:T(8,128)(2,1)S(1)}, bf16[2,128,384]{2,1,0:T(8,128)(2,1)S(1)}, u32[]{:S(2)}, u32[]{:S(2)}) collective-permute-start(bf16[2,128,384]{2,1,0:T(8,128)(2,1)S(1)} %get-tuple-element.42), channel_id=1, source_target_pairs={{0,2},{1,3},{2,0},{3,1},{4,6},{5,7},{6,4},{7,5},{8,10},{9,11},{10,... | collective-permute-start | bytes 589832 | tf_op jit(solution)/shard_map/ppermute | solution.py:29
  27.2 17.2 %collective-permute-start.8 = (bf16[128,896]{1,0:T(8,128)(2,1)S(1)}, bf16[128,896]{1,0:T(8,128)(2,1)S(1)}, u32[]{:S(2)}, u32[]{:S(2)}) collective-permute-start(bf16[128,896]{1,0:T(8,128)(2,1)S(1)} %bitcast.8), channel_id=1, source_target_pairs={{0,5},{1,4},{2,7},{3,6},{4,1},{5,0},{6,3},{7,2},{8,13},{9,12},{10,... | collective-permute-start | bytes 688136 | tf_op jit(solution)/shard_map/ppermute | solution.py:35
  28.7 15.7 %collective-permute-start.12 = (bf16[128,896]{1,0:T(8,128)(2,1)S(1)}, bf16[128,896]{1,0:T(8,128)(2,1)S(1)}, u32[]{:S(2)}, u32[]{:S(2)}) collective-permute-start(bf16[128,896]{1,0:T(8,128)(2,1)S(1)} %fusion), channel_id=1, source_target_pairs={{0,6},{1,7},{2,4},{3,5},{4,2},{5,3},{6,0},{7,1},{8,14},{9,15},{10,... | collective-permute-start | bytes 688136 | tf_op jit(solution)/shard_map/ppermute | solution.py:35
  37.8 5.6 %collective-permute-start.11 = (bf16[128,384]{1,0:T(8,128)(2,1)S(1)}, bf16[128,384]{1,0:T(8,128)(2,1)S(1)}, u32[]{:S(2)}, u32[]{:S(2)}) collective-permute-start(bf16[128,384]{1,0:T(8,128)(2,1)S(1)} %get-tuple-element.47), channel_id=1, source_target_pairs={{0,5},{1,4},{2,7},{3,6},{4,1},{5,0},{6,3},{7,2},{8,13},{9,12},{10,... | collective-permute-start | bytes 294920 | tf_op jit(solution)/shard_map/ppermute | solution.py:35
  38.7 5.7 %collective-permute-start.10 = (bf16[128,384]{1,0:T(8,128)(2,1)S(1)}, bf16[128,384]{1,0:T(8,128)(2,1)S(1)}, u32[]{:S(2)}, u32[]{:S(2)}) collective-permute-start(bf16[128,384]{1,0:T(8,128)(2,1)S(1)} %get-tuple-element.48), channel_id=1, source_target_pairs={{0,4},{1,5},{2,6},{3,7},{4,0},{5,1},{6,2},{7,3},{8,12},{9,13},{10,... | collective-permute-start | bytes 294920 | tf_op jit(solution)/shard_map/ppermute | solution.py:35
